TPU v7x, 512 devices: a whole 4x4x16 slice. The times are simulated.
512 devices in a mesh: dp: 64 (over y_lo, z, core), fsdp: 8 (over x, y_hi).
Axes of the slice: x: 4, y: 4 (y_hi: 2, y_lo: 2; y = y_hi * 2 + y_lo), z: 16, core: 2. Of those that a mesh axis runs over, the one named last changes fastest.
Arguments:
- patches: bfloat16 [64, 8, 7, 64, 1280], P('dp', 'fsdp'), may hold values from -20 to 20
- norm_gain: float32 [1280], replicated, may hold values from 0.1 to 1.9
- w_qkv: bfloat16 [1280, 3840], P('fsdp'), may hold values from -0.5 to 0.5
- b_qkv: float32 [3840], replicated, may hold values from -3 to 3
- w_proj: bfloat16 [1280, 1280], P(None, 'fsdp'), may hold values from -0.15625 to 0.15625
- b_proj: float32 [1280], replicated, may hold values from -3 to 3
- merge_gain: float32 [1280], replicated, may hold values from 0.1 to 1.9
- groups: int32 [64, 8, 7], P(None, 'fsdp'), may hold values from 1 to 16
- route: int32 [64, 8, 7, 2], P(None, 'fsdp'), may hold values from -1 to 63, as said below
Outputs:
- merged: bfloat16 [64, 8, 4, 16, 5120], P('dp', 'fsdp')
Inputs may be any that keep to these rules, and one draw needn't show every extreme that they name: In lane f, rank r keeps k_r windows (1 to 4) at slots 0 to k_r - 1 with route (r, j), and has s_r surplus windows (0 to 3) at slots 4 to 4 + s_r - 1; its k-th surplus slot 4 + k goes to rank (r + k + 1) mod 64 at a slot from k_(r + k + 1) to 3. All other slots hold -1, -1. Every owner rank of a lane receives exactly 4 windows, one at each owner slot 0 to 3; some rank of each lane has s_r = 3.
All inputs are finite; a program needn't handle non-finite values.
Results may differ from a plain program's by a relative error of at most 0.0055.
The roundings to bfloat16 on the way count: a program that leaves them out, or rounds other values in their place, can miss the bound.
Values may be sent and summed in bfloat16 or wider, within the bound.
No kernel may reach another device: no remote copies, remote signals or barrier semaphores. Data moves between devices by JAX's collectives and lax.ppermute only.
A program may use at most 64 MiB of HBM per device.

v0:
```python
import jax
import jax.numpy as jnp
from jax import lax
from jax.sharding import PartitionSpec as P

HEADS = 16
MERGE = 4
RECV = 4


def passed_along(value, axis, by):
    devices = lax.axis_size(axis)
    return lax.ppermute(value, axis, [(i, (i + by) % devices) for i in range(devices)])


def encode(windows, group_counts, norm_gain, w_qkv, b_qkv, w_proj, b_proj, merge_gain):
    count_windows, window_len, features = windows.shape
    head_size = features // HEADS
    whole = windows.astype(jnp.float32)
    normed_in = (
        whole * lax.rsqrt(jnp.mean(whole * whole, axis=-1, keepdims=True) + 1e-06) * norm_gain
    ).astype(jnp.bfloat16)
    flat_rows = normed_in.reshape(count_windows * window_len, features)
    summed = jnp.dot(
        flat_rows,
        lax.all_gather(w_qkv, "fsdp", axis=0, tiled=True),
        preferred_element_type=jnp.float32,
    )
    projected = (summed + b_qkv).astype(jnp.bfloat16)
    split_heads = projected.reshape(count_windows, window_len, 3, HEADS, head_size)
    queries = split_heads[:, :, 0]
    key_rows = split_heads[:, :, 1]
    values = split_heads[:, :, 2]
    scores = jnp.einsum(
        "nqhd,nkhd->nhqk", queries, key_rows, preferred_element_type=jnp.float32
    ) * head_size ** (-0.5)
    live_keys = jnp.arange(window_len, dtype=jnp.int32)[None, :] < MERGE * group_counts[:, None]
    scores = jnp.where(live_keys[:, None, None, :], scores, -1e30)
    row_top = jnp.max(scores, axis=-1, keepdims=True)
    raised = jnp.exp(scores - row_top)
    probability = (raised / jnp.sum(raised, axis=-1, keepdims=True)).astype(jnp.bfloat16)
    attended = jnp.einsum(
        "nhqk,nkhd->nqhd", probability, values, preferred_element_type=jnp.float32
    ).astype(jnp.bfloat16)
    attended = attended.reshape(count_windows * window_len, features)
    update = jnp.dot(
        attended,
        lax.all_gather(w_proj, "fsdp", axis=1, tiled=True),
        preferred_element_type=jnp.float32,
    )
    residual = whole.reshape(count_windows * window_len, features) + update + b_proj
    normed = (
        residual
        * lax.rsqrt(jnp.mean(residual * residual, axis=-1, keepdims=True) + 1e-06)
        * merge_gain
    )
    normed = normed.reshape(count_windows, window_len // MERGE, MERGE * features)
    kept_rows = jnp.arange(window_len // MERGE, dtype=jnp.int32)[None, :] < group_counts[:, None]
    return jnp.where(kept_rows[:, :, None], normed, 0.0).astype(jnp.bfloat16)


def arrival(lane_route, lane_groups, my_rank, rank_count, moved_index):
    sender = (my_rank - moved_index - 1) % rank_count
    sender_row = lax.dynamic_index_in_dim(lane_route, sender, 0, keepdims=False)[RECV + moved_index]
    sender_group = lax.dynamic_index_in_dim(lane_groups, sender, 0, keepdims=False)[
        RECV + moved_index
    ]
    target_ids = jnp.arange(RECV, dtype=jnp.int32)
    landing = (target_ids == sender_row[1]) & (sender_row[0] == my_rank)
    return (landing, sender_group)


def on_device(patches, norm_gain, w_qkv, b_qkv, w_proj, b_proj, merge_gain, groups, route):
    rank_count = lax.axis_size("dp")
    my_rank = lax.axis_index("dp")
    windows = patches[0, 0]
    slot_count = windows.shape[0]
    lane_route = route[:, 0]
    lane_groups = groups[:, 0]
    my_route = lax.dynamic_index_in_dim(lane_route, my_rank, 0, keepdims=False)
    my_groups = lax.dynamic_index_in_dim(lane_groups, my_rank, 0, keepdims=False)
    kept_here = my_route[:RECV, 0] == my_rank
    moved_live = my_route[RECV:, 0] >= 0
    at_home = encode(windows, my_groups, norm_gain, w_qkv, b_qkv, w_proj, b_proj, merge_gain)
    merged = jnp.where(kept_here[:, None, None], at_home[:RECV], jnp.zeros_like(at_home[:RECV]))
    for moved_index in range(slot_count - RECV):
        outgoing = jnp.where(
            moved_live[moved_index], at_home[RECV + moved_index], jnp.zeros_like(at_home[0])
        )
        incoming = passed_along(outgoing, "dp", moved_index + 1)
        landing, sender_group = arrival(lane_route, lane_groups, my_rank, rank_count, moved_index)
        merged = jnp.where(landing[:, None, None], incoming[None], merged)
    return merged[None, None]


def solution(mesh):
    return jax.shard_map(
        on_device,
        mesh=mesh,
        in_specs=(
            P("dp", "fsdp", None, None, None),
            P(),
            P("fsdp", None),
            P(),
            P(None, "fsdp"),
            P(),
            P(),
            P(None, "fsdp", None),
            P(None, "fsdp", None, None),
        ),
        out_specs=P("dp", "fsdp", None, None, None),
        check_vma=False,
    )
```

profile of v0, /device:TPU:1, one launch (start us, length us, event | category | flops | bytes accessed | tf_op | source)
XLA Modules:
  0.0 268.1 jit_solution(12635162011329861364)
XLA Ops:
  6.5 0.0 copy-start
  6.5 0.0 copy-start.1
  6.5 0.0 copy-start.2
  6.5 0.0 copy-start.3
  6.5 0.0 all-gather.3.cloned.1.call-start
  6.6 0.7 all-gather.3.cloned.1.call-update
  7.3 0.0 copy-start.5
  7.3 0.0 all-gather.5.cloned.1.call-start
  7.3 0.7 all-gather.5.cloned.1.call-update
  8.1 0.0 copy-done.1
  8.1 0.3 multiply_reduce_fusion.1
  8.4 0.1 rsqrt.20
  8.5 0.0 copy-done.2
  8.5 0.1 constant_dynamic-slice_fusion.5
  8.6 0.1 copy.15
  8.7 0.7 constant_dynamic-slice_fusion.1
  9.9 0.0 copy-done
  9.9 0.3 dynamic-slice_reduce_fusion
  10.3 0.1 slice_compare_fusion
  10.3 0.7 fusion.21
  11.0 0.1 iota_compare_fusion.1
  11.1 0.1 iota_compare_fusion
  11.2 0.0 copy-done.3
  11.2 0.3 fusion.4
  11.5 141.5 %all-gather.3.cloned.1.call-done = bf16[1280,3840]{1,0:T(8,128)(2,1)} async-done(((bf16[160,3840]{1,0:T(8,128)(2,1)}), bf16[1280,3840]{1,0:T(8,128)(2,1)}) %all-gather.3.cloned.1.call-update) | async-done | bytes 9830416 | tf_op jit(solution)/shard_map/all_gather | solution.py:26
  153.0 0.0 copy-done.5
  153.0 10.0 %add_convert_fusion = bf16[448,3840]{1,0:T(8,128)(2,1)} fusion(bf16[448,1280]{1,0:T(8,128)(2,1)S(1)} %fusion.4, bf16[1280,3840]{1,0:T(8,128)(2,1)} %all-gather.3.cloned.1.call-done, f32[3840]{0:T(1024)S(1)} %copy-done.5), kind=kOutput, calls=%fused_computation.1 | convolution fusion | flops 4407459840 | bytes 14433280 | tf_op jit(solution)/shard_map/dot_general | solution.py:24
  163.0 11.4 %reshape.166 = bf16[7,64,3,16,80]{4,3,2,1,0:T(8,128)(2,1)} reshape(bf16[448,3840]{1,0:T(8,128)(2,1)} %add_convert_fusion) | data formatting | bytes 6881280 | tf_op jit(solution)/shard_map/reshape | solution.py:30
  174.4 3.9 %fusion.20 = (bf16[7,64,1,16,80]{4,3,2,1,0:T(8,128)(2,1)S(1)}, bf16[7,64,1,16,80]{4,3,2,1,0:T(8,128)(2,1)S(1)}, bf16[7,64,1,16,80]{4,3,2,1,0:T(8,128)(2,1)S(1)}) fusion(bf16[7,64,3,16,80]{4,3,2,1,0:T(8,128)(2,1)} %reshape.166), kind=kLoop, calls=%fused_computation.56 | loop fusion | bytes 6881280 | tf_op jit(solution)/shard_map/slice | solution.py:33
  178.4 1.1 fusion.6
  179.5 2.0 fusion.22
  181.5 1.0 convert_bitcast_fusion
  182.5 1.2 copy.20
  183.7 0.0 copy-start.6
  183.7 2.9 %reshape.167 = bf16[448,1280]{1,0:T(8,128)(2,1)} reshape(bf16[7,64,16,80]{3,2,1,0:T(8,128)(2,1)S(1)} %copy.20) | data formatting | bytes 2293760 | tf_op jit(solution)/shard_map/reshape | solution.py:45
  186.6 47.3 %all-gather.5.cloned.1.call-done = bf16[1280,1280]{0,1:T(8,128)(2,1)} async-done(((bf16[1280,160]{0,1:T(8,128)(2,1)}), bf16[1280,1280]{0,1:T(8,128)(2,1)}) %all-gather.5.cloned.1.call-update) | async-done | bytes 3276816 | tf_op jit(solution)/shard_map/all_gather | solution.py:48
  233.8 0.0 copy-done.6
  233.8 0.0 copy-start.4
  233.8 4.1 %multiply_reduce_fusion = (f32[448]{0:T(512)S(1)}, f32[448,1280]{1,0:T(8,128)S(1)}) fusion(f32[1280]{0:T(1024)S(1)} %copy-done.6, bf16[448,1280]{1,0:T(8,128)(2,1)} %reshape.167, bf16[1280,1280]{0,1:T(8,128)(2,1)} %all-gather.5.cloned.1.call-done, bf16[448,1280]{1,0:T(8,128)(2,1)S(1)} %bitcast.46), kind=kOutput, calls=%fused_computation.13 | convolution fusion | flops 1470873088 | bytes 7871232 | tf_op jit(solution)/shard_map/dot_general | solution.py:46
  238.0 0.0 copy-done.4
  238.0 0.3 multiply_multiply_fusion
  238.3 0.7 reshape.168
  239.0 0.3 select_convert_fusion
  239.3 1.8 fusion.17
  241.2 4.1 %collective-permute-start.2 = (bf16[16,5120]{1,0:T(8,128)(2,1)S(1)}, bf16[16,5120]{1,0:T(8,128)(2,1)S(1)}, u32[]{:S(2)}, u32[]{:S(2)}) collective-permute-start(bf16[16,5120]{1,0:T(8,128)(2,1)S(1)} %get-tuple-element.9), channel_id=1, source_target_pairs={{0,8},{8,16},{16,24},{24,32},{32,40},{40,48},{48,56},{56,64},{64,7... | collective-permute-start | bytes 491528 | tf_op jit(solution)/shard_map/ppermute | solution.py:13
  245.3 3.2 %collective-permute-start.1 = (bf16[16,5120]{1,0:T(8,128)(2,1)S(1)}, bf16[16,5120]{1,0:T(8,128)(2,1)S(1)}, u32[]{:S(2)}, u32[]{:S(2)}) collective-permute-start(bf16[16,5120]{1,0:T(8,128)(2,1)S(1)} %get-tuple-element.10), channel_id=1, source_target_pairs={{0,16},{8,24},{16,32},{24,40},{32,48},{40,56},{48,64},{56,72},{64,... | collective-permute-start | bytes 491528 | tf_op jit(solution)/shard_map/ppermute | solution.py:13
  248.5 3.2 %collective-permute-start = (bf16[16,5120]{1,0:T(8,128)(2,1)S(1)}, bf16[16,5120]{1,0:T(8,128)(2,1)S(1)}, u32[]{:S(2)}, u32[]{:S(2)}) collective-permute-start(bf16[16,5120]{1,0:T(8,128)(2,1)S(1)} %get-tuple-element.8), channel_id=1, source_target_pairs={{0,24},{8,32},{16,40},{24,48},{32,56},{40,64},{48,72},{56,80},{64,... | collective-permute-start | bytes 491528 | tf_op jit(solution)/shard_map/ppermute | solution.py:13
  251.7 0.7 compare_and_fusion.2
  253.7 1.3 compare_and_fusion
  255.0 0.0 collective-permute-done.2
  255.0 0.0 collective-permute-done.1
  255.0 5.2 %collective-permute-done = bf16[16,5120]{1,0:T(8,128)(2,1)S(1)} collective-permute-done((bf16[16,5120]{1,0:T(8,128)(2,1)S(1)}, bf16[16,5120]{1,0:T(8,128)(2,1)S(1)}, u32[]{:S(2)}, u32[]{:S(2)}) %collective-permute-start) | collective-permute-done | bytes 163872 | tf_op jit(solution)/shard_map/ppermute | solution.py:13
  260.2 1.1 fusion.14
  (4 shorter events, 0.0 us)
Async XLA Ops:
  6.5 3.4 %copy-start = (s32[64,1,7]{0,1,2:T(1,128)S(1)}, s32[64,1,7]{0,1,2:T(1,128)}, u32[]{:S(2)}) copy-start(s32[64,1,7]{0,1,2:T(1,128)} %param.16) | copy-start | bytes 5380
  6.5 1.6 copy-start.1
  6.5 2.0 copy-start.2
  6.5 4.6 %copy-start.3 = (f32[1280]{0:T(1024)S(1)}, f32[1280]{0:T(1024)}, u32[]{:S(2)}) copy-start(f32[1280]{0:T(1024)} %param.10) | copy-start | bytes 15364
  6.5 146.5 %all-gather.3.cloned.1.call-start = ((), (), s32[]{:S(2)}) async-start(), calls=%async_computation | async-start | bytes 11059200 | tf_op jit(solution)/shard_map/all_gather | solution.py:26
  7.3 145.8 %copy-start.5 = (f32[3840]{0:T(1024)S(1)}, f32[3840]{0:T(1024)}, u32[]{:S(2)}) copy-start(f32[3840]{0:T(1024)} %param.12) | copy-start | bytes 46084
  7.3 226.5 %all-gather.5.cloned.1.call-start = ((), (), s32[]{:S(2)}) async-start(), calls=%async_computation.1 | async-start | bytes 3686400 | tf_op jit(solution)/shard_map/all_gather | solution.py:48
  183.7 50.2 %copy-start.6 = (f32[1280]{0:T(1024)S(1)}, f32[1280]{0:T(1024)}, u32[]{:S(2)}) copy-start(f32[1280]{0:T(1024)} %param.14) | copy-start | bytes 15364
  233.8 4.2 %copy-start.4 = (f32[1280]{0:T(1024)S(1)}, f32[1280]{0:T(1024)}, u32[]{:S(2)}) copy-start(f32[1280]{0:T(1024)} %param.15) | copy-start | bytes 15364
  241.2 13.8 %collective-permute-start.2 = (bf16[16,5120]{1,0:T(8,128)(2,1)S(1)}, bf16[16,5120]{1,0:T(8,128)(2,1)S(1)}, u32[]{:S(2)}, u32[]{:S(2)}) collective-permute-start(bf16[16,5120]{1,0:T(8,128)(2,1)S(1)} %get-tuple-element.9), channel_id=1, source_target_pairs={{0,8},{8,16},{16,24},{24,32},{32,40},{40,48},{48,56},{56,64},{64,7... | collective-permute-start | bytes 491528 | tf_op jit(solution)/shard_map/ppermute | solution.py:13
  245.3 9.7 %collective-permute-start.1 = (bf16[16,5120]{1,0:T(8,128)(2,1)S(1)}, bf16[16,5120]{1,0:T(8,128)(2,1)S(1)}, u32[]{:S(2)}, u32[]{:S(2)}) collective-permute-start(bf16[16,5120]{1,0:T(8,128)(2,1)S(1)} %get-tuple-element.10), channel_id=1, source_target_pairs={{0,16},{8,24},{16,32},{24,40},{32,48},{40,56},{48,64},{56,72},{64,... | collective-permute-start | bytes 491528 | tf_op jit(solution)/shard_map/ppermute | solution.py:13
  248.5 11.7 %collective-permute-start = (bf16[16,5120]{1,0:T(8,128)(2,1)S(1)}, bf16[16,5120]{1,0:T(8,128)(2,1)S(1)}, u32[]{:S(2)}, u32[]{:S(2)}) collective-permute-start(bf16[16,5120]{1,0:T(8,128)(2,1)S(1)} %get-tuple-element.8), channel_id=1, source_target_pairs={{0,24},{8,32},{16,40},{24,48},{32,56},{40,64},{48,72},{56,80},{64,... | collective-permute-start | bytes 491528 | tf_op jit(solution)/shard_map/ppermute | solution.py:13
Sparse Core Ops, SparseCore 0:
  10.6 142.4 all-gather.2
  156.2 77.5 all-gather.4
where the time goes:
time: 269 us; the launch traced here: 268 us
  waiting for transfers between devices  195 us (72%)
  local copies, waits for them, and re-layouts  22.1 us (8%)
  matrix products  16.2 us (6%)
  between operations  15.6 us (6%)
  starting transfers between devices  10.6 us (4%)
  other arithmetic  8.24 us (3%)
    all_gather x1, waiting for transfers between devices, encode(): lax.all_gather(w_qkv, 'fsdp', axis=0, tiled=True)  142 us
    all_gather x1, waiting for transfers between devices, encode(): lax.all_gather(w_proj, 'fsdp', axis=1, tiled=True)  47.3 us
    reshape x1, local copies, waits for them, and re-layouts, encode(): projected.reshape(count_windows, window_len, 3, HEADS, head_size)  11.4 us
    ppermute x3, starting transfers between devices, passed_along(): lax.ppermute(value, axis, [(i, (i + by) % devices) for i in range(devices)])  10.5 us
    dot_general x1, matrix products, encode(): jnp.dot(flat_rows, lax.all_gather(w_qkv, 'fsdp', axis=0, tiled=True), pre...  9.97 us
  transfers between devices with their start and end apart: 5, of which 3 were waited for; matrix products, arithmetic and copies ran while one was open for 14% of the time, Pallas kernels for 0%

commit v1 on v0

v1 whole, which is shorter than its diff:
```python
import jax
import jax.numpy as jnp
from jax import lax
from jax.experimental import pallas as pl
from jax.experimental.pallas import tpu as pltpu
from jax.sharding import PartitionSpec as P

HEADS = 16
MERGE = 4
RECV = 4
SLOTS = 7
WIN = 64
D = 1280
HALF = D // 2
HEAD = D // HEADS
SHARDS = 8
DEPTH = D // SHARDS
ROWS = RECV * WIN
NX, NYH, NYL, NZ, NC = 4, 2, 2, 16, 2
AXES = ("dp", "fsdp")
EPS = 1e-06

NT = (((1,), (1,)), ((), ()))
TN = (((0,), (0,)), ((), ()))


def flat(x, yh, yl, z, c):
    return (((yl % NYL) * NZ + z % NZ) * NC + c) * SHARDS + (x % NX) * NYH + yh % NYH


def perm(move):
    places = [
        (x, yh, yl, z, c)
        for x in range(NX)
        for yh in range(NYH)
        for yl in range(NYL)
        for z in range(NZ)
        for c in range(NC)
    ]
    return [(flat(*p), flat(*move(*p))) for p in places]


def by_x(d):
    return perm(lambda x, yh, yl, z, c: (x + d, yh, yl, z, c))


def across_y():
    return perm(lambda x, yh, yl, z, c: (x, 1 - yh, 1 - yl, z, c))


def other_core():
    return perm(lambda x, yh, yl, z, c: (x, yh, yl, z, 1 - c))


def send(value, pairs):
    return lax.ppermute(value, AXES, pairs)


def by_rank(value, by):
    devices = lax.axis_size("dp")
    return lax.ppermute(value, "dp", [(i, (i + by) % devices) for i in range(devices)])


def place_kernel(meta, own, in0, in1, in2, gain, placed, normed):
    for t in range(RECV):
        src = meta[t]
        window = jnp.where(
            src < RECV,
            own[0, 0, t],
            jnp.where(src == RECV, in0[...], jnp.where(src == RECV + 1, in1[...], in2[...])),
        )
        placed[pl.ds(t * WIN, WIN), :] = window
        x = window.astype(jnp.float32)
        ms = jnp.mean(x * x, axis=-1, keepdims=True)
        normed[pl.ds(t * WIN, WIN), :] = (x * lax.rsqrt(ms + EPS) * gain[...]).astype(jnp.bfloat16)


def attend_kernel(meta, xa, xb, bias, *rest):
    pieces, (outa, outb, w, q, k, v, sems) = rest[:SHARDS], rest[SHARDS:]
    copies = []
    for i in range(SHARDS):
        at = pl.multiple_of(meta[12 + i] * DEPTH, DEPTH)
        copies.append(pltpu.make_async_copy(pieces[i], w.at[pl.ds(at, DEPTH), :], sems.at[i]))
    for copy in copies:
        copy.start()
    for copy in copies:
        copy.wait()
    for j, dst in enumerate((q, k, v)):
        cols = pl.ds(j * HALF, HALF)
        for i, src in enumerate((xa, xb)):
            dst[pl.ds(i * ROWS, ROWS), :] = (
                jnp.dot(src[...], w[:, cols], preferred_element_type=jnp.float32) + bias[:, cols]
            ).astype(jnp.bfloat16)
    pair = 2 * HEAD
    lane = lax.broadcasted_iota(jnp.int32, (1, 256), 1)
    key_at = lax.broadcasted_iota(jnp.int32, (WIN, 1), 0)
    for wnd in range(2 * RECV):
        rows = pl.ds(wnd * WIN, WIN)
        live = key_at < MERGE * meta[4 + wnd]
        out = outa if wnd < RECV else outb
        tiles = [None] * (HALF // 128)
        for i in range(HALF // pair):
            lo = i * pair // 128 * 128
            off = i * pair - lo
            first = (lane >= off) & (lane < off + HEAD)
            second = (lane >= off + HEAD) & (lane < off + pair)
            cols = pl.ds(lo, 256)
            qw = q[rows, cols]
            q2 = jnp.concatenate(
                [
                    qw * first.astype(jnp.float32).astype(jnp.bfloat16),
                    qw * second.astype(jnp.float32).astype(jnp.bfloat16),
                ],
                axis=0,
            )
            s = lax.dot_general(k[rows, cols], q2, NT, preferred_element_type=jnp.float32)
            s = jnp.where(live, s * HEAD ** (-0.5), -1e30)
            e = jnp.exp(s - jnp.max(s, axis=0, keepdims=True))
            p = (e / jnp.sum(e, axis=0, keepdims=True)).astype(jnp.bfloat16)
            o = lax.dot_general(p, v[rows, cols], TN, preferred_element_type=jnp.float32)
            o = jnp.where(first, o[:WIN], jnp.where(second, o[WIN:], 0.0))
            for n in range(2):
                part = o[:, n * 128 : (n + 1) * 128]
                tile = lo // 128 + n
                tiles[tile] = part if tiles[tile] is None else tiles[tile] + part
        at = pl.ds(wnd % RECV * WIN, WIN)
        for n, tile in enumerate(tiles):
            out[at, pl.ds(n * 128, 128)] = tile.astype(jnp.bfloat16)


def merge_kernel(meta, atta, attb, wa, wb, placed, bias, gain, out, y):
    update = lax.dot_general(atta[...], wa[...], NT, preferred_element_type=jnp.float32)
    update += lax.dot_general(attb[...], wb[...], NT, preferred_element_type=jnp.float32)
    r = placed[...].astype(jnp.float32) + update + bias[...]
    ms = jnp.mean(r * r, axis=-1, keepdims=True)
    normed = r * lax.rsqrt(ms + EPS) * gain[...]
    for n in range(D // 128):
        y[n] = normed[:, n * 128 : (n + 1) * 128]
    tokens = WIN // MERGE
    at = lax.broadcasted_iota(jnp.int32, (RECV * tokens, 1), 0)
    limit = jnp.full((RECV * tokens, 1), meta[4], jnp.int32)
    for t in range(1, RECV):
        limit = jnp.where(at >= t * tokens, meta[4 + t] + t * tokens, limit)
    live = at < limit
    for i in range(MERGE):
        for n in range(D // 128):
            part = y[n, pl.ds(i, RECV * tokens, stride=MERGE), :]
            out[:, pl.ds(i * D + n * 128, 128)] = jnp.where(live, part, 0.0).astype(jnp.bfloat16)


def vmem(n):
    return [pl.BlockSpec(memory_space=pltpu.VMEM)] * n


SMEM = pl.BlockSpec(memory_space=pltpu.SMEM)
PARAMS = pltpu.CompilerParams(vmem_limit_bytes=20 * 1024 * 1024)


def tables(route, groups, rank, x, yh):
    ranks = lax.axis_size("dp")
    who = jnp.stack([rank, rank ^ 1])
    slot = jnp.arange(SLOTS, dtype=jnp.int32)
    sender = jnp.where(slot < RECV, who[:, None], (who[:, None] - slot + RECV - 1) % ranks)
    hot = sender[:, :, None] == jnp.arange(ranks, dtype=jnp.int32)
    lane_route = jnp.transpose(route[:, 0], (1, 2, 0))
    lane_groups = jnp.transpose(groups[:, 0], (1, 0))
    there = jnp.sum(jnp.where(hot[:, :, None], lane_route, 0), axis=-1)
    count = jnp.sum(jnp.where(hot, lane_groups, 0), axis=-1)
    target = jnp.arange(RECV, dtype=jnp.int32)
    lands = (there[:, :, 0] == who[:, None])[:, :, None] & (there[:, :, 1][:, :, None] == target)
    src = jnp.sum(jnp.where(lands, slot[None, :, None], 0), axis=1)
    grp = jnp.sum(jnp.where(lands, count[:, :, None], 0), axis=1)
    steps = [(0, 0), (-1, 0), (1, 0), (0, 1), (2, 0), (-1, 1), (1, 1), (2, 1)]
    shard = jnp.stack([((x + dx) % NX) * NYH + (yh + dy) % NYH for dx, dy in steps])
    return jnp.concatenate([src[0], grp[0], grp[1], shard]).astype(jnp.int32)


def on_device(patches, norm_gain, w_qkv, b_qkv, w_proj, b_proj, merge_gain, groups, route):
    rank = lax.axis_index("dp")
    lane = lax.axis_index("fsdp")
    core = rank % NC
    half = core * HALF

    piece = jnp.concatenate(
        [lax.dynamic_slice_in_dim(w_qkv, j * D + half, HALF, 1) for j in range(3)], axis=1
    )
    bias = jnp.concatenate(
        [lax.dynamic_slice_in_dim(b_qkv, j * D + half, HALF, 0) for j in range(3)]
    )
    plus = send(piece, by_x(1))
    minus = send(piece, by_x(-1))
    cross = send(piece, across_y())
    far = send(piece, by_x(2))
    moved = []
    for m in range(SLOTS - RECV):
        window = patches[0, 0, RECV + m]
        if moved:
            window, moved[-1] = lax.optimization_barrier((window, moved[-1]))
        moved.append(by_rank(window, m + 1))

    w_out = lax.dynamic_slice_in_dim(jnp.transpose(w_proj), half, HALF, 1)
    plus, minus, cross, far, w_out, *moved = lax.optimization_barrier(
        (plus, minus, cross, far, w_out, *moved)
    )
    cross_plus = send(cross, by_x(1))
    cross_minus = send(cross, by_x(-1))
    cross_far = send(far, across_y())
    w_mine = lax.all_gather(w_out, "fsdp", axis=0, tiled=True)
    meta = tables(route, groups, rank, lane // NYH, lane % NYH)

    placed, normed = pl.pallas_call(
        place_kernel,
        out_shape=[jax.ShapeDtypeStruct((ROWS, D), jnp.bfloat16)] * 2,
        in_specs=[SMEM] + vmem(5),
        out_specs=vmem(2),
        compiler_params=PARAMS,
    )(meta, patches[:, :, :RECV], *moved, norm_gain.reshape(1, D))
    normed_other = send(normed, other_core())
    cross_plus, cross_minus, cross_far, w_mine, normed_other = lax.optimization_barrier(
        (cross_plus, cross_minus, cross_far, w_mine, normed_other)
    )
    w_other = send(w_mine, other_core())

    att, att_theirs = pl.pallas_call(
        attend_kernel,
        out_shape=[jax.ShapeDtypeStruct((ROWS, HALF), jnp.bfloat16)] * 2,
        in_specs=[SMEM] + vmem(3) + [pl.BlockSpec(memory_space=pltpu.HBM)] * SHARDS,
        out_specs=vmem(2),
        scratch_shapes=[pltpu.VMEM((D, 3 * HALF), jnp.bfloat16)]
        + [pltpu.VMEM((2 * ROWS, HALF), jnp.bfloat16)] * 3
        + [pltpu.SemaphoreType.DMA((SHARDS,))],
        compiler_params=PARAMS,
    )(
        meta, normed, normed_other, bias.reshape(1, 3 * HALF),
        piece, plus, minus, cross, far, cross_plus, cross_minus, cross_far,
    )
    att_other = send(att_theirs, other_core())

    merged = pl.pallas_call(
        merge_kernel,
        out_shape=jax.ShapeDtypeStruct((ROWS // MERGE, MERGE * D), jnp.bfloat16),
        in_specs=[SMEM] + vmem(7),
        out_specs=vmem(1)[0],
        scratch_shapes=[pltpu.VMEM((D // 128, ROWS, 128), jnp.float32)],
        compiler_params=PARAMS,
    )(
        meta, att, att_other, w_mine, w_other, placed,
        b_proj.reshape(1, D), merge_gain.reshape(1, D),
    )
    return merged.reshape(1, 1, RECV, WIN // MERGE, MERGE * D)


def solution(mesh):
    return jax.shard_map(
        on_device,
        mesh=mesh,
        in_specs=(
            P("dp", "fsdp", None, None, None),
            P(),
            P("fsdp", None),
            P(),
            P(None, "fsdp"),
            P(),
            P(),
            P(None, "fsdp", None),
            P(None, "fsdp", None, None),
        ),
        out_specs=P("dp", "fsdp", None, None, None),
        check_vma=False,
    )
```

time: 269 us -> 156 us (0.58)
  waiting for transfers between devices: 195 us -> 60.1 us
  starting transfers between devices: 10.6 us -> 48.2 us
  matrix products: 16.2 us -> 0 us
  Pallas kernels: 0 us -> 11 us
  other arithmetic: 8.24 us -> 1.19 us
    all_gather x2 -> x1, waiting for transfers between devices: 189 us -> 26.8 us  [on_device(): w_mine = lax.all_gather(w_out, 'fsdp', axis=0, tiled=True)]
    ppermute x3 -> x13, starting transfers between devices: 10.5 us -> 48.2 us  [the longest x10 35.9 us: send(): return lax.ppermute(value, AXES, pairs)]
    ppermute x3 -> x13, waiting for transfers between devices: 5.19 us -> 33.3 us  [the longest x3 17.9 us: by_rank(): lax.ppermute(value, 'dp', [(i, (i + by) % devices) for i in range(devices)])]
    dot_general x4 -> x0, matrix products: 16.2 us -> none  [the longest x1 9.97 us: encode(): jnp.dot(flat_rows, lax.all_gather(w_qkv, 'fsdp', axis=0, tiled=True), pre...]
    reshape x3 -> x4, local copies, waits for them, and re-layouts: 15 us -> 0.03 us  [the longest x1 0.01 us: on_device(): bias.reshape(1, 3 * HALF)]
    unnamed x14 -> x53, local copies, waits for them, and re-layouts: 0.03 us -> 14.9 us
    pallas_call x0 -> x3, Pallas kernels: none -> 11 us  [the longest x1 6.72 us: on_device(): pl.pallas_call(attend_kernel, out_shape=[jax.ShapeDtypeStruct((ROWS, HALF...]
    slice x3 -> x2, local copies, waits for them, and re-layouts: 5.28 us -> 1.65 us  [the longest x1 1.43 us: on_device(): patches[:, :, :RECV]]
  transfers between devices with their start and end apart: 5 -> 14, of which waited for: 3 -> 7; matrix products, arithmetic and copies ran while one was open for 14% -> 4% of each run, Pallas kernels for 0% -> 5%
where the time goes in v1:
time: 156 us; the launch traced here: 155 us
  waiting for transfers between devices  60.1 us (39%)
  starting transfers between devices  48.2 us (31%)
  local copies, waits for them, and re-layouts  20.5 us (13%)
  between operations  13.8 us (9%)
  Pallas kernels  11 us (7%)
    ppermute x10, starting transfers between devices, send(): return lax.ppermute(value, AXES, pairs)  35.9 us
    all_gather x1, waiting for transfers between devices, on_device(): w_mine = lax.all_gather(w_out, 'fsdp', axis=0, tiled=True)  26.8 us
    ppermute x3, waiting for transfers between devices, by_rank(): lax.ppermute(value, 'dp', [(i, (i + by) % devices) for i in range(devices)])  17.9 us
    ppermute x10, waiting for transfers between devices, send(): return lax.ppermute(value, AXES, pairs)  15.4 us
    unnamed x53, local copies, waits for them, and re-layouts  14.9 us
    ppermute x3, starting transfers between devices, by_rank(): lax.ppermute(value, 'dp', [(i, (i + by) % devices) for i in range(devices)])  12.3 us
    pallas_call x1, Pallas kernels, on_device(): pl.pallas_call(attend_kernel, out_shape=[jax.ShapeDtypeStruct((ROWS, HALF...  6.72 us
  transfers between devices with their start and end apart: 14, of which 7 were waited for; matrix products, arithmetic and copies ran while one was open for 4% of the time, Pallas kernels for 5%

profile of v1, /device:TPU:1, one launch (start us, length us, event | category | flops | bytes accessed | tf_op | source)
XLA Modules:
  0.0 154.8 jit_solution(11380248839602057648)
XLA Ops:
  6.5 1.2 constant_dynamic-slice_fusion.2
  7.8 0.1 pad_maximum_fusion.rest_0_
  7.8 3.9 %collective-permute-start = (bf16[160,1920]{1,0:T(8,128)(2,1)S(1)}, bf16[160,1920]{1,0:T(8,128)(2,1)S(1)}, u32[]{:S(2)}, u32[]{:S(2)}) collective-permute-start(bf16[160,1920]{1,0:T(8,128)(2,1)S(1)} %pad_maximum_fusion.rest_0_), channel_id=1, source_target_pairs={{0,2},{8,10},{16,18},{24,26},{32,34},{40,42},{48,50},{56,58},{64,6... | collective-permute-start | bytes 1843208 | tf_op jit(solution)/shard_map/ppermute | solution.py:56
  11.8 3.2 %collective-permute-start.1 = (bf16[160,1920]{1,0:T(8,128)(2,1)S(1)}, bf16[160,1920]{1,0:T(8,128)(2,1)S(1)}, u32[]{:S(2)}, u32[]{:S(2)}) collective-permute-start(bf16[160,1920]{1,0:T(8,128)(2,1)S(1)} %pad_maximum_fusion.rest_0_), channel_id=1, source_target_pairs={{0,6},{8,14},{16,22},{24,30},{32,38},{40,46},{48,54},{56,62},{64,7... | collective-permute-start | bytes 1843208 | tf_op jit(solution)/shard_map/ppermute | solution.py:56
  15.0 4.8 %collective-permute-start.2 = (bf16[160,1920]{1,0:T(8,128)(2,1)S(1)}, bf16[160,1920]{1,0:T(8,128)(2,1)S(1)}, u32[]{:S(2)}, u32[]{:S(2)}) collective-permute-start(bf16[160,1920]{1,0:T(8,128)(2,1)S(1)} %pad_maximum_fusion.rest_0_), channel_id=1, source_target_pairs={{0,257},{8,265},{16,273},{24,281},{32,289},{40,297},{48,305},{56,3... | collective-permute-start | bytes 1843208 | tf_op jit(solution)/shard_map/ppermute | solution.py:56
  19.8 3.4 %collective-permute-start.3 = (bf16[160,1920]{1,0:T(8,128)(2,1)S(1)}, bf16[160,1920]{1,0:T(8,128)(2,1)S(1)}, u32[]{:S(2)}, u32[]{:S(2)}) collective-permute-start(bf16[160,1920]{1,0:T(8,128)(2,1)S(1)} %pad_maximum_fusion.rest_0_), channel_id=1, source_target_pairs={{0,4},{8,12},{16,20},{24,28},{32,36},{40,44},{48,52},{56,60},{64,6... | collective-permute-start | bytes 1843208 | tf_op jit(solution)/shard_map/ppermute | solution.py:56
  23.3 1.8 %slice_bitcast_fusion = (bf16[64,1280]{1,0:T(8,128)(2,1)}, bf16[64,1280]{1,0:T(8,128)(2,1)S(1)}, bf16[64,1280]{1,0:T(8,128)(2,1)S(1)}) fusion(bf16[1,1,7,64,1280]{4,3,2,1,0:T(8,128)(2,1)} %param.9), kind=kLoop, calls=%fused_computation.2 | loop fusion | bytes 983040 | tf_op jit(solution)/shard_map/squeeze | solution.py:196
  25.1 5.3 %collective-permute-start.4 = (bf16[64,1280]{1,0:T(8,128)(2,1)S(1)}, bf16[64,1280]{1,0:T(8,128)(2,1)S(1)}, u32[]{:S(2)}, u32[]{:S(2)}) collective-permute-start(bf16[64,1280]{1,0:T(8,128)(2,1)S(1)} %get-tuple-element.56), channel_id=1, source_target_pairs={{0,8},{8,16},{16,24},{24,32},{32,40},{40,48},{48,56},{56,64},{64,7... | collective-permute-start | bytes 491528 | tf_op jit(solution)/shard_map/ppermute | solution.py:61
  30.4 2.2 %collective-permute-done.4.in0 = bf16[64,1280]{1,0:T(8,128)(2,1)S(1)} collective-permute-done((bf16[64,1280]{1,0:T(8,128)(2,1)S(1)}, bf16[64,1280]{1,0:T(8,128)(2,1)S(1)}, u32[]{:S(2)}, u32[]{:S(2)}) %collective-permute-start.4) | collective-permute-done | bytes 163872 | tf_op jit(solution)/shard_map/ppermute | solution.py:61
  32.7 0.7 copy-done.16
  33.3 3.5 %collective-permute-start.5 = (bf16[64,1280]{1,0:T(8,128)(2,1)S(1)}, bf16[64,1280]{1,0:T(8,128)(2,1)S(1)}, u32[]{:S(2)}, u32[]{:S(2)}) collective-permute-start(bf16[64,1280]{1,0:T(8,128)(2,1)S(1)} %get-tuple-element.27), channel_id=1, source_target_pairs={{0,16},{8,24},{16,32},{24,40},{32,48},{40,56},{48,64},{56,72},{64,... | collective-permute-start | bytes 491528 | tf_op jit(solution)/shard_map/ppermute | solution.py:61
  36.9 7.0 %collective-permute-done.5.in1 = bf16[64,1280]{1,0:T(8,128)(2,1)S(1)} collective-permute-done((bf16[64,1280]{1,0:T(8,128)(2,1)S(1)}, bf16[64,1280]{1,0:T(8,128)(2,1)S(1)}, u32[]{:S(2)}, u32[]{:S(2)}) %collective-permute-start.5) | collective-permute-done | bytes 163872 | tf_op jit(solution)/shard_map/ppermute | solution.py:61
  43.8 0.7 copy-done.18
  44.5 3.4 %collective-permute-start.6 = (bf16[64,1280]{1,0:T(8,128)(2,1)}, bf16[64,1280]{1,0:T(8,128)(2,1)}, u32[]{:S(2)}, u32[]{:S(2)}) collective-permute-start(bf16[64,1280]{1,0:T(8,128)(2,1)} %get-tuple-element.29), channel_id=1, source_target_pairs={{0,24},{8,32},{16,40},{24,48},{32,56},{40,64},{48,72},{56,80},{64,... | collective-permute-start | bytes 491528 | tf_op jit(solution)/shard_map/ppermute | solution.py:61
  47.9 0.7 dynamic-slice_bitcast_fusion
  48.6 8.7 %collective-permute-done.6.in2 = bf16[64,1280]{1,0:T(8,128)(2,1)} collective-permute-done((bf16[64,1280]{1,0:T(8,128)(2,1)}, bf16[64,1280]{1,0:T(8,128)(2,1)}, u32[]{:S(2)}, u32[]{:S(2)}) %collective-permute-start.6) | collective-permute-done | bytes 163872 | tf_op jit(solution)/shard_map/ppermute | solution.py:61
  57.4 0.0 collective-permute-done.rest_1_
  57.4 0.8 copy-done.2
  58.2 0.0 collective-permute-done.1.rest_2_
  58.2 0.8 copy-done.4
  59.0 0.0 collective-permute-done.2.rest_3_
  59.0 0.0 collective-permute-done.3.rest_4_
  59.0 0.0 all-gather.2.cloned.1.call-update
  59.2 0.0 copy-start.20
  59.2 1.4 slice.32.own
  60.7 0.1 pad_add_fusion
  60.7 0.1 fusion.2
  60.8 0.3 select_reduce_fusion.1
  61.1 0.1 copy.13
  61.2 0.3 select_reduce_fusion
  61.5 0.2 slice_reduce_fusion
  61.8 0.2 fusion
  62.0 0.2 select_reduce_fusion.2
  62.2 0.1 concatenate.9.meta
  62.3 0.9 copy-done.17
  63.2 0.9 copy-done.19
  64.1 1.3 shard_map.91
  65.4 5.2 %collective-permute-start.10 = (bf16[256,1280]{1,0:T(8,128)(2,1)S(1)}, bf16[256,1280]{1,0:T(8,128)(2,1)S(1)}, u32[]{:S(2)}, u32[]{:S(2)}) collective-permute-start(bf16[256,1280]{1,0:T(8,128)(2,1)S(1)} %get-tuple-element.33.xa), channel_id=1, source_target_pairs={{0,8},{8,0},{16,24},{24,16},{32,40},{40,32},{48,56},{56,48},{64,72... | collective-permute-start | bytes 1966088 | tf_op jit(solution)/shard_map/ppermute | solution.py:56
  70.6 2.2 %collective-permute-start.7 = (bf16[160,1920]{1,0:T(8,128)(2,1)}, bf16[160,1920]{1,0:T(8,128)(2,1)S(1)}, u32[]{:S(2)}, u32[]{:S(2)}) collective-permute-start(bf16[160,1920]{1,0:T(8,128)(2,1)} %copy-done.6), channel_id=1, source_target_pairs={{0,2},{8,10},{16,18},{24,26},{32,34},{40,42},{48,50},{56,58},{64,6... | collective-permute-start | bytes 1843208 | tf_op jit(solution)/shard_map/ppermute | solution.py:56
  72.8 4.3 %collective-permute-start.8 = (bf16[160,1920]{1,0:T(8,128)(2,1)}, bf16[160,1920]{1,0:T(8,128)(2,1)S(1)}, u32[]{:S(2)}, u32[]{:S(2)}) collective-permute-start(bf16[160,1920]{1,0:T(8,128)(2,1)} %copy-done.6), channel_id=1, source_target_pairs={{0,6},{8,14},{16,22},{24,30},{32,38},{40,46},{48,54},{56,62},{64,7... | collective-permute-start | bytes 1843208 | tf_op jit(solution)/shard_map/ppermute | solution.py:56
  77.1 2.7 %collective-permute-start.9 = (bf16[160,1920]{1,0:T(8,128)(2,1)}, bf16[160,1920]{1,0:T(8,128)(2,1)S(1)}, u32[]{:S(2)}, u32[]{:S(2)}) collective-permute-start(bf16[160,1920]{1,0:T(8,128)(2,1)} %copy-done.8), channel_id=1, source_target_pairs={{0,257},{8,265},{16,273},{24,281},{32,289},{40,297},{48,305},{56,3... | collective-permute-start | bytes 1843208 | tf_op jit(solution)/shard_map/ppermute | solution.py:56
  79.8 12.9 %collective-permute-done.7.rest_5_ = bf16[160,1920]{1,0:T(8,128)(2,1)S(1)} collective-permute-done((bf16[160,1920]{1,0:T(8,128)(2,1)}, bf16[160,1920]{1,0:T(8,128)(2,1)S(1)}, u32[]{:S(2)}, u32[]{:S(2)}) %collective-permute-start.7) | collective-permute-done | bytes 614432 | tf_op jit(solution)/shard_map/ppermute | solution.py:56
  92.7 0.8 copy-done.10
  93.5 0.0 collective-permute-done.8.rest_6_
  93.5 0.8 copy-done.12
  94.3 0.9 collective-permute-done.9.rest_7_
  95.3 0.9 copy-done.14
  96.1 0.0 collective-permute-done.10.xb
  96.1 26.8 %all-gather.2.cloned.1.call-done.wa = bf16[1280,640]{1,0:T(8,128)(2,1)} async-done(((bf16[160,640]{1,0:T(8,128)(2,1)}), bf16[1280,640]{1,0:T(8,128)(2,1)}) %all-gather.2.cloned.1.call-update) | async-done | bytes 1638416 | tf_op jit(solution)/shard_map/all_gather | solution.py:208
  122.9 4.2 %collective-permute-start.12 = (bf16[1280,640]{1,0:T(8,128)(2,1)}, bf16[1280,640]{1,0:T(8,128)(2,1)S(1)}, u32[]{:S(2)}, u32[]{:S(2)}) collective-permute-start(bf16[1280,640]{1,0:T(8,128)(2,1)} %all-gather.2.cloned.1.call-done.wa), channel_id=1, source_target_pairs={{0,8},{8,0},{16,24},{24,16},{32,40},{40,32},{48,56},{56,48},{64,72... | collective-permute-start | bytes 4915208 | tf_op jit(solution)/shard_map/ppermute | solution.py:56
  127.1 0.1 fusion.4
  127.2 0.0 copy-start.3
  127.2 1.1 copy-done.3
  128.3 1.1 copy-done.5
  129.3 1.1 copy-done.7
  130.4 1.1 copy-done.9
  131.5 1.1 copy-done.11
  132.6 1.1 copy-done.13
  133.6 1.1 copy-done.15
  134.7 6.7 %shard_map.92 = (bf16[256,640]{1,0:T(8,128)(2,1)S(1)}, bf16[256,640]{1,0:T(8,128)(2,1)S(1)}) custom-call(s32[20]{0:T(128)S(1)} %concatenate.9.meta, bf16[256,1280]{1,0:T(8,128)(2,1)S(1)} %get-tuple-element.33.xa, bf16[256,1280]{1,0:T(8,128)(2,1)S(1)} %collective-permute-done.10.xb, f32[1,1920]{1,0:T(1,128)S(1)} %reshape.81.bias, ...), custom_call_target="tpu_custom_call" | custom-call | tf_op jit(solution)/shard_map/pallas_call | solution.py:224
  141.4 1.9 %collective-permute-start.11 = (bf16[256,640]{1,0:T(8,128)(2,1)S(1)}, bf16[256,640]{1,0:T(8,128)(2,1)S(1)}, u32[]{:S(2)}, u32[]{:S(2)}) collective-permute-start(bf16[256,640]{1,0:T(8,128)(2,1)S(1)} %get-tuple-element.44), channel_id=1, source_target_pairs={{0,8},{8,0},{16,24},{24,16},{32,40},{40,32},{48,56},{56,48},{64,72... | collective-permute-start | bytes 983048 | tf_op jit(solution)/shard_map/ppermute | solution.py:56
  143.4 1.5 collective-permute-done.11.attb
  145.0 0.0 collective-permute-done.12.wb
  145.0 3.0 %shard_map.93 = bf16[64,5120]{1,0:T(8,128)(2,1)} custom-call(s32[20]{0:T(128)S(1)} %concatenate.9.meta, bf16[256,640]{1,0:T(8,128)(2,1)S(1)} %get-tuple-element.43.atta, bf16[256,640]{1,0:T(8,128)(2,1)S(1)} %collective-permute-done.11.attb, bf16[1280,640]{1,0:T(8,128)(2,1)S(1)} %copy-done.1, bf16[1280,640]{1,0:T(8,128)(2,1)S(1)} %collective-permute-done.12.wb, ...), custom_call_target="tpu_custom_call" | custom-call | tf_op jit(solution)/shard_map/pallas_call | solution.py:239
  (45 shorter events, 0.1 us)
Async XLA Ops:
  6.5 41.4 %copy-start = (bf16[1280,160]{0,1:T(8,128)(2,1)S(1)}, bf16[1280,160]{0,1:T(8,128)(2,1)}, u32[]{:S(2)}) copy-start(bf16[1280,160]{0,1:T(8,128)(2,1)} %param.13) | copy-start | bytes 1228804
  6.5 116.4 %all-gather.2.cloned.1.call-start = ((), (), s32[]{:S(2)}) async-start(), calls=%async_computation | async-start | bytes 1843200 | tf_op jit(solution)/shard_map/all_gather | solution.py:208
  7.8 49.5 %collective-permute-start = (bf16[160,1920]{1,0:T(8,128)(2,1)S(1)}, bf16[160,1920]{1,0:T(8,128)(2,1)S(1)}, u32[]{:S(2)}, u32[]{:S(2)}) collective-permute-start(bf16[160,1920]{1,0:T(8,128)(2,1)S(1)} %pad_maximum_fusion.rest_0_), channel_id=1, source_target_pairs={{0,2},{8,10},{16,18},{24,26},{32,34},{40,42},{48,50},{56,58},{64,6... | collective-permute-start | bytes 1843208 | tf_op jit(solution)/shard_map/ppermute | solution.py:56
  11.8 46.4 %collective-permute-start.1 = (bf16[160,1920]{1,0:T(8,128)(2,1)S(1)}, bf16[160,1920]{1,0:T(8,128)(2,1)S(1)}, u32[]{:S(2)}, u32[]{:S(2)}) collective-permute-start(bf16[160,1920]{1,0:T(8,128)(2,1)S(1)} %pad_maximum_fusion.rest_0_), channel_id=1, source_target_pairs={{0,6},{8,14},{16,22},{24,30},{32,38},{40,46},{48,54},{56,62},{64,7... | collective-permute-start | bytes 1843208 | tf_op jit(solution)/shard_map/ppermute | solution.py:56
  15.0 44.0 %collective-permute-start.2 = (bf16[160,1920]{1,0:T(8,128)(2,1)S(1)}, bf16[160,1920]{1,0:T(8,128)(2,1)S(1)}, u32[]{:S(2)}, u32[]{:S(2)}) collective-permute-start(bf16[160,1920]{1,0:T(8,128)(2,1)S(1)} %pad_maximum_fusion.rest_0_), channel_id=1, source_target_pairs={{0,257},{8,265},{16,273},{24,281},{32,289},{40,297},{48,305},{56,3... | collective-permute-start | bytes 1843208 | tf_op jit(solution)/shard_map/ppermute | solution.py:56
  19.8 39.2 %collective-permute-start.3 = (bf16[160,1920]{1,0:T(8,128)(2,1)S(1)}, bf16[160,1920]{1,0:T(8,128)(2,1)S(1)}, u32[]{:S(2)}, u32[]{:S(2)}) collective-permute-start(bf16[160,1920]{1,0:T(8,128)(2,1)S(1)} %pad_maximum_fusion.rest_0_), channel_id=1, source_target_pairs={{0,4},{8,12},{16,20},{24,28},{32,36},{40,44},{48,52},{56,60},{64,6... | collective-permute-start | bytes 1843208 | tf_op jit(solution)/shard_map/ppermute | solution.py:56
  25.0 35.6 %copy-start.25 = (s32[64,1,7]{0,1,2:T(1,128)S(1)}, s32[64,1,7]{0,1,2:T(1,128)}, u32[]{:S(2)}) copy-start(s32[64,1,7]{0,1,2:T(1,128)} %param.16) | copy-start | bytes 5380
  25.1 36.1 %copy-start.21 = (f32[1280]{0:T(1024)S(1)}, f32[1280]{0:T(1024)}, u32[]{:S(2)}) copy-start(f32[1280]{0:T(1024)} %param.10) | copy-start | bytes 15364
  25.1 36.2 %copy-start.24 = (s32[64,1,7,2]{0,3,2,1:T(2,128)S(1)}, s32[64,1,7,2]{0,3,2,1:T(2,128)}, u32[]{:S(2)}) copy-start(s32[64,1,7,2]{0,3,2,1:T(2,128)} %param.17) | copy-start | bytes 10756
  25.1 7.6 %collective-permute-start.4 = (bf16[64,1280]{1,0:T(8,128)(2,1)S(1)}, bf16[64,1280]{1,0:T(8,128)(2,1)S(1)}, u32[]{:S(2)}, u32[]{:S(2)}) collective-permute-start(bf16[64,1280]{1,0:T(8,128)(2,1)S(1)} %get-tuple-element.56), channel_id=1, source_target_pairs={{0,8},{8,16},{16,24},{24,32},{32,40},{40,48},{48,56},{56,64},{64,7... | collective-permute-start | bytes 491528 | tf_op jit(solution)/shard_map/ppermute | solution.py:61
  32.7 0.7 copy-start.16
  33.3 10.5 %collective-permute-start.5 = (bf16[64,1280]{1,0:T(8,128)(2,1)S(1)}, bf16[64,1280]{1,0:T(8,128)(2,1)S(1)}, u32[]{:S(2)}, u32[]{:S(2)}) collective-permute-start(bf16[64,1280]{1,0:T(8,128)(2,1)S(1)} %get-tuple-element.27), channel_id=1, source_target_pairs={{0,16},{8,24},{16,32},{24,40},{32,48},{40,56},{48,64},{56,72},{64,... | collective-permute-start | bytes 491528 | tf_op jit(solution)/shard_map/ppermute | solution.py:61
  43.8 0.7 copy-start.18
  44.5 12.9 %collective-permute-start.6 = (bf16[64,1280]{1,0:T(8,128)(2,1)}, bf16[64,1280]{1,0:T(8,128)(2,1)}, u32[]{:S(2)}, u32[]{:S(2)}) collective-permute-start(bf16[64,1280]{1,0:T(8,128)(2,1)} %get-tuple-element.29), channel_id=1, source_target_pairs={{0,24},{8,32},{16,40},{24,48},{32,56},{40,64},{48,72},{56,80},{64,... | collective-permute-start | bytes 491528 | tf_op jit(solution)/shard_map/ppermute | solution.py:61
  57.4 0.8 copy-start.2
  58.2 0.8 copy-start.4
  59.0 3.1 %copy-start.6 = (bf16[160,1920]{1,0:T(8,128)(2,1)}, bf16[160,1920]{1,0:T(8,128)(2,1)S(1)}, u32[]{:S(2)}) copy-start(bf16[160,1920]{1,0:T(8,128)(2,1)S(1)} %collective-permute-done.2.rest_3_) | copy-start | bytes 1843204
  59.0 3.1 %copy-start.8 = (bf16[160,1920]{1,0:T(8,128)(2,1)}, bf16[160,1920]{1,0:T(8,128)(2,1)S(1)}, u32[]{:S(2)}) copy-start(bf16[160,1920]{1,0:T(8,128)(2,1)S(1)} %collective-permute-done.3.rest_4_) | copy-start | bytes 1843204
  59.2 67.9 %copy-start.20 = (f32[3840]{0:T(1024)S(1)}, f32[3840]{0:T(1024)}, u32[]{:S(2)}) copy-start(f32[3840]{0:T(1024)} %param.12) | copy-start | bytes 46084
  62.3 0.9 copy-start.17
  63.2 0.9 copy-start.19
  65.4 30.7 %collective-permute-start.10 = (bf16[256,1280]{1,0:T(8,128)(2,1)S(1)}, bf16[256,1280]{1,0:T(8,128)(2,1)S(1)}, u32[]{:S(2)}, u32[]{:S(2)}) collective-permute-start(bf16[256,1280]{1,0:T(8,128)(2,1)S(1)} %get-tuple-element.33.xa), channel_id=1, source_target_pairs={{0,8},{8,0},{16,24},{24,16},{32,40},{40,32},{48,56},{56,48},{64,72... | collective-permute-start | bytes 1966088 | tf_op jit(solution)/shard_map/ppermute | solution.py:56
  70.6 22.1 %collective-permute-start.7 = (bf16[160,1920]{1,0:T(8,128)(2,1)}, bf16[160,1920]{1,0:T(8,128)(2,1)S(1)}, u32[]{:S(2)}, u32[]{:S(2)}) collective-permute-start(bf16[160,1920]{1,0:T(8,128)(2,1)} %copy-done.6), channel_id=1, source_target_pairs={{0,2},{8,10},{16,18},{24,26},{32,34},{40,42},{48,50},{56,58},{64,6... | collective-permute-start | bytes 1843208 | tf_op jit(solution)/shard_map/ppermute | solution.py:56
  72.8 20.7 %collective-permute-start.8 = (bf16[160,1920]{1,0:T(8,128)(2,1)}, bf16[160,1920]{1,0:T(8,128)(2,1)S(1)}, u32[]{:S(2)}, u32[]{:S(2)}) collective-permute-start(bf16[160,1920]{1,0:T(8,128)(2,1)} %copy-done.6), channel_id=1, source_target_pairs={{0,6},{8,14},{16,22},{24,30},{32,38},{40,46},{48,54},{56,62},{64,7... | collective-permute-start | bytes 1843208 | tf_op jit(solution)/shard_map/ppermute | solution.py:56
  77.1 18.2 %collective-permute-start.9 = (bf16[160,1920]{1,0:T(8,128)(2,1)}, bf16[160,1920]{1,0:T(8,128)(2,1)S(1)}, u32[]{:S(2)}, u32[]{:S(2)}) collective-permute-start(bf16[160,1920]{1,0:T(8,128)(2,1)} %copy-done.8), channel_id=1, source_target_pairs={{0,257},{8,265},{16,273},{24,281},{32,289},{40,297},{48,305},{56,3... | collective-permute-start | bytes 1843208 | tf_op jit(solution)/shard_map/ppermute | solution.py:56
  92.7 0.8 copy-start.10
  93.5 0.8 copy-start.12
  95.3 0.9 copy-start.14
  122.9 22.1 %collective-permute-start.12 = (bf16[1280,640]{1,0:T(8,128)(2,1)}, bf16[1280,640]{1,0:T(8,128)(2,1)S(1)}, u32[]{:S(2)}, u32[]{:S(2)}) collective-permute-start(bf16[1280,640]{1,0:T(8,128)(2,1)} %all-gather.2.cloned.1.call-done.wa), channel_id=1, source_target_pairs={{0,8},{8,0},{16,24},{24,16},{32,40},{40,32},{48,56},{56,48},{64,72... | collective-permute-start | bytes 4915208 | tf_op jit(solution)/shard_map/ppermute | solution.py:56
  127.2 1.1 copy-start.3
  128.3 1.1 copy-start.5
  129.3 1.1 copy-start.7
  130.4 1.1 copy-start.9
  131.5 1.1 copy-start.11
  132.6 1.1 copy-start.13
  133.6 1.1 copy-start.15
  134.7 8.7 %copy-start.22 = (f32[1280]{0:T(1024)S(1)}, f32[1280]{0:T(1024)}, u32[]{:S(2)}) copy-start(f32[1280]{0:T(1024)} %param.14) | copy-start | bytes 15364
  134.7 8.7 %copy-start.23 = (f32[1280]{0:T(1024)S(1)}, f32[1280]{0:T(1024)}, u32[]{:S(2)}) copy-start(f32[1280]{0:T(1024)} %param.15) | copy-start | bytes 15364
  134.7 10.3 %copy-start.1 = (bf16[1280,640]{1,0:T(8,128)(2,1)S(1)}, bf16[1280,640]{1,0:T(8,128)(2,1)}, u32[]{:S(2)}) copy-start(bf16[1280,640]{1,0:T(8,128)(2,1)} %all-gather.2.cloned.1.call-done.wa) | copy-start | bytes 4915204
  141.4 3.5 %collective-permute-start.11 = (bf16[256,640]{1,0:T(8,128)(2,1)S(1)}, bf16[256,640]{1,0:T(8,128)(2,1)S(1)}, u32[]{:S(2)}, u32[]{:S(2)}) collective-permute-start(bf16[256,640]{1,0:T(8,128)(2,1)S(1)} %get-tuple-element.44), channel_id=1, source_target_pairs={{0,8},{8,0},{16,24},{24,16},{32,40},{40,32},{48,56},{56,48},{64,72... | collective-permute-start | bytes 983048 | tf_op jit(solution)/shard_map/ppermute | solution.py:56
Sparse Core Ops, SparseCore 0:
  59.2 63.6 all-gather.1

commit v2 on v1

--- a/solution.py
+++ b/solution.py
@@ -61,30 +61,42 @@
     return lax.ppermute(value, "dp", [(i, (i + by) % devices) for i in range(devices)])
 
 
-def place_kernel(meta, own, in0, in1, in2, gain, placed, normed):
+def place_kernel(meta, own, in0, in1, in2, gain, placed, normed, sems):
     for t in range(RECV):
-        src = meta[t]
-        window = jnp.where(
-            src < RECV,
-            own[0, 0, t],
-            jnp.where(src == RECV, in0[...], jnp.where(src == RECV + 1, in1[...], in2[...])),
-        )
-        placed[pl.ds(t * WIN, WIN), :] = window
-        x = window.astype(jnp.float32)
+        rows = placed.at[pl.ds(t * WIN, WIN), :]
+        kept = own.at[0, 0, t]
+        for at, ref in enumerate((kept, in0, in1, in2)):
+            here = meta[t] < RECV if at == 0 else meta[t] == RECV - 1 + at
+
+            @pl.when(here)
+            def _(ref=ref, rows=rows, t=t):
+                pltpu.make_async_copy(ref, rows, sems.at[t]).start()
+
+    for t in range(RECV):
+        rows = pl.ds(t * WIN, WIN)
+        pltpu.make_async_copy(own.at[0, 0, t], placed.at[rows, :], sems.at[t]).wait()
+        x = placed[rows, :].astype(jnp.float32)
         ms = jnp.mean(x * x, axis=-1, keepdims=True)
-        normed[pl.ds(t * WIN, WIN), :] = (x * lax.rsqrt(ms + EPS) * gain[...]).astype(jnp.bfloat16)
-
-
-def attend_kernel(meta, xa, xb, bias, *rest):
-    pieces, (outa, outb, w, q, k, v, sems) = rest[:SHARDS], rest[SHARDS:]
+        normed[rows, :] = (x * lax.rsqrt(ms + EPS) * gain[...]).astype(jnp.bfloat16)
+
+
+def gather_kernel(meta, *rest):
+    pieces, (_, w, wo, sems) = rest[:SHARDS], rest[SHARDS:]
     copies = []
     for i in range(SHARDS):
-        at = pl.multiple_of(meta[12 + i] * DEPTH, DEPTH)
-        copies.append(pltpu.make_async_copy(pieces[i], w.at[pl.ds(at, DEPTH), :], sems.at[i]))
+        at = pl.ds(pl.multiple_of(meta[12 + i] * DEPTH, DEPTH), DEPTH)
+        for j, dst in enumerate((w, wo)):
+            cols = pl.ds(j * 3 * HALF, (3 - 2 * j) * HALF)
+            copies.append(
+                pltpu.make_async_copy(pieces[i].at[:, cols], dst.at[at, :], sems.at[i, j])
+            )
     for copy in copies:
         copy.start()
     for copy in copies:
         copy.wait()
+
+
+def attend_kernel(meta, xa, xb, bias, w, outa, outb, q, k, v):
     for j, dst in enumerate((q, k, v)):
         cols = pl.ds(j * HALF, HALF)
         for i, src in enumerate((xa, xb)):
@@ -152,6 +164,8 @@
     return [pl.BlockSpec(memory_space=pltpu.VMEM)] * n
 
 
+ANY = pl.BlockSpec(memory_space=pl.ANY)
+SMALL = pltpu.CompilerParams(vmem_limit_bytes=4 * 1024 * 1024)
 SMEM = pl.BlockSpec(memory_space=pltpu.SMEM)
 PARAMS = pltpu.CompilerParams(vmem_limit_bytes=20 * 1024 * 1024)
 
@@ -182,58 +196,56 @@
     half = core * HALF
 
     piece = jnp.concatenate(
-        [lax.dynamic_slice_in_dim(w_qkv, j * D + half, HALF, 1) for j in range(3)], axis=1
+        [lax.dynamic_slice_in_dim(w_qkv, j * D + half, HALF, 1) for j in range(3)]
+        + [lax.dynamic_slice_in_dim(jnp.transpose(w_proj), half, HALF, 1)],
+        axis=1,
     )
     bias = jnp.concatenate(
         [lax.dynamic_slice_in_dim(b_qkv, j * D + half, HALF, 0) for j in range(3)]
     )
+    far = send(piece, by_x(2))
+    cross = send(piece, across_y())
     plus = send(piece, by_x(1))
     minus = send(piece, by_x(-1))
-    cross = send(piece, across_y())
-    far = send(piece, by_x(2))
-    moved = []
-    for m in range(SLOTS - RECV):
-        window = patches[0, 0, RECV + m]
-        if moved:
-            window, moved[-1] = lax.optimization_barrier((window, moved[-1]))
-        moved.append(by_rank(window, m + 1))
-
-    w_out = lax.dynamic_slice_in_dim(jnp.transpose(w_proj), half, HALF, 1)
-    plus, minus, cross, far, w_out, *moved = lax.optimization_barrier(
-        (plus, minus, cross, far, w_out, *moved)
-    )
     cross_plus = send(cross, by_x(1))
     cross_minus = send(cross, by_x(-1))
     cross_far = send(far, across_y())
-    w_mine = lax.all_gather(w_out, "fsdp", axis=0, tiled=True)
+
+    moved = [by_rank(patches[0, 0, RECV + m], m + 1) for m in range(SLOTS - RECV)]
+
     meta = tables(route, groups, rank, lane // NYH, lane % NYH)
 
     placed, normed = pl.pallas_call(
         place_kernel,
         out_shape=[jax.ShapeDtypeStruct((ROWS, D), jnp.bfloat16)] * 2,
-        in_specs=[SMEM] + vmem(5),
+        in_specs=[SMEM] + [ANY] * 4 + vmem(1),
         out_specs=vmem(2),
+        scratch_shapes=[pltpu.SemaphoreType.DMA((RECV,))],
+        compiler_params=SMALL,
+    )(meta, patches, *moved, norm_gain.reshape(1, D))
+    normed_other = send(normed, other_core())
+
+    w, w_mine = pl.pallas_call(
+        gather_kernel,
+        out_shape=[
+            jax.ShapeDtypeStruct((D, 3 * HALF), jnp.bfloat16),
+            jax.ShapeDtypeStruct((D, HALF), jnp.bfloat16),
+        ],
+        in_specs=[SMEM] + [ANY] * (SHARDS + 1),
+        out_specs=vmem(2),
+        scratch_shapes=[pltpu.SemaphoreType.DMA((SHARDS, 2))],
         compiler_params=PARAMS,
-    )(meta, patches[:, :, :RECV], *moved, norm_gain.reshape(1, D))
-    normed_other = send(normed, other_core())
-    cross_plus, cross_minus, cross_far, w_mine, normed_other = lax.optimization_barrier(
-        (cross_plus, cross_minus, cross_far, w_mine, normed_other)
-    )
+    )(meta, piece, plus, minus, cross, far, cross_plus, cross_minus, cross_far, normed_other)
     w_other = send(w_mine, other_core())
 
     att, att_theirs = pl.pallas_call(
         attend_kernel,
         out_shape=[jax.ShapeDtypeStruct((ROWS, HALF), jnp.bfloat16)] * 2,
-        in_specs=[SMEM] + vmem(3) + [pl.BlockSpec(memory_space=pltpu.HBM)] * SHARDS,
+        in_specs=[SMEM] + vmem(4),
         out_specs=vmem(2),
-        scratch_shapes=[pltpu.VMEM((D, 3 * HALF), jnp.bfloat16)]
-        + [pltpu.VMEM((2 * ROWS, HALF), jnp.bfloat16)] * 3
-        + [pltpu.SemaphoreType.DMA((SHARDS,))],
+        scratch_shapes=[pltpu.VMEM((2 * ROWS, HALF), jnp.bfloat16)] * 3,
         compiler_params=PARAMS,
-    )(
-        meta, normed, normed_other, bias.reshape(1, 3 * HALF),
-        piece, plus, minus, cross, far, cross_plus, cross_minus, cross_far,
-    )
+    )(meta, normed, normed_other, bias.reshape(1, 3 * HALF), w)
     att_other = send(att_theirs, other_core())
 
     merged = pl.pallas_call(

time: 156 us -> 89.4 us (0.57)
  waiting for transfers between devices: 60.1 us -> 18.3 us
  local copies, waits for them, and re-layouts: 20.5 us -> 5.25 us
  between operations: 13.8 us -> 0.46 us
  Pallas kernels: 11 us -> 13.4 us
  starting transfers between devices: 48.2 us -> 49.9 us
    all_gather x1 -> x0, waiting for transfers between devices: 26.8 us -> none  [on_device(): w_mine = lax.all_gather(w_out, 'fsdp', axis=0, tiled=True)]
    ppermute x3, waiting for transfers between devices: 17.9 us -> 3.12 us  [by_rank(): lax.ppermute(value, 'dp', [(i, (i + by) % devices) for i in range(devices)])]
    unnamed x53 -> x21, local copies, waits for them, and re-layouts: 14.9 us -> 2.62 us
    pallas_call x0 -> x1, Pallas kernels: none -> 3.13 us  [on_device(): pl.pallas_call(gather_kernel, out_shape=[jax.ShapeDtypeStruct((D, 3 * HAL...]
    ppermute x10, starting transfers between devices: 35.9 us -> 37.9 us  [send(): return lax.ppermute(value, AXES, pairs)]
  transfers between devices with their start and end apart: 14 -> 13, of which waited for: 7 -> 6; matrix products, arithmetic and copies ran while one was open for 4% -> 3% of each run, Pallas kernels for 5% -> 8%
where the time goes in v2:
time: 89.4 us; the launch traced here: 88.6 us
  starting transfers between devices  49.9 us (56%)
  waiting for transfers between devices  18.3 us (20%)
  Pallas kernels  13.4 us (15%)
  local copies, waits for them, and re-layouts  5.25 us (6%)
  other arithmetic  1.19 us (1%)
    ppermute x10, starting transfers between devices, send(): return lax.ppermute(value, AXES, pairs)  37.9 us
    ppermute x10, waiting for transfers between devices, send(): return lax.ppermute(value, AXES, pairs)  15.2 us
    ppermute x3, starting transfers between devices, by_rank(): lax.ppermute(value, 'dp', [(i, (i + by) % devices) for i in range(devices)])  12 us
    pallas_call x1, Pallas kernels, on_device(): pl.pallas_call(attend_kernel, out_shape=[jax.ShapeDtypeStruct((ROWS, HALF...  5.25 us
    pallas_call x1, Pallas kernels, on_device(): pl.pallas_call(gather_kernel, out_shape=[jax.ShapeDtypeStruct((D, 3 * HAL...  3.13 us
    ppermute x3, waiting for transfers between devices, by_rank(): lax.ppermute(value, 'dp', [(i, (i + by) % devices) for i in range(devices)])  3.12 us
    pallas_call x1, Pallas kernels, on_device(): pl.pallas_call(merge_kernel, out_shape=jax.ShapeDtypeStruct((ROWS // MERG...  2.94 us
    unnamed x21, local copies, waits for them, and re-layouts  2.62 us
  transfers between devices with their start and end apart: 13, of which 6 were waited for; matrix products, arithmetic and copies ran while one was open for 3% of the time, Pallas kernels for 8%

profile of v2, /device:TPU:1, one launch (start us, length us, event | category | flops | bytes accessed | tf_op | source)
XLA Modules:
  0.0 88.6 jit_solution(18164481534764016223)
XLA Ops:
  0.0 0.0 copy-start
  0.0 1.0 %copy-done = bf16[1280,160]{0,1:T(8,128)(2,1)S(1)} copy-done((bf16[1280,160]{0,1:T(8,128)(2,1)S(1)}, bf16[1280,160]{0,1:T(8,128)(2,1)}, u32[]{:S(2)}) %copy-start) | copy-done | bytes 409624
  1.0 0.0 copy-start.1
  1.0 0.0 copy-start.9
  1.0 1.3 %constant_dynamic-slice_fusion.2 = (bf16[160,640]{1,0:T(8,128)(2,1)S(1)}, bf16[160,640]{1,0:T(8,128)(2,1)S(1)}, bf16[160,640]{1,0:T(8,128)(2,1)S(1)}) fusion(bf16[160,3840]{1,0:T(8,128)(2,1)} %param.11, s32[]{:T(128)S(6)} %select_n.123, s32[]{:T(128)S(6)} %select_n.125, s32[]{:T(128)S(6)} %select_n.124), kind=kLoop, calls=%fused_computation.24 | loop fusion | bytes 1228812 | tf_op jit(solution)/shard_map/dynamic_slice | solution.py:199
  2.3 0.0 copy-start.8
  2.3 0.0 copy-start.5
  2.3 0.1 pad_maximum_fusion.rest_0_
  2.4 5.5 %collective-permute-start.7 = (bf16[160,2560]{1,0:T(8,128)(2,1)S(1)}, bf16[160,2560]{1,0:T(8,128)(2,1)S(1)}, u32[]{:S(2)}, u32[]{:S(2)}) collective-permute-start(bf16[160,2560]{1,0:T(8,128)(2,1)S(1)} %pad_maximum_fusion.rest_0_), channel_id=1, source_target_pairs={{0,4},{8,12},{16,20},{24,28},{32,36},{40,44},{48,52},{56,60},{64,6... | collective-permute-start | bytes 2457608 | tf_op jit(solution)/shard_map/ppermute | solution.py:56
  7.9 4.6 %collective-permute-start.6 = (bf16[160,2560]{1,0:T(8,128)(2,1)S(1)}, bf16[160,2560]{1,0:T(8,128)(2,1)}, u32[]{:S(2)}, u32[]{:S(2)}) collective-permute-start(bf16[160,2560]{1,0:T(8,128)(2,1)S(1)} %pad_maximum_fusion.rest_0_), channel_id=1, source_target_pairs={{0,257},{8,265},{16,273},{24,281},{32,289},{40,297},{48,305},{56,3... | collective-permute-start | bytes 2457608 | tf_op jit(solution)/shard_map/ppermute | solution.py:56
  12.6 2.2 %collective-permute-start.4 = (bf16[160,2560]{1,0:T(8,128)(2,1)S(1)}, bf16[160,2560]{1,0:T(8,128)(2,1)}, u32[]{:S(2)}, u32[]{:S(2)}) collective-permute-start(bf16[160,2560]{1,0:T(8,128)(2,1)S(1)} %pad_maximum_fusion.rest_0_), channel_id=1, source_target_pairs={{0,2},{8,10},{16,18},{24,26},{32,34},{40,42},{48,50},{56,58},{64,6... | collective-permute-start | bytes 2457608 | tf_op jit(solution)/shard_map/ppermute | solution.py:56
  14.8 0.0 copy-done.1
  14.8 0.8 slice_bitcast_fusion
  15.6 4.9 %collective-permute-start = (bf16[64,1280]{1,0:T(8,128)(2,1)}, bf16[64,1280]{1,0:T(8,128)(2,1)S(1)}, u32[]{:S(2)}, u32[]{:S(2)}) collective-permute-start(bf16[64,1280]{1,0:T(8,128)(2,1)} %get-tuple-element.26), channel_id=1, source_target_pairs={{0,8},{8,16},{16,24},{24,32},{32,40},{40,48},{48,56},{56,64},{64,7... | collective-permute-start | bytes 491528 | tf_op jit(solution)/shard_map/ppermute | solution.py:61
  20.5 3.5 %collective-permute-start.1 = (bf16[64,1280]{1,0:T(8,128)(2,1)}, bf16[64,1280]{1,0:T(8,128)(2,1)S(1)}, u32[]{:S(2)}, u32[]{:S(2)}) collective-permute-start(bf16[64,1280]{1,0:T(8,128)(2,1)} %get-tuple-element.25), channel_id=1, source_target_pairs={{0,16},{8,24},{16,32},{24,40},{32,48},{40,56},{48,64},{56,72},{64,... | collective-permute-start | bytes 491528 | tf_op jit(solution)/shard_map/ppermute | solution.py:61
  24.1 0.0 copy-done.9
  24.1 0.1 pad_add_fusion
  24.2 0.1 fusion.2
  24.3 0.3 select_reduce_fusion.1
  24.6 0.0 copy-done.8
  24.6 0.3 select_reduce_fusion
  24.9 0.2 fusion
  25.1 0.2 slice_reduce_fusion
  25.5 0.1 copy.13
  25.5 0.0 copy-done.5
  25.6 0.1 select_reduce_fusion.2
  25.7 0.0 collective-permute-done.in0
  25.7 3.6 %collective-permute-start.2 = (bf16[64,1280]{1,0:T(8,128)(2,1)}, bf16[64,1280]{1,0:T(8,128)(2,1)S(1)}, u32[]{:S(2)}, u32[]{:S(2)}) collective-permute-start(bf16[64,1280]{1,0:T(8,128)(2,1)} %get-tuple-element.24), channel_id=1, source_target_pairs={{0,24},{8,32},{16,40},{24,48},{32,56},{40,64},{48,72},{56,80},{64,... | collective-permute-start | bytes 491528 | tf_op jit(solution)/shard_map/ppermute | solution.py:61
  29.3 2.1 %collective-permute-done.1.in1 = bf16[64,1280]{1,0:T(8,128)(2,1)S(1)} collective-permute-done((bf16[64,1280]{1,0:T(8,128)(2,1)}, bf16[64,1280]{1,0:T(8,128)(2,1)S(1)}, u32[]{:S(2)}, u32[]{:S(2)}) %collective-permute-start.1) | collective-permute-done | bytes 163872 | tf_op jit(solution)/shard_map/ppermute | solution.py:61
  31.4 4.0 %collective-permute-start.5 = (bf16[160,2560]{1,0:T(8,128)(2,1)S(1)}, bf16[160,2560]{1,0:T(8,128)(2,1)}, u32[]{:S(2)}, u32[]{:S(2)}) collective-permute-start(bf16[160,2560]{1,0:T(8,128)(2,1)S(1)} %pad_maximum_fusion.rest_0_), channel_id=1, source_target_pairs={{0,6},{8,14},{16,22},{24,30},{32,38},{40,46},{48,54},{56,62},{64,7... | collective-permute-start | bytes 2457608 | tf_op jit(solution)/shard_map/ppermute | solution.py:56
  35.4 0.0 collective-permute-done.6.rest_3_
  35.4 1.9 %collective-permute-start.8 = (bf16[160,2560]{1,0:T(8,128)(2,1)}, bf16[160,2560]{1,0:T(8,128)(2,1)}, u32[]{:S(2)}, u32[]{:S(2)}) collective-permute-start(bf16[160,2560]{1,0:T(8,128)(2,1)} %collective-permute-done.6.rest_3_), channel_id=1, source_target_pairs={{0,2},{8,10},{16,18},{24,26},{32,34},{40,42},{48,50},{56,58},{64,6... | collective-permute-start | bytes 2457608 | tf_op jit(solution)/shard_map/ppermute | solution.py:56
  37.3 1.0 %collective-permute-done.2.in2 = bf16[64,1280]{1,0:T(8,128)(2,1)S(1)} collective-permute-done((bf16[64,1280]{1,0:T(8,128)(2,1)}, bf16[64,1280]{1,0:T(8,128)(2,1)S(1)}, u32[]{:S(2)}, u32[]{:S(2)}) %collective-permute-start.2) | collective-permute-done | bytes 163872 | tf_op jit(solution)/shard_map/ppermute | solution.py:61
  38.3 0.0 copy-start.2
  38.3 0.7 copy-done.2
  39.0 4.3 %collective-permute-start.9 = (bf16[160,2560]{1,0:T(8,128)(2,1)}, bf16[160,2560]{1,0:T(8,128)(2,1)}, u32[]{:S(2)}, u32[]{:S(2)}) collective-permute-start(bf16[160,2560]{1,0:T(8,128)(2,1)} %collective-permute-done.6.rest_3_), channel_id=1, source_target_pairs={{0,6},{8,14},{16,22},{24,30},{32,38},{40,46},{48,54},{56,62},{64,7... | collective-permute-start | bytes 2457608 | tf_op jit(solution)/shard_map/ppermute | solution.py:56
  43.2 0.0 collective-permute-done.7.rest_4_
  43.3 2.7 %collective-permute-start.10 = (bf16[160,2560]{1,0:T(8,128)(2,1)S(1)}, bf16[160,2560]{1,0:T(8,128)(2,1)}, u32[]{:S(2)}, u32[]{:S(2)}) collective-permute-start(bf16[160,2560]{1,0:T(8,128)(2,1)S(1)} %collective-permute-done.7.rest_4_), channel_id=1, source_target_pairs={{0,257},{8,265},{16,273},{24,281},{32,289},{40,297},{48,305},{56,3... | collective-permute-start | bytes 2457608 | tf_op jit(solution)/shard_map/ppermute | solution.py:56
  46.0 0.1 concatenate.9.meta
  46.1 0.0 copy-start.3
  46.1 0.9 %copy-done.3 = bf16[64,1280]{1,0:T(8,128)(2,1)S(1)} copy-done((bf16[64,1280]{1,0:T(8,128)(2,1)S(1)}, bf16[64,1280]{1,0:T(8,128)(2,1)}, u32[]{:S(2)}) %copy-start.3) | copy-done | bytes 163864
  47.0 2.1 %shard_map.91 = (bf16[256,1280]{1,0:T(8,128)(2,1)S(1)}, bf16[256,1280]{1,0:T(8,128)(2,1)S(1)}) custom-call(s32[20]{0:T(128)S(1)} %concatenate.9.meta, bf16[1,1,7,64,1280]{4,3,2,1,0:T(8,128)(2,1)S(1)} %copy-done.1, bf16[64,1280]{1,0:T(8,128)(2,1)S(1)} %collective-permute-done.in0, bf16[64,1280]{1,0:T(8,128)(2,1)S(1)} %collective-permute-done.1.in1, ...), custom_call_target="tpu_custom_call" | custom-call | tf_op jit(solution)/shard_map/pallas_call | solution.py:218
  49.0 0.0 collective-permute-done.4.rest_1_
  49.1 0.0 copy-start.4
  49.1 5.8 %collective-permute-start.3 = (bf16[256,1280]{1,0:T(8,128)(2,1)S(1)}, bf16[256,1280]{1,0:T(8,128)(2,1)S(1)}, u32[]{:S(2)}, u32[]{:S(2)}) collective-permute-start(bf16[256,1280]{1,0:T(8,128)(2,1)S(1)} %get-tuple-element.11.xa), channel_id=1, source_target_pairs={{0,8},{8,0},{16,24},{24,16},{32,40},{40,32},{48,56},{56,48},{64,72... | collective-permute-start | bytes 1966088 | tf_op jit(solution)/shard_map/ppermute | solution.py:56
  54.9 0.0 collective-permute-done.5.rest_2_
  54.9 1.7 %collective-permute-done.3.rest_8_.xb = bf16[256,1280]{1,0:T(8,128)(2,1)S(1)} collective-permute-done((bf16[256,1280]{1,0:T(8,128)(2,1)S(1)}, bf16[256,1280]{1,0:T(8,128)(2,1)S(1)}, u32[]{:S(2)}, u32[]{:S(2)}) %collective-permute-start.3) | collective-permute-done | bytes 655392 | tf_op jit(solution)/shard_map/ppermute | solution.py:56
  56.6 6.0 %collective-permute-done.10.rest_7_ = bf16[160,2560]{1,0:T(8,128)(2,1)} collective-permute-done((bf16[160,2560]{1,0:T(8,128)(2,1)S(1)}, bf16[160,2560]{1,0:T(8,128)(2,1)}, u32[]{:S(2)}, u32[]{:S(2)}) %collective-permute-start.10) | collective-permute-done | bytes 819232 | tf_op jit(solution)/shard_map/ppermute | solution.py:56
  62.6 0.0 collective-permute-done.8.rest_5_
  62.6 6.0 %collective-permute-done.9.rest_6_ = bf16[160,2560]{1,0:T(8,128)(2,1)} collective-permute-done((bf16[160,2560]{1,0:T(8,128)(2,1)}, bf16[160,2560]{1,0:T(8,128)(2,1)}, u32[]{:S(2)}, u32[]{:S(2)}) %collective-permute-start.9) | collective-permute-done | bytes 819232 | tf_op jit(solution)/shard_map/ppermute | solution.py:56
  68.5 3.1 %shard_map.92 = (bf16[1280,1920]{1,0:T(8,128)(2,1)S(1)}, bf16[1280,640]{1,0:T(8,128)(2,1)S(1)}) custom-call(s32[20]{0:T(128)S(1)} %concatenate.9.meta, bf16[160,2560]{1,0:T(8,128)(2,1)S(1)} %pad_maximum_fusion.rest_0_, bf16[160,2560]{1,0:T(8,128)(2,1)} %collective-permute-done.4.rest_1_, bf16[160,2560]{1,0:T(8,128)(2,1)} %collective-permute-done.5.rest_2_, ...), custom_call_target="tpu_custom_call" | custom-call | tf_op jit(solution)/shard_map/pallas_call | solution.py:228
  71.7 5.0 %collective-permute-start.12 = (bf16[1280,640]{1,0:T(8,128)(2,1)S(1)}, bf16[1280,640]{1,0:T(8,128)(2,1)S(1)}, u32[]{:S(2)}, u32[]{:S(2)}) collective-permute-start(bf16[1280,640]{1,0:T(8,128)(2,1)S(1)} %get-tuple-element.15.wa), channel_id=1, source_target_pairs={{0,8},{8,0},{16,24},{24,16},{32,40},{40,32},{48,56},{56,48},{64,72... | collective-permute-start | bytes 4915208 | tf_op jit(solution)/shard_map/ppermute | solution.py:56
  76.7 0.0 copy-done.4
  76.7 0.1 fusion.4
  76.8 0.0 copy-start.6
  76.8 0.0 copy-start.7
  76.8 5.3 %shard_map.93 = (bf16[256,640]{1,0:T(8,128)(2,1)S(1)}, bf16[256,640]{1,0:T(8,128)(2,1)S(1)}) custom-call(s32[20]{0:T(128)S(1)} %concatenate.9.meta, bf16[256,1280]{1,0:T(8,128)(2,1)S(1)} %get-tuple-element.11.xa, bf16[256,1280]{1,0:T(8,128)(2,1)S(1)} %collective-permute-done.3.rest_8_.xb, f32[1,1920]{1,0:T(1,128)S(1)} %reshape.81.bias, ...), custom_call_target="tpu_custom_call" | custom-call | tf_op jit(solution)/shard_map/pallas_call | solution.py:241
  82.1 1.9 %collective-permute-start.11 = (bf16[256,640]{1,0:T(8,128)(2,1)S(1)}, bf16[256,640]{1,0:T(8,128)(2,1)S(1)}, u32[]{:S(2)}, u32[]{:S(2)}) collective-permute-start(bf16[256,640]{1,0:T(8,128)(2,1)S(1)} %get-tuple-element.14), channel_id=1, source_target_pairs={{0,8},{8,0},{16,24},{24,16},{32,40},{40,32},{48,56},{56,48},{64,72... | collective-permute-start | bytes 983048 | tf_op jit(solution)/shard_map/ppermute | solution.py:56
  84.0 0.0 copy-done.6
  84.0 0.0 copy-done.7
  84.1 1.5 %collective-permute-done.11.attb = bf16[256,640]{1,0:T(8,128)(2,1)S(1)} collective-permute-done((bf16[256,640]{1,0:T(8,128)(2,1)S(1)}, bf16[256,640]{1,0:T(8,128)(2,1)S(1)}, u32[]{:S(2)}, u32[]{:S(2)}) %collective-permute-start.11) | collective-permute-done | bytes 327712 | tf_op jit(solution)/shard_map/ppermute | solution.py:56
  85.6 0.0 collective-permute-done.12.wb
  85.6 2.9 %shard_map.94 = bf16[64,5120]{1,0:T(8,128)(2,1)} custom-call(s32[20]{0:T(128)S(1)} %concatenate.9.meta, bf16[256,640]{1,0:T(8,128)(2,1)S(1)} %get-tuple-element.13.atta, bf16[256,640]{1,0:T(8,128)(2,1)S(1)} %collective-permute-done.11.attb, bf16[1280,640]{1,0:T(8,128)(2,1)S(1)} %get-tuple-element.15.wa, bf16[1280,640]{1,0:T(8,128)(2,1)S(1)} %collective-permute-done.12.wb, ...), custom_call_target="tpu_custom_call" | custom-call | tf_op jit(solution)/shard_map/pallas_call | solution.py:251
  (11 shorter events, 0.1 us)
Async XLA Ops:
  0.0 1.0 %copy-start = (bf16[1280,160]{0,1:T(8,128)(2,1)S(1)}, bf16[1280,160]{0,1:T(8,128)(2,1)}, u32[]{:S(2)}) copy-start(bf16[1280,160]{0,1:T(8,128)(2,1)} %param.13) | copy-start | bytes 1228804
  1.0 13.8 %copy-start.1 = (bf16[1,1,7,64,1280]{4,3,2,1,0:T(8,128)(2,1)S(1)}, bf16[1,1,7,64,1280]{4,3,2,1,0:T(8,128)(2,1)}, u32[]{:S(2)}) copy-start(bf16[1,1,7,64,1280]{4,3,2,1,0:T(8,128)(2,1)} %own.1) | copy-start | bytes 3440644
  1.0 23.1 %copy-start.9 = (s32[64,1,7]{0,1,2:T(1,128)S(1)}, s32[64,1,7]{0,1,2:T(1,128)}, u32[]{:S(2)}) copy-start(s32[64,1,7]{0,1,2:T(1,128)} %param.16) | copy-start | bytes 5380
  2.3 22.3 %copy-start.8 = (s32[64,1,7,2]{0,3,2,1:T(2,128)S(1)}, s32[64,1,7,2]{0,3,2,1:T(2,128)}, u32[]{:S(2)}) copy-start(s32[64,1,7,2]{0,3,2,1:T(2,128)} %param.17) | copy-start | bytes 10756
  2.3 23.2 %copy-start.5 = (f32[1280]{0:T(1024)S(1)}, f32[1280]{0:T(1024)}, u32[]{:S(2)}) copy-start(f32[1280]{0:T(1024)} %param.10) | copy-start | bytes 15364
  2.4 40.8 %collective-permute-start.7 = (bf16[160,2560]{1,0:T(8,128)(2,1)S(1)}, bf16[160,2560]{1,0:T(8,128)(2,1)S(1)}, u32[]{:S(2)}, u32[]{:S(2)}) collective-permute-start(bf16[160,2560]{1,0:T(8,128)(2,1)S(1)} %pad_maximum_fusion.rest_0_), channel_id=1, source_target_pairs={{0,4},{8,12},{16,20},{24,28},{32,36},{40,44},{48,52},{56,60},{64,6... | collective-permute-start | bytes 2457608 | tf_op jit(solution)/shard_map/ppermute | solution.py:56
  7.9 27.5 %collective-permute-start.6 = (bf16[160,2560]{1,0:T(8,128)(2,1)S(1)}, bf16[160,2560]{1,0:T(8,128)(2,1)}, u32[]{:S(2)}, u32[]{:S(2)}) collective-permute-start(bf16[160,2560]{1,0:T(8,128)(2,1)S(1)} %pad_maximum_fusion.rest_0_), channel_id=1, source_target_pairs={{0,257},{8,265},{16,273},{24,281},{32,289},{40,297},{48,305},{56,3... | collective-permute-start | bytes 2457608 | tf_op jit(solution)/shard_map/ppermute | solution.py:56
  12.6 36.5 %collective-permute-start.4 = (bf16[160,2560]{1,0:T(8,128)(2,1)S(1)}, bf16[160,2560]{1,0:T(8,128)(2,1)}, u32[]{:S(2)}, u32[]{:S(2)}) collective-permute-start(bf16[160,2560]{1,0:T(8,128)(2,1)S(1)} %pad_maximum_fusion.rest_0_), channel_id=1, source_target_pairs={{0,2},{8,10},{16,18},{24,26},{32,34},{40,42},{48,50},{56,58},{64,6... | collective-permute-start | bytes 2457608 | tf_op jit(solution)/shard_map/ppermute | solution.py:56
  15.6 10.1 %collective-permute-start = (bf16[64,1280]{1,0:T(8,128)(2,1)}, bf16[64,1280]{1,0:T(8,128)(2,1)S(1)}, u32[]{:S(2)}, u32[]{:S(2)}) collective-permute-start(bf16[64,1280]{1,0:T(8,128)(2,1)} %get-tuple-element.26), channel_id=1, source_target_pairs={{0,8},{8,16},{16,24},{24,32},{32,40},{40,48},{48,56},{56,64},{64,7... | collective-permute-start | bytes 491528 | tf_op jit(solution)/shard_map/ppermute | solution.py:61
  20.5 10.9 %collective-permute-start.1 = (bf16[64,1280]{1,0:T(8,128)(2,1)}, bf16[64,1280]{1,0:T(8,128)(2,1)S(1)}, u32[]{:S(2)}, u32[]{:S(2)}) collective-permute-start(bf16[64,1280]{1,0:T(8,128)(2,1)} %get-tuple-element.25), channel_id=1, source_target_pairs={{0,16},{8,24},{16,32},{24,40},{32,48},{40,56},{48,64},{56,72},{64,... | collective-permute-start | bytes 491528 | tf_op jit(solution)/shard_map/ppermute | solution.py:61
  25.7 12.6 %collective-permute-start.2 = (bf16[64,1280]{1,0:T(8,128)(2,1)}, bf16[64,1280]{1,0:T(8,128)(2,1)S(1)}, u32[]{:S(2)}, u32[]{:S(2)}) collective-permute-start(bf16[64,1280]{1,0:T(8,128)(2,1)} %get-tuple-element.24), channel_id=1, source_target_pairs={{0,24},{8,32},{16,40},{24,48},{32,56},{40,64},{48,72},{56,80},{64,... | collective-permute-start | bytes 491528 | tf_op jit(solution)/shard_map/ppermute | solution.py:61
  31.4 23.5 %collective-permute-start.5 = (bf16[160,2560]{1,0:T(8,128)(2,1)S(1)}, bf16[160,2560]{1,0:T(8,128)(2,1)}, u32[]{:S(2)}, u32[]{:S(2)}) collective-permute-start(bf16[160,2560]{1,0:T(8,128)(2,1)S(1)} %pad_maximum_fusion.rest_0_), channel_id=1, source_target_pairs={{0,6},{8,14},{16,22},{24,30},{32,38},{40,46},{48,54},{56,62},{64,7... | collective-permute-start | bytes 2457608 | tf_op jit(solution)/shard_map/ppermute | solution.py:56
  35.4 27.2 %collective-permute-start.8 = (bf16[160,2560]{1,0:T(8,128)(2,1)}, bf16[160,2560]{1,0:T(8,128)(2,1)}, u32[]{:S(2)}, u32[]{:S(2)}) collective-permute-start(bf16[160,2560]{1,0:T(8,128)(2,1)} %collective-permute-done.6.rest_3_), channel_id=1, source_target_pairs={{0,2},{8,10},{16,18},{24,26},{32,34},{40,42},{48,50},{56,58},{64,6... | collective-permute-start | bytes 2457608 | tf_op jit(solution)/shard_map/ppermute | solution.py:56
  38.3 0.7 copy-start.2
  39.0 29.6 %collective-permute-start.9 = (bf16[160,2560]{1,0:T(8,128)(2,1)}, bf16[160,2560]{1,0:T(8,128)(2,1)}, u32[]{:S(2)}, u32[]{:S(2)}) collective-permute-start(bf16[160,2560]{1,0:T(8,128)(2,1)} %collective-permute-done.6.rest_3_), channel_id=1, source_target_pairs={{0,6},{8,14},{16,22},{24,30},{32,38},{40,46},{48,54},{56,62},{64,7... | collective-permute-start | bytes 2457608 | tf_op jit(solution)/shard_map/ppermute | solution.py:56
  43.3 19.3 %collective-permute-start.10 = (bf16[160,2560]{1,0:T(8,128)(2,1)S(1)}, bf16[160,2560]{1,0:T(8,128)(2,1)}, u32[]{:S(2)}, u32[]{:S(2)}) collective-permute-start(bf16[160,2560]{1,0:T(8,128)(2,1)S(1)} %collective-permute-done.7.rest_4_), channel_id=1, source_target_pairs={{0,257},{8,265},{16,273},{24,281},{32,289},{40,297},{48,305},{56,3... | collective-permute-start | bytes 2457608 | tf_op jit(solution)/shard_map/ppermute | solution.py:56
  46.1 0.9 %copy-start.3 = (bf16[64,1280]{1,0:T(8,128)(2,1)S(1)}, bf16[64,1280]{1,0:T(8,128)(2,1)}, u32[]{:S(2)}) copy-start(bf16[64,1280]{1,0:T(8,128)(2,1)} %copy-done.2) | copy-start | bytes 491524
  49.1 27.6 %copy-start.4 = (f32[3840]{0:T(1024)S(1)}, f32[3840]{0:T(1024)}, u32[]{:S(2)}) copy-start(f32[3840]{0:T(1024)} %param.12) | copy-start | bytes 46084
  49.1 7.5 %collective-permute-start.3 = (bf16[256,1280]{1,0:T(8,128)(2,1)S(1)}, bf16[256,1280]{1,0:T(8,128)(2,1)S(1)}, u32[]{:S(2)}, u32[]{:S(2)}) collective-permute-start(bf16[256,1280]{1,0:T(8,128)(2,1)S(1)} %get-tuple-element.11.xa), channel_id=1, source_target_pairs={{0,8},{8,0},{16,24},{24,16},{32,40},{40,32},{48,56},{56,48},{64,72... | collective-permute-start | bytes 1966088 | tf_op jit(solution)/shard_map/ppermute | solution.py:56
  71.7 13.9 %collective-permute-start.12 = (bf16[1280,640]{1,0:T(8,128)(2,1)S(1)}, bf16[1280,640]{1,0:T(8,128)(2,1)S(1)}, u32[]{:S(2)}, u32[]{:S(2)}) collective-permute-start(bf16[1280,640]{1,0:T(8,128)(2,1)S(1)} %get-tuple-element.15.wa), channel_id=1, source_target_pairs={{0,8},{8,0},{16,24},{24,16},{32,40},{40,32},{48,56},{56,48},{64,72... | collective-permute-start | bytes 4915208 | tf_op jit(solution)/shard_map/ppermute | solution.py:56
  76.8 7.2 %copy-start.6 = (f32[1280]{0:T(1024)S(1)}, f32[1280]{0:T(1024)}, u32[]{:S(2)}) copy-start(f32[1280]{0:T(1024)} %param.14) | copy-start | bytes 15364
  76.8 7.2 %copy-start.7 = (f32[1280]{0:T(1024)S(1)}, f32[1280]{0:T(1024)}, u32[]{:S(2)}) copy-start(f32[1280]{0:T(1024)} %param.15) | copy-start | bytes 15364
  82.1 3.5 %collective-permute-start.11 = (bf16[256,640]{1,0:T(8,128)(2,1)S(1)}, bf16[256,640]{1,0:T(8,128)(2,1)S(1)}, u32[]{:S(2)}, u32[]{:S(2)}) collective-permute-start(bf16[256,640]{1,0:T(8,128)(2,1)S(1)} %get-tuple-element.14), channel_id=1, source_target_pairs={{0,8},{8,0},{16,24},{24,16},{32,40},{40,32},{48,56},{56,48},{64,72... | collective-permute-start | bytes 983048 | tf_op jit(solution)/shard_map/ppermute | solution.py:56

commit v3 on v2

--- a/solution.py
+++ b/solution.py
@@ -15,6 +15,7 @@
 HEAD = D // HEADS
 SHARDS = 8
 DEPTH = D // SHARDS
+PART = DEPTH // 2
 ROWS = RECV * WIN
 NX, NYH, NYL, NZ, NC = 4, 2, 2, 16, 2
 AXES = ("dp", "fsdp")
@@ -44,6 +45,10 @@
     return perm(lambda x, yh, yl, z, c: (x + d, yh, yl, z, c))
 
 
+def by_z(d):
+    return perm(lambda x, yh, yl, z, c: (x, yh, yl, z + d, c))
+
+
 def across_y():
     return perm(lambda x, yh, yl, z, c: (x, 1 - yh, 1 - yl, z, c))
 
@@ -80,28 +85,67 @@
         normed[rows, :] = (x * lax.rsqrt(ms + EPS) * gain[...]).astype(jnp.bfloat16)
 
 
-def gather_kernel(meta, *rest):
-    pieces, (_, w, wo, sems) = rest[:SHARDS], rest[SHARDS:]
-    copies = []
-    for i in range(SHARDS):
-        at = pl.ds(pl.multiple_of(meta[12 + i] * DEPTH, DEPTH), DEPTH)
+def spot(odd_half):
+    rank = lax.axis_index("dp")
+    half = pl.multiple_of(lax.rem(rank, NC) * HALF, 128)
+    odd = lax.rem(lax.div(rank, NC), 2)
+    return half, pl.multiple_of((1 - odd if odd_half else odd) * PART, PART)
+
+
+def build_kernel(w, wo, *rest):
+    out, sems = rest[-2:]
+    half, row = spot(False)
+    rows = pl.ds(0 if out.shape[0] == DEPTH else row, out.shape[0])
+    copies = [
+        pltpu.make_async_copy(
+            w.at[rows, pl.ds(pl.multiple_of(half + j * D, 128), HALF)],
+            out.at[:, pl.ds(j * HALF, HALF)],
+            sems.at[j],
+        )
+        for j in range(3)
+    ]
+    copies.append(
+        pltpu.make_async_copy(
+            wo.at[rows, pl.ds(half, HALF)], out.at[:, pl.ds(3 * HALF, HALF)], sems.at[3]
+        )
+    )
+    for copy in copies:
+        copy.start()
+    for copy in copies:
+        copy.wait()
+
+
+WHOLE = (0, 3, 4, 5, 6, 7)
+HALVES = (1, 2)
+PIECES = SHARDS + 2
+
+
+def attend_kernel(meta, xa, xb, bias, *rest):
+    mine, theirs, x, w, wo, q, k, v, att, x_sems, sems = rest[PIECES:]
+    copies = [
+        pltpu.make_async_copy(src, x.at[pl.ds(i * ROWS, ROWS), :], x_sems.at[i])
+        for i, src in enumerate((xa, xb))
+    ]
+    for i, shard in enumerate((*WHOLE, *HALVES, *HALVES)):
+        at = meta[12 + shard] * DEPTH
+        if i >= len(WHOLE):
+            at = at + spot(i >= SHARDS)[1]
+        at = pl.ds(pl.multiple_of(at, PART), rest[i].shape[0])
         for j, dst in enumerate((w, wo)):
             cols = pl.ds(j * 3 * HALF, (3 - 2 * j) * HALF)
             copies.append(
-                pltpu.make_async_copy(pieces[i].at[:, cols], dst.at[at, :], sems.at[i, j])
+                pltpu.make_async_copy(rest[i].at[:, cols], dst.at[at, :], sems.at[i, j])
             )
     for copy in copies:
         copy.start()
     for copy in copies:
         copy.wait()
-
-
-def attend_kernel(meta, xa, xb, bias, w, outa, outb, q, k, v):
     for j, dst in enumerate((q, k, v)):
         cols = pl.ds(j * HALF, HALF)
-        for i, src in enumerate((xa, xb)):
-            dst[pl.ds(i * ROWS, ROWS), :] = (
-                jnp.dot(src[...], w[:, cols], preferred_element_type=jnp.float32) + bias[:, cols]
+        for i in range(2):
+            rows = pl.ds(i * ROWS, ROWS)
+            dst[rows, :] = (
+                jnp.dot(x[rows, :], w[:, cols], preferred_element_type=jnp.float32) + bias[:, cols]
             ).astype(jnp.bfloat16)
     pair = 2 * HEAD
     lane = lax.broadcasted_iota(jnp.int32, (1, 256), 1)
@@ -109,7 +153,6 @@
     for wnd in range(2 * RECV):
         rows = pl.ds(wnd * WIN, WIN)
         live = key_at < MERGE * meta[4 + wnd]
-        out = outa if wnd < RECV else outb
         tiles = [None] * (HALF // 128)
         for i in range(HALF // pair):
             lo = i * pair // 128 * 128
@@ -135,15 +178,16 @@
                 part = o[:, n * 128 : (n + 1) * 128]
                 tile = lo // 128 + n
                 tiles[tile] = part if tiles[tile] is None else tiles[tile] + part
-        at = pl.ds(wnd % RECV * WIN, WIN)
         for n, tile in enumerate(tiles):
-            out[at, pl.ds(n * 128, 128)] = tile.astype(jnp.bfloat16)
-
-
-def merge_kernel(meta, atta, attb, wa, wb, placed, bias, gain, out, y):
-    update = lax.dot_general(atta[...], wa[...], NT, preferred_element_type=jnp.float32)
-    update += lax.dot_general(attb[...], wb[...], NT, preferred_element_type=jnp.float32)
-    r = placed[...].astype(jnp.float32) + update + bias[...]
+            att[rows, pl.ds(n * 128, 128)] = tile.astype(jnp.bfloat16)
+    for i, out in enumerate((mine, theirs)):
+        out[...] = lax.dot_general(
+            att[pl.ds(i * ROWS, ROWS), :], wo[...], NT, preferred_element_type=jnp.float32
+        )
+
+
+def merge_kernel(meta, mine, other, placed, bias, gain, out, y):
+    r = placed[...].astype(jnp.float32) + (mine[...] + other[...]) + bias[...]
     ms = jnp.mean(r * r, axis=-1, keepdims=True)
     normed = r * lax.rsqrt(ms + EPS) * gain[...]
     for n in range(D // 128):
@@ -160,14 +204,27 @@
             out[:, pl.ds(i * D + n * 128, 128)] = jnp.where(live, part, 0.0).astype(jnp.bfloat16)
 
 
+def build(rows, w, wo, *earlier):
+    return pl.pallas_call(
+        build_kernel,
+        out_shape=jax.ShapeDtypeStruct((rows, 4 * HALF), jnp.bfloat16),
+        in_specs=[ANY] * (2 + len(earlier)),
+        out_specs=ANY,
+        scratch_shapes=[pltpu.SemaphoreType.DMA((4,))],
+        compiler_params=SMALL if earlier else LARGE,
+    )(w, wo, *earlier)
+
+
 def vmem(n):
     return [pl.BlockSpec(memory_space=pltpu.VMEM)] * n
 
 
 ANY = pl.BlockSpec(memory_space=pl.ANY)
+SMEM = pl.BlockSpec(memory_space=pltpu.SMEM)
 SMALL = pltpu.CompilerParams(vmem_limit_bytes=4 * 1024 * 1024)
-SMEM = pl.BlockSpec(memory_space=pltpu.SMEM)
-PARAMS = pltpu.CompilerParams(vmem_limit_bytes=20 * 1024 * 1024)
+MIDDLE = pltpu.CompilerParams(vmem_limit_bytes=52 * 1024 * 1024)
+LARGE = pltpu.CompilerParams(vmem_limit_bytes=60 * 1024 * 1024)
+PARAMS = pltpu.CompilerParams(vmem_limit_bytes=24 * 1024 * 1024)
 
 
 def tables(route, groups, rank, x, yh):
@@ -195,23 +252,22 @@
     core = rank % NC
     half = core * HALF
 
-    piece = jnp.concatenate(
-        [lax.dynamic_slice_in_dim(w_qkv, j * D + half, HALF, 1) for j in range(3)]
-        + [lax.dynamic_slice_in_dim(jnp.transpose(w_proj), half, HALF, 1)],
-        axis=1,
-    )
+    w_out = jnp.transpose(w_proj)
+    piece = build(DEPTH, w_qkv, w_out)
     bias = jnp.concatenate(
         [lax.dynamic_slice_in_dim(b_qkv, j * D + half, HALF, 0) for j in range(3)]
     )
     far = send(piece, by_x(2))
     cross = send(piece, across_y())
-    plus = send(piece, by_x(1))
-    minus = send(piece, by_x(-1))
+    moved = [by_rank(patches[0, 0, RECV + m], m + 1) for m in range(SLOTS - RECV)]
+    part = build(PART, w_qkv, w_out, moved[0])
+    plus = send(part, by_x(1))
+    minus = send(part, by_x(-1))
     cross_plus = send(cross, by_x(1))
     cross_minus = send(cross, by_x(-1))
     cross_far = send(far, across_y())
-
-    moved = [by_rank(patches[0, 0, RECV + m], m + 1) for m in range(SLOTS - RECV)]
+    plus_rest = send(plus, by_z(1))
+    minus_rest = send(minus, by_z(-1))
 
     meta = tables(route, groups, rank, lane // NYH, lane % NYH)
 
@@ -225,38 +281,35 @@
     )(meta, patches, *moved, norm_gain.reshape(1, D))
     normed_other = send(normed, other_core())
 
-    w, w_mine = pl.pallas_call(
-        gather_kernel,
-        out_shape=[
-            jax.ShapeDtypeStruct((D, 3 * HALF), jnp.bfloat16),
-            jax.ShapeDtypeStruct((D, HALF), jnp.bfloat16),
-        ],
-        in_specs=[SMEM] + [ANY] * (SHARDS + 1),
+    mine, theirs = pl.pallas_call(
+        attend_kernel,
+        out_shape=[jax.ShapeDtypeStruct((ROWS, D), jnp.float32)] * 2,
+        in_specs=[SMEM] + [ANY] * 2 + vmem(1) + [ANY] * PIECES,
         out_specs=vmem(2),
-        scratch_shapes=[pltpu.SemaphoreType.DMA((SHARDS, 2))],
-        compiler_params=PARAMS,
-    )(meta, piece, plus, minus, cross, far, cross_plus, cross_minus, cross_far, normed_other)
-    w_other = send(w_mine, other_core())
-
-    att, att_theirs = pl.pallas_call(
-        attend_kernel,
-        out_shape=[jax.ShapeDtypeStruct((ROWS, HALF), jnp.bfloat16)] * 2,
-        in_specs=[SMEM] + vmem(4),
-        out_specs=vmem(2),
-        scratch_shapes=[pltpu.VMEM((2 * ROWS, HALF), jnp.bfloat16)] * 3,
-        compiler_params=PARAMS,
-    )(meta, normed, normed_other, bias.reshape(1, 3 * HALF), w)
-    att_other = send(att_theirs, other_core())
+        scratch_shapes=[
+            pltpu.VMEM((2 * ROWS, D), jnp.bfloat16),
+            pltpu.VMEM((D, 3 * HALF), jnp.bfloat16),
+            pltpu.VMEM((D, HALF), jnp.bfloat16),
+        ]
+        + [pltpu.VMEM((2 * ROWS, HALF), jnp.bfloat16)] * 4
+        + [pltpu.SemaphoreType.DMA((2,)), pltpu.SemaphoreType.DMA((PIECES, 2))],
+        compiler_params=MIDDLE,
+    )(
+        meta, normed, normed_other, bias.reshape(1, 3 * HALF),
+        piece, cross, far, cross_plus, cross_minus, cross_far,
+        plus, minus, plus_rest, minus_rest,
+    )
+    other = send(theirs, other_core())
 
     merged = pl.pallas_call(
         merge_kernel,
         out_shape=jax.ShapeDtypeStruct((ROWS // MERGE, MERGE * D), jnp.bfloat16),
-        in_specs=[SMEM] + vmem(7),
+        in_specs=[SMEM] + vmem(5),
         out_specs=vmem(1)[0],
         scratch_shapes=[pltpu.VMEM((D // 128, ROWS, 128), jnp.float32)],
         compiler_params=PARAMS,
     )(
-        meta, att, att_other, w_mine, w_other, placed,
+        meta, mine, other, placed,
         b_proj.reshape(1, D), merge_gain.reshape(1, D),
     )
     return merged.reshape(1, 1, RECV, WIN // MERGE, MERGE * D)

time: 89.4 us -> 118 us (1.32)
  Pallas kernels: 13.4 us -> 40.8 us
  waiting for transfers between devices: 18.3 us -> 22.2 us
  local copies, waits for them, and re-layouts: 5.25 us -> 3.53 us
    pallas_call x2 -> x3, Pallas kernels: 8.39 us -> 36.4 us  [the longest x2 26.1 us: build(): pl.pallas_call(build_kernel, out_shape=jax.ShapeDtypeStruct((rows, 4 * HA...]
    ppermute x3, waiting for transfers between devices: 3.12 us -> 6.59 us  [by_rank(): lax.ppermute(value, 'dp', [(i, (i + by) % devices) for i in range(devices)])]
    dynamic_slice x2 -> x0, local copies, waits for them, and re-layouts: 1.3 us -> none  [the longest x1 1.28 us: on_device(): lax.dynamic_slice_in_dim(w_qkv, j * D + half, HALF, 1)]
    unnamed x21 -> x27, local copies, waits for them, and re-layouts: 2.62 us -> 2.24 us
    ppermute x10 -> x11, waiting for transfers between devices: 15.2 us -> 15.6 us  [send(): return lax.ppermute(value, AXES, pairs)]
    ppermute x10 -> x11, starting transfers between devices: 37.9 us -> 37.9 us  [send(): return lax.ppermute(value, AXES, pairs)]
  transfers between devices with their start and end apart: 13 -> 14, of which waited for: 6 -> 8; matrix products, arithmetic and copies ran while one was open for 3% -> 2% of each run, Pallas kernels for 8% -> 2%
where the time goes in v3:
time: 118 us
  starting transfers between devices  49.7 us (42%)
  Pallas kernels  40.8 us (35%)
  waiting for transfers between devices  22.2 us (19%)
  local copies, waits for them, and re-layouts  3.53 us (3%)
    ppermute x11, starting transfers between devices, send(): return lax.ppermute(value, AXES, pairs)  37.9 us
    pallas_call x2, Pallas kernels, build(): pl.pallas_call(build_kernel, out_shape=jax.ShapeDtypeStruct((rows, 4 * HA...  26.1 us
    ppermute x11, waiting for transfers between devices, send(): return lax.ppermute(value, AXES, pairs)  15.6 us
    ppermute x3, starting transfers between devices, by_rank(): lax.ppermute(value, 'dp', [(i, (i + by) % devices) for i in range(devices)])  11.8 us
    pallas_call x1, Pallas kernels, on_device(): pl.pallas_call(attend_kernel, out_shape=[jax.ShapeDtypeStruct((ROWS, D),...  10.4 us
    ppermute x3, waiting for transfers between devices, by_rank(): lax.ppermute(value, 'dp', [(i, (i + by) % devices) for i in range(devices)])  6.59 us
  transfers between devices with their start and end apart: 14, of which 8 were waited for; matrix products, arithmetic and copies ran while one was open for 2% of the time, Pallas kernels for 2%

profile of v3, /device:TPU:1, one launch (start us, length us, event | category | flops | bytes accessed | tf_op | source)
XLA Modules:
  0.0 117.8 jit_solution(17451404337347387462)
XLA Ops:
  0.0 0.0 copy-start.8
  0.0 0.0 copy-start
  0.0 0.0 copy-start.2
  0.0 26.0 %shard_map.92.rest_0_ = bf16[160,2560]{1,0:T(8,128)(2,1)} custom-call(bf16[160,3840]{1,0:T(8,128)(2,1)} %w.3, bf16[160,1280]{1,0:T(8,128)(2,1)} %bitcast.32), custom_call_target="tpu_custom_call" | custom-call | tf_op jit(solution)/shard_map/pallas_call | solution.py:208
  26.0 5.5 %collective-permute-start.4 = (bf16[160,2560]{1,0:T(8,128)(2,1)}, bf16[160,2560]{1,0:T(8,128)(2,1)}, u32[]{:S(2)}, u32[]{:S(2)}) collective-permute-start(bf16[160,2560]{1,0:T(8,128)(2,1)} %shard_map.92.rest_0_), channel_id=1, source_target_pairs={{0,257},{8,265},{16,273},{24,281},{32,289},{40,297},{48,305},{56,3... | collective-permute-start | bytes 2457608 | tf_op jit(solution)/shard_map/ppermute | solution.py:61
  31.5 4.7 %collective-permute-start.5 = (bf16[160,2560]{1,0:T(8,128)(2,1)}, bf16[160,2560]{1,0:T(8,128)(2,1)}, u32[]{:S(2)}, u32[]{:S(2)}) collective-permute-start(bf16[160,2560]{1,0:T(8,128)(2,1)} %shard_map.92.rest_0_), channel_id=1, source_target_pairs={{0,4},{8,12},{16,20},{24,28},{32,36},{40,44},{48,52},{56,60},{64,6... | collective-permute-start | bytes 2457608 | tf_op jit(solution)/shard_map/ppermute | solution.py:61
  36.2 0.0 copy-done.1
  36.2 0.8 slice_bitcast_fusion
  36.9 4.7 %collective-permute-start = (bf16[64,1280]{1,0:T(8,128)(2,1)S(1)}, bf16[64,1280]{1,0:T(8,128)(2,1)S(1)}, u32[]{:S(2)}, u32[]{:S(2)}) collective-permute-start(bf16[64,1280]{1,0:T(8,128)(2,1)S(1)} %get-tuple-element.19), channel_id=1, source_target_pairs={{0,8},{8,16},{16,24},{24,32},{32,40},{40,48},{48,56},{56,64},{64,7... | collective-permute-start | bytes 491528 | tf_op jit(solution)/shard_map/ppermute | solution.py:66
  41.6 3.5 %collective-permute-start.1 = (bf16[64,1280]{1,0:T(8,128)(2,1)}, bf16[64,1280]{1,0:T(8,128)(2,1)S(1)}, u32[]{:S(2)}, u32[]{:S(2)}) collective-permute-start(bf16[64,1280]{1,0:T(8,128)(2,1)} %get-tuple-element.18), channel_id=1, source_target_pairs={{0,16},{8,24},{16,32},{24,40},{32,48},{40,56},{48,64},{56,72},{64,... | collective-permute-start | bytes 491528 | tf_op jit(solution)/shard_map/ppermute | solution.py:66
  45.1 3.6 %collective-permute-start.2 = (bf16[64,1280]{1,0:T(8,128)(2,1)}, bf16[64,1280]{1,0:T(8,128)(2,1)}, u32[]{:S(2)}, u32[]{:S(2)}) collective-permute-start(bf16[64,1280]{1,0:T(8,128)(2,1)} %get-tuple-element.17), channel_id=1, source_target_pairs={{0,24},{8,32},{16,40},{24,48},{32,56},{40,64},{48,72},{56,80},{64,... | collective-permute-start | bytes 491528 | tf_op jit(solution)/shard_map/ppermute | solution.py:66
  48.7 0.0 copy-done.12
  48.8 0.1 pad_add_fusion
  48.8 0.1 fusion.2
  48.9 0.3 select_reduce_fusion.1
  49.2 0.0 copy-done.11
  49.2 0.3 select_reduce_fusion
  49.5 0.2 fusion
  49.7 0.2 slice_reduce_fusion
  50.1 0.1 copy.13
  50.2 0.0 copy-done.8
  50.2 0.1 select_reduce_fusion.2
  50.3 0.0 collective-permute-done.in0.rest_0_
  50.3 0.0 copy-done
  50.4 0.0 copy-done.2
  50.4 0.1 shard_map.93
  50.5 0.0 copy-start.7
  50.5 2.2 %collective-permute-start.9 = (bf16[80,2560]{1,0:T(8,128)(2,1)S(1)}, bf16[80,2560]{1,0:T(8,128)(2,1)S(1)}, u32[]{:S(2)}, u32[]{:S(2)}) collective-permute-start(bf16[80,2560]{1,0:T(8,128)(2,1)S(1)} %shard_map.93), channel_id=1, source_target_pairs={{0,2},{8,10},{16,18},{24,26},{32,34},{40,42},{48,50},{56,58},{64,6... | collective-permute-start | bytes 1228808 | tf_op jit(solution)/shard_map/ppermute | solution.py:61
  52.7 0.1 concatenate.6.meta
  52.8 0.3 collective-permute-done.1.in1
  53.1 6.3 %collective-permute-done.2.in2 = bf16[64,1280]{1,0:T(8,128)(2,1)} collective-permute-done((bf16[64,1280]{1,0:T(8,128)(2,1)}, bf16[64,1280]{1,0:T(8,128)(2,1)}, u32[]{:S(2)}, u32[]{:S(2)}) %collective-permute-start.2) | collective-permute-done | bytes 163872 | tf_op jit(solution)/shard_map/ppermute | solution.py:66
  59.4 2.3 %shard_map.91 = (bf16[256,1280]{1,0:T(8,128)(2,1)S(1)}, bf16[256,1280]{1,0:T(8,128)(2,1)S(1)}) custom-call(s32[20]{0:T(128)S(1)} %concatenate.6.meta, bf16[1,1,7,64,1280]{4,3,2,1,0:T(8,128)(2,1)S(1)} %copy-done.1, bf16[64,1280]{1,0:T(8,128)(2,1)S(1)} %collective-permute-done.in0.rest_0_, bf16[64,1280]{1,0:T(8,128)(2,1)S(1)} %collective-permute-done.1.in1, ...), custom_call_target="tpu_custom_call" | custom-call | tf_op jit(solution)/shard_map/pallas_call | solution.py:274
  61.8 0.0 copy-start.5
  61.8 0.9 copy-done.5
  62.7 3.6 %collective-permute-start.3 = (bf16[256,1280]{1,0:T(8,128)(2,1)S(1)}, bf16[256,1280]{1,0:T(8,128)(2,1)}, u32[]{:S(2)}, u32[]{:S(2)}) collective-permute-start(bf16[256,1280]{1,0:T(8,128)(2,1)S(1)} %get-tuple-element.9.xa), channel_id=1, source_target_pairs={{0,8},{8,0},{16,24},{24,16},{32,40},{40,32},{48,56},{56,48},{64,72... | collective-permute-start | bytes 1966088 | tf_op jit(solution)/shard_map/ppermute | solution.py:61
  66.3 2.5 %collective-permute-start.10 = (bf16[80,2560]{1,0:T(8,128)(2,1)S(1)}, bf16[80,2560]{1,0:T(8,128)(2,1)S(1)}, u32[]{:S(2)}, u32[]{:S(2)}) collective-permute-start(bf16[80,2560]{1,0:T(8,128)(2,1)S(1)} %shard_map.93), channel_id=1, source_target_pairs={{0,6},{8,14},{16,22},{24,30},{32,38},{40,46},{48,54},{56,62},{64,7... | collective-permute-start | bytes 1228808 | tf_op jit(solution)/shard_map/ppermute | solution.py:61
  68.7 0.0 collective-permute-done.4.rest_1_
  68.7 2.8 %collective-permute-start.6 = (bf16[160,2560]{1,0:T(8,128)(2,1)}, bf16[160,2560]{1,0:T(8,128)(2,1)}, u32[]{:S(2)}, u32[]{:S(2)}) collective-permute-start(bf16[160,2560]{1,0:T(8,128)(2,1)} %collective-permute-done.4.rest_1_), channel_id=1, source_target_pairs={{0,2},{8,10},{16,18},{24,26},{32,34},{40,42},{48,50},{56,58},{64,6... | collective-permute-start | bytes 2457608 | tf_op jit(solution)/shard_map/ppermute | solution.py:61
  71.6 0.0 collective-permute-done.9.rest_6_
  71.6 3.7 %collective-permute-start.7 = (bf16[160,2560]{1,0:T(8,128)(2,1)}, bf16[160,2560]{1,0:T(8,128)(2,1)}, u32[]{:S(2)}, u32[]{:S(2)}) collective-permute-start(bf16[160,2560]{1,0:T(8,128)(2,1)} %collective-permute-done.4.rest_1_), channel_id=1, source_target_pairs={{0,6},{8,14},{16,22},{24,30},{32,38},{40,46},{48,54},{56,62},{64,7... | collective-permute-start | bytes 2457608 | tf_op jit(solution)/shard_map/ppermute | solution.py:61
  75.3 0.0 collective-permute-done.5.rest_2_
  75.3 2.7 %collective-permute-start.8 = (bf16[160,2560]{1,0:T(8,128)(2,1)}, bf16[160,2560]{1,0:T(8,128)(2,1)}, u32[]{:S(2)}, u32[]{:S(2)}) collective-permute-start(bf16[160,2560]{1,0:T(8,128)(2,1)} %collective-permute-done.5.rest_2_), channel_id=1, source_target_pairs={{0,257},{8,265},{16,273},{24,281},{32,289},{40,297},{48,305},{56,3... | collective-permute-start | bytes 2457608 | tf_op jit(solution)/shard_map/ppermute | solution.py:61
  78.0 1.4 %collective-permute-done.10.rest_7_ = bf16[80,2560]{1,0:T(8,128)(2,1)S(1)} collective-permute-done((bf16[80,2560]{1,0:T(8,128)(2,1)S(1)}, bf16[80,2560]{1,0:T(8,128)(2,1)S(1)}, u32[]{:S(2)}, u32[]{:S(2)}) %collective-permute-start.10) | collective-permute-done | bytes 409632 | tf_op jit(solution)/shard_map/ppermute | solution.py:61
  79.3 1.9 %collective-permute-start.11 = (bf16[80,2560]{1,0:T(8,128)(2,1)S(1)}, bf16[80,2560]{1,0:T(8,128)(2,1)S(1)}, u32[]{:S(2)}, u32[]{:S(2)}) collective-permute-start(bf16[80,2560]{1,0:T(8,128)(2,1)S(1)} %collective-permute-done.9.rest_6_), channel_id=1, source_target_pairs={{0,16},{8,24},{16,32},{24,40},{32,48},{40,56},{48,64},{56,72},{64,... | collective-permute-start | bytes 1228808 | tf_op jit(solution)/shard_map/ppermute | solution.py:61
  81.3 0.0 collective-permute-done.3.xb
  81.3 4.8 %collective-permute-start.12 = (bf16[80,2560]{1,0:T(8,128)(2,1)S(1)}, bf16[80,2560]{1,0:T(8,128)(2,1)S(1)}, u32[]{:S(2)}, u32[]{:S(2)}) collective-permute-start(bf16[80,2560]{1,0:T(8,128)(2,1)S(1)} %collective-permute-done.10.rest_7_), channel_id=1, source_target_pairs={{0,240},{8,248},{16,0},{24,8},{32,16},{40,24},{48,32},{56,40},{64,... | collective-permute-start | bytes 1228808 | tf_op jit(solution)/shard_map/ppermute | solution.py:61
  86.1 0.0 copy-done.7
  86.1 0.1 fusion.4
  86.2 0.0 copy-start.9
  86.2 0.0 copy-start.10
  86.2 0.0 copy-start.6
  86.2 6.6 %collective-permute-done.11.rest_8_ = bf16[80,2560]{1,0:T(8,128)(2,1)S(1)} collective-permute-done((bf16[80,2560]{1,0:T(8,128)(2,1)S(1)}, bf16[80,2560]{1,0:T(8,128)(2,1)S(1)}, u32[]{:S(2)}, u32[]{:S(2)}) %collective-permute-start.11) | collective-permute-done | bytes 409632 | tf_op jit(solution)/shard_map/ppermute | solution.py:61
  92.8 0.8 collective-permute-done.12.rest_9_
  93.6 0.0 collective-permute-done.6.rest_3_
  93.6 3.3 %collective-permute-done.7.rest_4_ = bf16[160,2560]{1,0:T(8,128)(2,1)} collective-permute-done((bf16[160,2560]{1,0:T(8,128)(2,1)}, bf16[160,2560]{1,0:T(8,128)(2,1)}, u32[]{:S(2)}, u32[]{:S(2)}) %collective-permute-start.7) | collective-permute-done | bytes 819232 | tf_op jit(solution)/shard_map/ppermute | solution.py:61
  96.9 0.7 collective-permute-done.8.rest_5_
  97.6 0.0 copy-done.4
  97.6 10.4 %shard_map.94 = (f32[256,1280]{1,0:T(8,128)}, f32[256,1280]{1,0:T(8,128)}) custom-call(s32[20]{0:T(128)S(1)} %concatenate.6.meta, bf16[256,1280]{1,0:T(8,128)(2,1)} %copy-done.4, bf16[256,1280]{1,0:T(8,128)(2,1)} %collective-permute-done.3.xb, f32[1,1920]{1,0:T(1,128)S(1)} %reshape.81.bias, bf16[160,2560]{1,0:T(8,128)(2,1)} %shard_map.92.rest_0_, ...), custom_call_target="tpu_custom_call" | custom-call | tf_op jit(solution)/shard_map/pallas_call | solution.py:284
  108.0 3.7 %collective-permute-start.13 = (f32[256,1280]{1,0:T(8,128)}, f32[256,1280]{1,0:T(8,128)S(1)}, u32[]{:S(2)}, u32[]{:S(2)}) collective-permute-start(f32[256,1280]{1,0:T(8,128)} %get-tuple-element.11), channel_id=1, source_target_pairs={{0,8},{8,0},{16,24},{24,16},{32,40},{40,32},{48,56},{56,48},{64,72... | collective-permute-start | bytes 3932168 | tf_op jit(solution)/shard_map/ppermute | solution.py:61
  111.6 0.0 copy-done.9
  111.6 0.0 copy-done.10
  111.7 2.8 %collective-permute-done.13.other = f32[256,1280]{1,0:T(8,128)S(1)} collective-permute-done((f32[256,1280]{1,0:T(8,128)}, f32[256,1280]{1,0:T(8,128)S(1)}, u32[]{:S(2)}, u32[]{:S(2)}) %collective-permute-start.13) | collective-permute-done | bytes 1310752 | tf_op jit(solution)/shard_map/ppermute | solution.py:61
  114.5 1.3 %copy-done.3 = f32[256,1280]{1,0:T(8,128)S(1)} copy-done((f32[256,1280]{1,0:T(8,128)S(1)}, f32[256,1280]{1,0:T(8,128)}, u32[]{:S(2)}) %copy-start.3) | copy-done | bytes 1310744
  115.8 2.0 %shard_map.95 = bf16[64,5120]{1,0:T(8,128)(2,1)} custom-call(s32[20]{0:T(128)S(1)} %concatenate.6.meta, f32[256,1280]{1,0:T(8,128)S(1)} %copy-done.3, f32[256,1280]{1,0:T(8,128)S(1)} %collective-permute-done.13.other, bf16[256,1280]{1,0:T(8,128)(2,1)S(1)} %copy-done.6, f32[1,1280]{1,0:T(1,128)S(1)} %reshape.82.bias, f32[1,1280]{1,0:T(1,128)S(1)} %reshape.83.gain), custom_call_target="tpu_custom_call" | custom-call | tf_op jit(solution)/shard_map/pallas_call | solution.py:304
  (16 shorter events, 0.1 us)
Async XLA Ops:
  0.0 36.2 %copy-start.1 = (bf16[1,1,7,64,1280]{4,3,2,1,0:T(8,128)(2,1)S(1)}, bf16[1,1,7,64,1280]{4,3,2,1,0:T(8,128)(2,1)}, u32[]{:S(2)}) copy-start(bf16[1,1,7,64,1280]{4,3,2,1,0:T(8,128)(2,1)} %own.1) | copy-start | bytes 3440644
  0.0 48.7 %copy-start.12 = (s32[64,1,7]{0,1,2:T(1,128)S(1)}, s32[64,1,7]{0,1,2:T(1,128)}, u32[]{:S(2)}) copy-start(s32[64,1,7]{0,1,2:T(1,128)} %param.16) | copy-start | bytes 5380
  0.0 49.2 %copy-start.11 = (s32[64,1,7,2]{0,3,2,1:T(2,128)S(1)}, s32[64,1,7,2]{0,3,2,1:T(2,128)}, u32[]{:S(2)}) copy-start(s32[64,1,7,2]{0,3,2,1:T(2,128)} %param.17) | copy-start | bytes 10756
  0.0 50.2 %copy-start.8 = (f32[1280]{0:T(1024)S(1)}, f32[1280]{0:T(1024)}, u32[]{:S(2)}) copy-start(f32[1280]{0:T(1024)} %param.10) | copy-start | bytes 15364
  0.0 50.3 %copy-start = (bf16[160,3840]{1,0:T(8,128)(2,1)S(1)}, bf16[160,3840]{1,0:T(8,128)(2,1)}, u32[]{:S(2)}) copy-start(bf16[160,3840]{1,0:T(8,128)(2,1)} %w.3) | copy-start | bytes 3686404
  0.0 50.3 %copy-start.2 = (bf16[1280,160]{0,1:T(8,128)(2,1)S(1)}, bf16[1280,160]{0,1:T(8,128)(2,1)}, u32[]{:S(2)}) copy-start(bf16[1280,160]{0,1:T(8,128)(2,1)} %param.13) | copy-start | bytes 1228804
  26.0 42.7 %collective-permute-start.4 = (bf16[160,2560]{1,0:T(8,128)(2,1)}, bf16[160,2560]{1,0:T(8,128)(2,1)}, u32[]{:S(2)}, u32[]{:S(2)}) collective-permute-start(bf16[160,2560]{1,0:T(8,128)(2,1)} %shard_map.92.rest_0_), channel_id=1, source_target_pairs={{0,257},{8,265},{16,273},{24,281},{32,289},{40,297},{48,305},{56,3... | collective-permute-start | bytes 2457608 | tf_op jit(solution)/shard_map/ppermute | solution.py:61
  31.5 43.8 %collective-permute-start.5 = (bf16[160,2560]{1,0:T(8,128)(2,1)}, bf16[160,2560]{1,0:T(8,128)(2,1)}, u32[]{:S(2)}, u32[]{:S(2)}) collective-permute-start(bf16[160,2560]{1,0:T(8,128)(2,1)} %shard_map.92.rest_0_), channel_id=1, source_target_pairs={{0,4},{8,12},{16,20},{24,28},{32,36},{40,44},{48,52},{56,60},{64,6... | collective-permute-start | bytes 2457608 | tf_op jit(solution)/shard_map/ppermute | solution.py:61
  36.9 13.4 %collective-permute-start = (bf16[64,1280]{1,0:T(8,128)(2,1)S(1)}, bf16[64,1280]{1,0:T(8,128)(2,1)S(1)}, u32[]{:S(2)}, u32[]{:S(2)}) collective-permute-start(bf16[64,1280]{1,0:T(8,128)(2,1)S(1)} %get-tuple-element.19), channel_id=1, source_target_pairs={{0,8},{8,16},{16,24},{24,32},{32,40},{40,48},{48,56},{56,64},{64,7... | collective-permute-start | bytes 491528 | tf_op jit(solution)/shard_map/ppermute | solution.py:66
  41.6 11.5 %collective-permute-start.1 = (bf16[64,1280]{1,0:T(8,128)(2,1)}, bf16[64,1280]{1,0:T(8,128)(2,1)S(1)}, u32[]{:S(2)}, u32[]{:S(2)}) collective-permute-start(bf16[64,1280]{1,0:T(8,128)(2,1)} %get-tuple-element.18), channel_id=1, source_target_pairs={{0,16},{8,24},{16,32},{24,40},{32,48},{40,56},{48,64},{56,72},{64,... | collective-permute-start | bytes 491528 | tf_op jit(solution)/shard_map/ppermute | solution.py:66
  45.1 14.3 %collective-permute-start.2 = (bf16[64,1280]{1,0:T(8,128)(2,1)}, bf16[64,1280]{1,0:T(8,128)(2,1)}, u32[]{:S(2)}, u32[]{:S(2)}) collective-permute-start(bf16[64,1280]{1,0:T(8,128)(2,1)} %get-tuple-element.17), channel_id=1, source_target_pairs={{0,24},{8,32},{16,40},{24,48},{32,56},{40,64},{48,72},{56,80},{64,... | collective-permute-start | bytes 491528 | tf_op jit(solution)/shard_map/ppermute | solution.py:66
  50.5 35.6 %copy-start.7 = (f32[3840]{0:T(1024)S(1)}, f32[3840]{0:T(1024)}, u32[]{:S(2)}) copy-start(f32[3840]{0:T(1024)} %param.12) | copy-start | bytes 46084
  50.5 21.1 %collective-permute-start.9 = (bf16[80,2560]{1,0:T(8,128)(2,1)S(1)}, bf16[80,2560]{1,0:T(8,128)(2,1)S(1)}, u32[]{:S(2)}, u32[]{:S(2)}) collective-permute-start(bf16[80,2560]{1,0:T(8,128)(2,1)S(1)} %shard_map.93), channel_id=1, source_target_pairs={{0,2},{8,10},{16,18},{24,26},{32,34},{40,42},{48,50},{56,58},{64,6... | collective-permute-start | bytes 1228808 | tf_op jit(solution)/shard_map/ppermute | solution.py:61
  61.8 0.9 copy-start.5
  62.7 34.9 %copy-start.4 = (bf16[256,1280]{1,0:T(8,128)(2,1)}, bf16[256,1280]{1,0:T(8,128)(2,1)S(1)}, u32[]{:S(2)}) copy-start(bf16[256,1280]{1,0:T(8,128)(2,1)S(1)} %get-tuple-element.9.xa) | copy-start | bytes 1966084
  62.7 18.6 %collective-permute-start.3 = (bf16[256,1280]{1,0:T(8,128)(2,1)S(1)}, bf16[256,1280]{1,0:T(8,128)(2,1)}, u32[]{:S(2)}, u32[]{:S(2)}) collective-permute-start(bf16[256,1280]{1,0:T(8,128)(2,1)S(1)} %get-tuple-element.9.xa), channel_id=1, source_target_pairs={{0,8},{8,0},{16,24},{24,16},{32,40},{40,32},{48,56},{56,48},{64,72... | collective-permute-start | bytes 1966088 | tf_op jit(solution)/shard_map/ppermute | solution.py:61
  66.3 13.1 %collective-permute-start.10 = (bf16[80,2560]{1,0:T(8,128)(2,1)S(1)}, bf16[80,2560]{1,0:T(8,128)(2,1)S(1)}, u32[]{:S(2)}, u32[]{:S(2)}) collective-permute-start(bf16[80,2560]{1,0:T(8,128)(2,1)S(1)} %shard_map.93), channel_id=1, source_target_pairs={{0,6},{8,14},{16,22},{24,30},{32,38},{40,46},{48,54},{56,62},{64,7... | collective-permute-start | bytes 1228808 | tf_op jit(solution)/shard_map/ppermute | solution.py:61
  68.7 24.9 %collective-permute-start.6 = (bf16[160,2560]{1,0:T(8,128)(2,1)}, bf16[160,2560]{1,0:T(8,128)(2,1)}, u32[]{:S(2)}, u32[]{:S(2)}) collective-permute-start(bf16[160,2560]{1,0:T(8,128)(2,1)} %collective-permute-done.4.rest_1_), channel_id=1, source_target_pairs={{0,2},{8,10},{16,18},{24,26},{32,34},{40,42},{48,50},{56,58},{64,6... | collective-permute-start | bytes 2457608 | tf_op jit(solution)/shard_map/ppermute | solution.py:61
  71.6 25.3 %collective-permute-start.7 = (bf16[160,2560]{1,0:T(8,128)(2,1)}, bf16[160,2560]{1,0:T(8,128)(2,1)}, u32[]{:S(2)}, u32[]{:S(2)}) collective-permute-start(bf16[160,2560]{1,0:T(8,128)(2,1)} %collective-permute-done.4.rest_1_), channel_id=1, source_target_pairs={{0,6},{8,14},{16,22},{24,30},{32,38},{40,46},{48,54},{56,62},{64,7... | collective-permute-start | bytes 2457608 | tf_op jit(solution)/shard_map/ppermute | solution.py:61
  75.3 22.3 %collective-permute-start.8 = (bf16[160,2560]{1,0:T(8,128)(2,1)}, bf16[160,2560]{1,0:T(8,128)(2,1)}, u32[]{:S(2)}, u32[]{:S(2)}) collective-permute-start(bf16[160,2560]{1,0:T(8,128)(2,1)} %collective-permute-done.5.rest_2_), channel_id=1, source_target_pairs={{0,257},{8,265},{16,273},{24,281},{32,289},{40,297},{48,305},{56,3... | collective-permute-start | bytes 2457608 | tf_op jit(solution)/shard_map/ppermute | solution.py:61
  79.3 13.5 %collective-permute-start.11 = (bf16[80,2560]{1,0:T(8,128)(2,1)S(1)}, bf16[80,2560]{1,0:T(8,128)(2,1)S(1)}, u32[]{:S(2)}, u32[]{:S(2)}) collective-permute-start(bf16[80,2560]{1,0:T(8,128)(2,1)S(1)} %collective-permute-done.9.rest_6_), channel_id=1, source_target_pairs={{0,16},{8,24},{16,32},{24,40},{32,48},{40,56},{48,64},{56,72},{64,... | collective-permute-start | bytes 1228808 | tf_op jit(solution)/shard_map/ppermute | solution.py:61
  81.3 12.4 %collective-permute-start.12 = (bf16[80,2560]{1,0:T(8,128)(2,1)S(1)}, bf16[80,2560]{1,0:T(8,128)(2,1)S(1)}, u32[]{:S(2)}, u32[]{:S(2)}) collective-permute-start(bf16[80,2560]{1,0:T(8,128)(2,1)S(1)} %collective-permute-done.10.rest_7_), channel_id=1, source_target_pairs={{0,240},{8,248},{16,0},{24,8},{32,16},{40,24},{48,32},{56,40},{64,... | collective-permute-start | bytes 1228808 | tf_op jit(solution)/shard_map/ppermute | solution.py:61
  86.2 25.4 %copy-start.9 = (f32[1280]{0:T(1024)S(1)}, f32[1280]{0:T(1024)}, u32[]{:S(2)}) copy-start(f32[1280]{0:T(1024)} %param.14) | copy-start | bytes 15364
  86.2 25.4 %copy-start.10 = (f32[1280]{0:T(1024)S(1)}, f32[1280]{0:T(1024)}, u32[]{:S(2)}) copy-start(f32[1280]{0:T(1024)} %param.15) | copy-start | bytes 15364
  86.2 28.3 %copy-start.6 = (bf16[256,1280]{1,0:T(8,128)(2,1)S(1)}, bf16[256,1280]{1,0:T(8,128)(2,1)}, u32[]{:S(2)}) copy-start(bf16[256,1280]{1,0:T(8,128)(2,1)} %copy-done.5) | copy-start | bytes 1966084
  108.0 6.5 %collective-permute-start.13 = (f32[256,1280]{1,0:T(8,128)}, f32[256,1280]{1,0:T(8,128)S(1)}, u32[]{:S(2)}, u32[]{:S(2)}) collective-permute-start(f32[256,1280]{1,0:T(8,128)} %get-tuple-element.11), channel_id=1, source_target_pairs={{0,8},{8,0},{16,24},{24,16},{32,40},{40,32},{48,56},{56,48},{64,72... | collective-permute-start | bytes 3932168 | tf_op jit(solution)/shard_map/ppermute | solution.py:61
  114.5 1.3 %copy-start.3 = (f32[256,1280]{1,0:T(8,128)S(1)}, f32[256,1280]{1,0:T(8,128)}, u32[]{:S(2)}) copy-start(f32[256,1280]{1,0:T(8,128)} %get-tuple-element.10.mine) | copy-start | bytes 3932164

commit v4 on v2

--- a/solution.py
+++ b/solution.py
@@ -61,7 +61,7 @@
     return lax.ppermute(value, "dp", [(i, (i + by) % devices) for i in range(devices)])
 
 
-def place_kernel(meta, own, in0, in1, in2, gain, placed, normed, sems):
+def place_kernel(meta, own, in0, in1, in2, gain, plus, minus, placed, normed, sems):
     for t in range(RECV):
         rows = placed.at[pl.ds(t * WIN, WIN), :]
         kept = own.at[0, 0, t]
@@ -203,6 +203,8 @@
     bias = jnp.concatenate(
         [lax.dynamic_slice_in_dim(b_qkv, j * D + half, HALF, 0) for j in range(3)]
     )
+    moved = [by_rank(patches[0, 0, RECV + m], m + 1) for m in range(SLOTS - RECV)]
+    piece, *moved = lax.optimization_barrier((piece, *moved))
     far = send(piece, by_x(2))
     cross = send(piece, across_y())
     plus = send(piece, by_x(1))
@@ -211,18 +213,16 @@
     cross_minus = send(cross, by_x(-1))
     cross_far = send(far, across_y())
 
-    moved = [by_rank(patches[0, 0, RECV + m], m + 1) for m in range(SLOTS - RECV)]
-
     meta = tables(route, groups, rank, lane // NYH, lane % NYH)
 
     placed, normed = pl.pallas_call(
         place_kernel,
         out_shape=[jax.ShapeDtypeStruct((ROWS, D), jnp.bfloat16)] * 2,
-        in_specs=[SMEM] + [ANY] * 4 + vmem(1),
+        in_specs=[SMEM] + [ANY] * 4 + vmem(1) + [ANY] * 2,
         out_specs=vmem(2),
         scratch_shapes=[pltpu.SemaphoreType.DMA((RECV,))],
         compiler_params=SMALL,
-    )(meta, patches, *moved, norm_gain.reshape(1, D))
+    )(meta, patches, *moved, norm_gain.reshape(1, D), plus, minus)
     normed_other = send(normed, other_core())
 
     w, w_mine = pl.pallas_call(

time: 89.4 us -> 103 us (1.15)
  waiting for transfers between devices: 18.3 us -> 36.8 us
  starting transfers between devices: 49.9 us -> 45.6 us
    ppermute x10, waiting for transfers between devices: 15.2 us -> 26.3 us  [send(): return lax.ppermute(value, AXES, pairs)]
    ppermute x3, waiting for transfers between devices: 3.12 us -> 10.5 us  [by_rank(): lax.ppermute(value, 'dp', [(i, (i + by) % devices) for i in range(devices)])]
    ppermute x10, starting transfers between devices: 37.9 us -> 33.5 us  [send(): return lax.ppermute(value, AXES, pairs)]
    unnamed x21 -> x15, local copies, waits for them, and re-layouts: 2.62 us -> 1.98 us
  transfers between devices with their start and end apart: 13 -> 13, of which waited for: 6 -> 8; matrix products, arithmetic and copies ran while one was open for 3% -> 4% of each run, Pallas kernels for 8% -> 7%
where the time goes in v4:
time: 103 us; the launch traced here: 102 us
  starting transfers between devices  45.6 us (44%)
  waiting for transfers between devices  36.8 us (36%)
  Pallas kernels  13.3 us (13%)
  local copies, waits for them, and re-layouts  4.86 us (5%)
  other arithmetic  1.2 us (1%)
    ppermute x10, starting transfers between devices, send(): return lax.ppermute(value, AXES, pairs)  33.5 us
    ppermute x10, waiting for transfers between devices, send(): return lax.ppermute(value, AXES, pairs)  26.3 us
    ppermute x3, starting transfers between devices, by_rank(): lax.ppermute(value, 'dp', [(i, (i + by) % devices) for i in range(devices)])  12 us
    ppermute x3, waiting for transfers between devices, by_rank(): lax.ppermute(value, 'dp', [(i, (i + by) % devices) for i in range(devices)])  10.5 us
    pallas_call x1, Pallas kernels, on_device(): pl.pallas_call(attend_kernel, out_shape=[jax.ShapeDtypeStruct((ROWS, HALF...  5.25 us
    pallas_call x1, Pallas kernels, on_device(): pl.pallas_call(gather_kernel, out_shape=[jax.ShapeDtypeStruct((D, 3 * HAL...  3.02 us
    pallas_call x1, Pallas kernels, on_device(): pl.pallas_call(merge_kernel, out_shape=jax.ShapeDtypeStruct((ROWS // MERG...  2.94 us
    pallas_call x1, Pallas kernels, on_device(): pl.pallas_call(place_kernel, out_shape=[jax.ShapeDtypeStruct((ROWS, D), j...  2.06 us
  transfers between devices with their start and end apart: 13, of which 8 were waited for; matrix products, arithmetic and copies ran while one was open for 4% of the time, Pallas kernels for 7%

profile of v4, /device:TPU:1, one launch (start us, length us, event | category | flops | bytes accessed | tf_op | source)
XLA Modules:
  0.0 102.1 jit_solution(8250891586935338887)
XLA Ops:
  0.0 0.0 copy-start
  0.0 1.2 %slice_bitcast_fusion = (bf16[64,1280]{1,0:T(8,128)(2,1)S(1)}, bf16[64,1280]{1,0:T(8,128)(2,1)S(1)}, bf16[64,1280]{1,0:T(8,128)(2,1)S(1)}) fusion(bf16[1,1,7,64,1280]{4,3,2,1,0:T(8,128)(2,1)} %own.1), kind=kLoop, calls=%fused_computation.2 | loop fusion | bytes 983040 | tf_op jit(solution)/shard_map/squeeze | solution.py:206
  1.2 4.9 %collective-permute-start = (bf16[64,1280]{1,0:T(8,128)(2,1)S(1)}, bf16[64,1280]{1,0:T(8,128)(2,1)S(1)}, u32[]{:S(2)}, u32[]{:S(2)}) collective-permute-start(bf16[64,1280]{1,0:T(8,128)(2,1)S(1)} %get-tuple-element.34), channel_id=1, source_target_pairs={{0,8},{8,16},{16,24},{24,32},{32,40},{40,48},{48,56},{56,64},{64,7... | collective-permute-start | bytes 491528 | tf_op jit(solution)/shard_map/ppermute | solution.py:61
  6.1 3.5 %collective-permute-start.1 = (bf16[64,1280]{1,0:T(8,128)(2,1)S(1)}, bf16[64,1280]{1,0:T(8,128)(2,1)S(1)}, u32[]{:S(2)}, u32[]{:S(2)}) collective-permute-start(bf16[64,1280]{1,0:T(8,128)(2,1)S(1)} %get-tuple-element.33), channel_id=1, source_target_pairs={{0,16},{8,24},{16,32},{24,40},{32,48},{40,56},{48,64},{56,72},{64,... | collective-permute-start | bytes 491528 | tf_op jit(solution)/shard_map/ppermute | solution.py:61
  9.7 3.6 %collective-permute-start.2 = (bf16[64,1280]{1,0:T(8,128)(2,1)S(1)}, bf16[64,1280]{1,0:T(8,128)(2,1)S(1)}, u32[]{:S(2)}, u32[]{:S(2)}) collective-permute-start(bf16[64,1280]{1,0:T(8,128)(2,1)S(1)} %get-tuple-element.32), channel_id=1, source_target_pairs={{0,24},{8,32},{16,40},{24,48},{32,56},{40,64},{48,72},{56,80},{64,... | collective-permute-start | bytes 491528 | tf_op jit(solution)/shard_map/ppermute | solution.py:61
  13.3 0.7 copy.16
  14.0 0.0 copy-done
  14.0 0.0 copy-start.6
  14.0 0.0 copy-start.3
  14.0 0.1 pad_add_fusion
  14.1 1.2 %constant_dynamic-slice_fusion.2 = (bf16[160,640]{1,0:T(8,128)(2,1)S(1)}, bf16[160,640]{1,0:T(8,128)(2,1)S(1)}, bf16[160,640]{1,0:T(8,128)(2,1)S(1)}) fusion(bf16[160,3840]{1,0:T(8,128)(2,1)} %param.11, s32[]{:T(128)S(6)} %select_n.123, s32[]{:T(128)S(6)} %select_n.125, s32[]{:T(128)S(6)} %select_n.124), kind=kLoop, calls=%fused_computation.24 | loop fusion | bytes 1228812 | tf_op jit(solution)/shard_map/dynamic_slice | solution.py:199
  15.3 0.1 pad_maximum_fusion.rest_0_
  15.3 0.1 fusion.2
  15.4 0.0 collective-permute-done.in0
  15.4 4.6 %collective-permute-done.1.in1 = bf16[64,1280]{1,0:T(8,128)(2,1)S(1)} collective-permute-done((bf16[64,1280]{1,0:T(8,128)(2,1)S(1)}, bf16[64,1280]{1,0:T(8,128)(2,1)S(1)}, u32[]{:S(2)}, u32[]{:S(2)}) %collective-permute-start.1) | collective-permute-done | bytes 163872 | tf_op jit(solution)/shard_map/ppermute | solution.py:61
  20.0 6.0 %collective-permute-done.2.in2 = bf16[64,1280]{1,0:T(8,128)(2,1)S(1)} collective-permute-done((bf16[64,1280]{1,0:T(8,128)(2,1)S(1)}, bf16[64,1280]{1,0:T(8,128)(2,1)S(1)}, u32[]{:S(2)}, u32[]{:S(2)}) %collective-permute-start.2) | collective-permute-done | bytes 163872 | tf_op jit(solution)/shard_map/ppermute | solution.py:61
  25.9 4.6 %collective-permute-start.7 = (bf16[160,2560]{1,0:T(8,128)(2,1)S(1)}, bf16[160,2560]{1,0:T(8,128)(2,1)}, u32[]{:S(2)}, u32[]{:S(2)}) collective-permute-start(bf16[160,2560]{1,0:T(8,128)(2,1)S(1)} %pad_maximum_fusion.rest_0_), channel_id=1, source_target_pairs={{0,4},{8,12},{16,20},{24,28},{32,36},{40,44},{48,52},{56,60},{64,6... | collective-permute-start | bytes 2457608 | tf_op jit(solution)/shard_map/ppermute | solution.py:56
  30.6 3.8 %collective-permute-start.6 = (bf16[160,2560]{1,0:T(8,128)(2,1)S(1)}, bf16[160,2560]{1,0:T(8,128)(2,1)}, u32[]{:S(2)}, u32[]{:S(2)}) collective-permute-start(bf16[160,2560]{1,0:T(8,128)(2,1)S(1)} %pad_maximum_fusion.rest_0_), channel_id=1, source_target_pairs={{0,257},{8,265},{16,273},{24,281},{32,289},{40,297},{48,305},{56,3... | collective-permute-start | bytes 2457608 | tf_op jit(solution)/shard_map/ppermute | solution.py:56
  34.4 0.3 select_reduce_fusion.1
  34.7 2.2 %collective-permute-start.3 = (bf16[160,2560]{1,0:T(8,128)(2,1)S(1)}, bf16[160,2560]{1,0:T(8,128)(2,1)S(1)}, u32[]{:S(2)}, u32[]{:S(2)}) collective-permute-start(bf16[160,2560]{1,0:T(8,128)(2,1)S(1)} %pad_maximum_fusion.rest_0_), channel_id=1, source_target_pairs={{0,2},{8,10},{16,18},{24,26},{32,34},{40,42},{48,50},{56,58},{64,6... | collective-permute-start | bytes 2457608 | tf_op jit(solution)/shard_map/ppermute | solution.py:56
  36.9 4.3 %collective-permute-start.4 = (bf16[160,2560]{1,0:T(8,128)(2,1)S(1)}, bf16[160,2560]{1,0:T(8,128)(2,1)S(1)}, u32[]{:S(2)}, u32[]{:S(2)}) collective-permute-start(bf16[160,2560]{1,0:T(8,128)(2,1)S(1)} %pad_maximum_fusion.rest_0_), channel_id=1, source_target_pairs={{0,6},{8,14},{16,22},{24,30},{32,38},{40,46},{48,54},{56,62},{64,7... | collective-permute-start | bytes 2457608 | tf_op jit(solution)/shard_map/ppermute | solution.py:56
  41.2 0.0 copy-done.6
  41.2 0.3 select_reduce_fusion
  41.6 0.1 copy.13
  41.7 0.0 copy-done.3
  41.8 0.2 slice_reduce_fusion
  42.0 0.2 fusion
  42.2 0.2 select_reduce_fusion.2
  42.4 10.1 %collective-permute-done.6.rest_3_ = bf16[160,2560]{1,0:T(8,128)(2,1)} collective-permute-done((bf16[160,2560]{1,0:T(8,128)(2,1)S(1)}, bf16[160,2560]{1,0:T(8,128)(2,1)}, u32[]{:S(2)}, u32[]{:S(2)}) %collective-permute-start.6) | collective-permute-done | bytes 819232 | tf_op jit(solution)/shard_map/ppermute | solution.py:56
  52.4 2.2 %collective-permute-start.8 = (bf16[160,2560]{1,0:T(8,128)(2,1)}, bf16[160,2560]{1,0:T(8,128)(2,1)}, u32[]{:S(2)}, u32[]{:S(2)}) collective-permute-start(bf16[160,2560]{1,0:T(8,128)(2,1)} %collective-permute-done.6.rest_3_), channel_id=1, source_target_pairs={{0,2},{8,10},{16,18},{24,26},{32,34},{40,42},{48,50},{56,58},{64,6... | collective-permute-start | bytes 2457608 | tf_op jit(solution)/shard_map/ppermute | solution.py:56
  54.7 4.3 %collective-permute-start.9 = (bf16[160,2560]{1,0:T(8,128)(2,1)}, bf16[160,2560]{1,0:T(8,128)(2,1)}, u32[]{:S(2)}, u32[]{:S(2)}) collective-permute-start(bf16[160,2560]{1,0:T(8,128)(2,1)} %collective-permute-done.6.rest_3_), channel_id=1, source_target_pairs={{0,6},{8,14},{16,22},{24,30},{32,38},{40,46},{48,54},{56,62},{64,7... | collective-permute-start | bytes 2457608 | tf_op jit(solution)/shard_map/ppermute | solution.py:56
  58.9 0.0 collective-permute-done.7.rest_4_
  59.0 3.8 %collective-permute-start.10 = (bf16[160,2560]{1,0:T(8,128)(2,1)}, bf16[160,2560]{1,0:T(8,128)(2,1)}, u32[]{:S(2)}, u32[]{:S(2)}) collective-permute-start(bf16[160,2560]{1,0:T(8,128)(2,1)} %collective-permute-done.7.rest_4_), channel_id=1, source_target_pairs={{0,257},{8,265},{16,273},{24,281},{32,289},{40,297},{48,305},{56,3... | collective-permute-start | bytes 2457608 | tf_op jit(solution)/shard_map/ppermute | solution.py:56
  62.8 0.1 concatenate.9.meta
  62.9 4.2 %collective-permute-done.3.plus.rest_1_ = bf16[160,2560]{1,0:T(8,128)(2,1)S(1)} collective-permute-done((bf16[160,2560]{1,0:T(8,128)(2,1)S(1)}, bf16[160,2560]{1,0:T(8,128)(2,1)S(1)}, u32[]{:S(2)}, u32[]{:S(2)}) %collective-permute-start.3) | collective-permute-done | bytes 819232 | tf_op jit(solution)/shard_map/ppermute | solution.py:56
  67.0 0.0 collective-permute-done.4.minus.rest_2_
  67.0 0.0 copy-start.1
  67.1 1.3 %copy-done.1 = bf16[1,1,7,64,1280]{4,3,2,1,0:T(8,128)(2,1)S(1)} copy-done((bf16[1,1,7,64,1280]{4,3,2,1,0:T(8,128)(2,1)S(1)}, bf16[1,1,7,64,1280]{4,3,2,1,0:T(8,128)(2,1)}, u32[]{:S(2)}) %copy-start.1) | copy-done | bytes 1146904
  68.3 2.1 %shard_map.91 = (bf16[256,1280]{1,0:T(8,128)(2,1)S(1)}, bf16[256,1280]{1,0:T(8,128)(2,1)S(1)}) custom-call(s32[20]{0:T(128)S(1)} %concatenate.9.meta, bf16[1,1,7,64,1280]{4,3,2,1,0:T(8,128)(2,1)S(1)} %copy-done.1, bf16[64,1280]{1,0:T(8,128)(2,1)S(1)} %collective-permute-done.in0, bf16[64,1280]{1,0:T(8,128)(2,1)S(1)} %collective-permute-done.1.in1, ...), custom_call_target="tpu_custom_call" | custom-call | tf_op jit(solution)/shard_map/pallas_call | solution.py:218
  70.4 0.0 copy-start.2
  70.4 3.8 %collective-permute-start.5 = (bf16[256,1280]{1,0:T(8,128)(2,1)S(1)}, bf16[256,1280]{1,0:T(8,128)(2,1)S(1)}, u32[]{:S(2)}, u32[]{:S(2)}) collective-permute-start(bf16[256,1280]{1,0:T(8,128)(2,1)S(1)} %get-tuple-element.19.xa), channel_id=1, source_target_pairs={{0,8},{8,0},{16,24},{24,16},{32,40},{40,32},{48,56},{56,48},{64,72... | collective-permute-start | bytes 1966088 | tf_op jit(solution)/shard_map/ppermute | solution.py:56
  74.2 1.7 %collective-permute-done.5.rest_8_.xb = bf16[256,1280]{1,0:T(8,128)(2,1)S(1)} collective-permute-done((bf16[256,1280]{1,0:T(8,128)(2,1)S(1)}, bf16[256,1280]{1,0:T(8,128)(2,1)S(1)}, u32[]{:S(2)}, u32[]{:S(2)}) %collective-permute-start.5) | collective-permute-done | bytes 655392 | tf_op jit(solution)/shard_map/ppermute | solution.py:56
  75.9 3.6 %collective-permute-done.10.rest_7_ = bf16[160,2560]{1,0:T(8,128)(2,1)} collective-permute-done((bf16[160,2560]{1,0:T(8,128)(2,1)}, bf16[160,2560]{1,0:T(8,128)(2,1)}, u32[]{:S(2)}, u32[]{:S(2)}) %collective-permute-start.10) | collective-permute-done | bytes 819232 | tf_op jit(solution)/shard_map/ppermute | solution.py:56
  79.5 5.2 %collective-permute-done.8.rest_5_ = bf16[160,2560]{1,0:T(8,128)(2,1)} collective-permute-done((bf16[160,2560]{1,0:T(8,128)(2,1)}, bf16[160,2560]{1,0:T(8,128)(2,1)}, u32[]{:S(2)}, u32[]{:S(2)}) %collective-permute-start.8) | collective-permute-done | bytes 819232 | tf_op jit(solution)/shard_map/ppermute | solution.py:56
  84.7 0.0 collective-permute-done.9.rest_6_
  84.7 3.0 %shard_map.92 = (bf16[1280,1920]{1,0:T(8,128)(2,1)S(1)}, bf16[1280,640]{1,0:T(8,128)(2,1)S(1)}) custom-call(s32[20]{0:T(128)S(1)} %concatenate.9.meta, bf16[160,2560]{1,0:T(8,128)(2,1)S(1)} %pad_maximum_fusion.rest_0_, bf16[160,2560]{1,0:T(8,128)(2,1)S(1)} %collective-permute-done.3.plus.rest_1_, bf16[160,2560]{1,0:T(8,128)(2,1)S(1)} %collective-permute-done.4.minus.rest_2_, ...), custom_call_target="tpu_custom_call" | custom-call | tf_op jit(solution)/shard_map/pallas_call | solution.py:228
  87.7 2.5 %collective-permute-start.12 = (bf16[1280,640]{1,0:T(8,128)(2,1)S(1)}, bf16[1280,640]{1,0:T(8,128)(2,1)S(1)}, u32[]{:S(2)}, u32[]{:S(2)}) collective-permute-start(bf16[1280,640]{1,0:T(8,128)(2,1)S(1)} %get-tuple-element.23.wa), channel_id=1, source_target_pairs={{0,8},{8,0},{16,24},{24,16},{32,40},{40,32},{48,56},{56,48},{64,72... | collective-permute-start | bytes 4915208 | tf_op jit(solution)/shard_map/ppermute | solution.py:56
  90.3 0.0 copy-done.2
  90.3 0.1 fusion.4
  90.4 0.0 copy-start.4
  90.4 0.0 copy-start.5
  90.4 5.3 %shard_map.93 = (bf16[256,640]{1,0:T(8,128)(2,1)S(1)}, bf16[256,640]{1,0:T(8,128)(2,1)S(1)}) custom-call(s32[20]{0:T(128)S(1)} %concatenate.9.meta, bf16[256,1280]{1,0:T(8,128)(2,1)S(1)} %get-tuple-element.19.xa, bf16[256,1280]{1,0:T(8,128)(2,1)S(1)} %collective-permute-done.5.rest_8_.xb, f32[1,1920]{1,0:T(1,128)S(1)} %reshape.81.bias, ...), custom_call_target="tpu_custom_call" | custom-call | tf_op jit(solution)/shard_map/pallas_call | solution.py:241
  95.7 1.9 %collective-permute-start.11 = (bf16[256,640]{1,0:T(8,128)(2,1)S(1)}, bf16[256,640]{1,0:T(8,128)(2,1)S(1)}, u32[]{:S(2)}, u32[]{:S(2)}) collective-permute-start(bf16[256,640]{1,0:T(8,128)(2,1)S(1)} %get-tuple-element.22), channel_id=1, source_target_pairs={{0,8},{8,0},{16,24},{24,16},{32,40},{40,32},{48,56},{56,48},{64,72... | collective-permute-start | bytes 983048 | tf_op jit(solution)/shard_map/ppermute | solution.py:56
  97.6 0.0 copy-done.4
  97.6 0.0 copy-done.5
  97.6 1.5 %collective-permute-done.11.attb = bf16[256,640]{1,0:T(8,128)(2,1)S(1)} collective-permute-done((bf16[256,640]{1,0:T(8,128)(2,1)S(1)}, bf16[256,640]{1,0:T(8,128)(2,1)S(1)}, u32[]{:S(2)}, u32[]{:S(2)}) %collective-permute-start.11) | collective-permute-done | bytes 327712 | tf_op jit(solution)/shard_map/ppermute | solution.py:56
  99.2 0.0 collective-permute-done.12.wb
  99.2 2.9 %shard_map.94 = bf16[64,5120]{1,0:T(8,128)(2,1)} custom-call(s32[20]{0:T(128)S(1)} %concatenate.9.meta, bf16[256,640]{1,0:T(8,128)(2,1)S(1)} %get-tuple-element.21.atta, bf16[256,640]{1,0:T(8,128)(2,1)S(1)} %collective-permute-done.11.attb, bf16[1280,640]{1,0:T(8,128)(2,1)S(1)} %get-tuple-element.23.wa, bf16[1280,640]{1,0:T(8,128)(2,1)S(1)} %collective-permute-done.12.wb, ...), custom_call_target="tpu_custom_call" | custom-call | tf_op jit(solution)/shard_map/pallas_call | solution.py:251
  (10 shorter events, 0.1 us)
Async XLA Ops:
  0.0 14.0 %copy-start = (bf16[1280,160]{0,1:T(8,128)(2,1)S(1)}, bf16[1280,160]{0,1:T(8,128)(2,1)}, u32[]{:S(2)}) copy-start(bf16[1280,160]{0,1:T(8,128)(2,1)} %param.13) | copy-start | bytes 1228804
  1.2 14.2 %collective-permute-start = (bf16[64,1280]{1,0:T(8,128)(2,1)S(1)}, bf16[64,1280]{1,0:T(8,128)(2,1)S(1)}, u32[]{:S(2)}, u32[]{:S(2)}) collective-permute-start(bf16[64,1280]{1,0:T(8,128)(2,1)S(1)} %get-tuple-element.34), channel_id=1, source_target_pairs={{0,8},{8,16},{16,24},{24,32},{32,40},{40,48},{48,56},{56,64},{64,7... | collective-permute-start | bytes 491528 | tf_op jit(solution)/shard_map/ppermute | solution.py:61
  6.1 13.9 %collective-permute-start.1 = (bf16[64,1280]{1,0:T(8,128)(2,1)S(1)}, bf16[64,1280]{1,0:T(8,128)(2,1)S(1)}, u32[]{:S(2)}, u32[]{:S(2)}) collective-permute-start(bf16[64,1280]{1,0:T(8,128)(2,1)S(1)} %get-tuple-element.33), channel_id=1, source_target_pairs={{0,16},{8,24},{16,32},{24,40},{32,48},{40,56},{48,64},{56,72},{64,... | collective-permute-start | bytes 491528 | tf_op jit(solution)/shard_map/ppermute | solution.py:61
  9.7 16.3 %collective-permute-start.2 = (bf16[64,1280]{1,0:T(8,128)(2,1)S(1)}, bf16[64,1280]{1,0:T(8,128)(2,1)S(1)}, u32[]{:S(2)}, u32[]{:S(2)}) collective-permute-start(bf16[64,1280]{1,0:T(8,128)(2,1)S(1)} %get-tuple-element.32), channel_id=1, source_target_pairs={{0,24},{8,32},{16,40},{24,48},{32,56},{40,64},{48,72},{56,80},{64,... | collective-permute-start | bytes 491528 | tf_op jit(solution)/shard_map/ppermute | solution.py:61
  14.0 27.3 %copy-start.6 = (s32[64,1,7,2]{0,3,2,1:T(2,128)S(1)}, s32[64,1,7,2]{0,3,2,1:T(2,128)}, u32[]{:S(2)}) copy-start(s32[64,1,7,2]{0,3,2,1:T(2,128)} %param.17) | copy-start | bytes 10756
  14.0 27.8 %copy-start.3 = (f32[1280]{0:T(1024)S(1)}, f32[1280]{0:T(1024)}, u32[]{:S(2)}) copy-start(f32[1280]{0:T(1024)} %param.10) | copy-start | bytes 15364
  25.9 33.0 %collective-permute-start.7 = (bf16[160,2560]{1,0:T(8,128)(2,1)S(1)}, bf16[160,2560]{1,0:T(8,128)(2,1)}, u32[]{:S(2)}, u32[]{:S(2)}) collective-permute-start(bf16[160,2560]{1,0:T(8,128)(2,1)S(1)} %pad_maximum_fusion.rest_0_), channel_id=1, source_target_pairs={{0,4},{8,12},{16,20},{24,28},{32,36},{40,44},{48,52},{56,60},{64,6... | collective-permute-start | bytes 2457608 | tf_op jit(solution)/shard_map/ppermute | solution.py:56
  30.6 21.9 %collective-permute-start.6 = (bf16[160,2560]{1,0:T(8,128)(2,1)S(1)}, bf16[160,2560]{1,0:T(8,128)(2,1)}, u32[]{:S(2)}, u32[]{:S(2)}) collective-permute-start(bf16[160,2560]{1,0:T(8,128)(2,1)S(1)} %pad_maximum_fusion.rest_0_), channel_id=1, source_target_pairs={{0,257},{8,265},{16,273},{24,281},{32,289},{40,297},{48,305},{56,3... | collective-permute-start | bytes 2457608 | tf_op jit(solution)/shard_map/ppermute | solution.py:56
  34.7 32.3 %collective-permute-start.3 = (bf16[160,2560]{1,0:T(8,128)(2,1)S(1)}, bf16[160,2560]{1,0:T(8,128)(2,1)S(1)}, u32[]{:S(2)}, u32[]{:S(2)}) collective-permute-start(bf16[160,2560]{1,0:T(8,128)(2,1)S(1)} %pad_maximum_fusion.rest_0_), channel_id=1, source_target_pairs={{0,2},{8,10},{16,18},{24,26},{32,34},{40,42},{48,50},{56,58},{64,6... | collective-permute-start | bytes 2457608 | tf_op jit(solution)/shard_map/ppermute | solution.py:56
  36.9 30.1 %collective-permute-start.4 = (bf16[160,2560]{1,0:T(8,128)(2,1)S(1)}, bf16[160,2560]{1,0:T(8,128)(2,1)S(1)}, u32[]{:S(2)}, u32[]{:S(2)}) collective-permute-start(bf16[160,2560]{1,0:T(8,128)(2,1)S(1)} %pad_maximum_fusion.rest_0_), channel_id=1, source_target_pairs={{0,6},{8,14},{16,22},{24,30},{32,38},{40,46},{48,54},{56,62},{64,7... | collective-permute-start | bytes 2457608 | tf_op jit(solution)/shard_map/ppermute | solution.py:56
  52.4 32.3 %collective-permute-start.8 = (bf16[160,2560]{1,0:T(8,128)(2,1)}, bf16[160,2560]{1,0:T(8,128)(2,1)}, u32[]{:S(2)}, u32[]{:S(2)}) collective-permute-start(bf16[160,2560]{1,0:T(8,128)(2,1)} %collective-permute-done.6.rest_3_), channel_id=1, source_target_pairs={{0,2},{8,10},{16,18},{24,26},{32,34},{40,42},{48,50},{56,58},{64,6... | collective-permute-start | bytes 2457608 | tf_op jit(solution)/shard_map/ppermute | solution.py:56
  54.7 30.0 %collective-permute-start.9 = (bf16[160,2560]{1,0:T(8,128)(2,1)}, bf16[160,2560]{1,0:T(8,128)(2,1)}, u32[]{:S(2)}, u32[]{:S(2)}) collective-permute-start(bf16[160,2560]{1,0:T(8,128)(2,1)} %collective-permute-done.6.rest_3_), channel_id=1, source_target_pairs={{0,6},{8,14},{16,22},{24,30},{32,38},{40,46},{48,54},{56,62},{64,7... | collective-permute-start | bytes 2457608 | tf_op jit(solution)/shard_map/ppermute | solution.py:56
  59.0 20.6 %collective-permute-start.10 = (bf16[160,2560]{1,0:T(8,128)(2,1)}, bf16[160,2560]{1,0:T(8,128)(2,1)}, u32[]{:S(2)}, u32[]{:S(2)}) collective-permute-start(bf16[160,2560]{1,0:T(8,128)(2,1)} %collective-permute-done.7.rest_4_), channel_id=1, source_target_pairs={{0,257},{8,265},{16,273},{24,281},{32,289},{40,297},{48,305},{56,3... | collective-permute-start | bytes 2457608 | tf_op jit(solution)/shard_map/ppermute | solution.py:56
  67.0 1.3 %copy-start.1 = (bf16[1,1,7,64,1280]{4,3,2,1,0:T(8,128)(2,1)S(1)}, bf16[1,1,7,64,1280]{4,3,2,1,0:T(8,128)(2,1)}, u32[]{:S(2)}) copy-start(bf16[1,1,7,64,1280]{4,3,2,1,0:T(8,128)(2,1)} %own.1) | copy-start | bytes 3440644
  70.4 19.9 %copy-start.2 = (f32[3840]{0:T(1024)S(1)}, f32[3840]{0:T(1024)}, u32[]{:S(2)}) copy-start(f32[3840]{0:T(1024)} %param.12) | copy-start | bytes 46084
  70.4 5.5 %collective-permute-start.5 = (bf16[256,1280]{1,0:T(8,128)(2,1)S(1)}, bf16[256,1280]{1,0:T(8,128)(2,1)S(1)}, u32[]{:S(2)}, u32[]{:S(2)}) collective-permute-start(bf16[256,1280]{1,0:T(8,128)(2,1)S(1)} %get-tuple-element.19.xa), channel_id=1, source_target_pairs={{0,8},{8,0},{16,24},{24,16},{32,40},{40,32},{48,56},{56,48},{64,72... | collective-permute-start | bytes 1966088 | tf_op jit(solution)/shard_map/ppermute | solution.py:56
  87.7 11.5 %collective-permute-start.12 = (bf16[1280,640]{1,0:T(8,128)(2,1)S(1)}, bf16[1280,640]{1,0:T(8,128)(2,1)S(1)}, u32[]{:S(2)}, u32[]{:S(2)}) collective-permute-start(bf16[1280,640]{1,0:T(8,128)(2,1)S(1)} %get-tuple-element.23.wa), channel_id=1, source_target_pairs={{0,8},{8,0},{16,24},{24,16},{32,40},{40,32},{48,56},{56,48},{64,72... | collective-permute-start | bytes 4915208 | tf_op jit(solution)/shard_map/ppermute | solution.py:56
  90.4 7.2 %copy-start.4 = (f32[1280]{0:T(1024)S(1)}, f32[1280]{0:T(1024)}, u32[]{:S(2)}) copy-start(f32[1280]{0:T(1024)} %param.14) | copy-start | bytes 15364
  90.4 7.2 %copy-start.5 = (f32[1280]{0:T(1024)S(1)}, f32[1280]{0:T(1024)}, u32[]{:S(2)}) copy-start(f32[1280]{0:T(1024)} %param.15) | copy-start | bytes 15364
  95.7 3.5 %collective-permute-start.11 = (bf16[256,640]{1,0:T(8,128)(2,1)S(1)}, bf16[256,640]{1,0:T(8,128)(2,1)S(1)}, u32[]{:S(2)}, u32[]{:S(2)}) collective-permute-start(bf16[256,640]{1,0:T(8,128)(2,1)S(1)} %get-tuple-element.22), channel_id=1, source_target_pairs={{0,8},{8,0},{16,24},{24,16},{32,40},{40,32},{48,56},{56,48},{64,72... | collective-permute-start | bytes 983048 | tf_op jit(solution)/shard_map/ppermute | solution.py:56

commit v5 on v2

--- a/solution.py
+++ b/solution.py
@@ -40,12 +40,13 @@
     return [(flat(*p), flat(*move(*p))) for p in places]
 
 
-def by_x(d):
-    return perm(lambda x, yh, yl, z, c: (x + d, yh, yl, z, c))
-
-
-def across_y():
-    return perm(lambda x, yh, yl, z, c: (x, 1 - yh, 1 - yl, z, c))
+def moves(even, odd=None):
+    def move(x, yh, yl, z, c):
+        dx, across = odd if c else even
+        return x + dx, yh ^ across, yl ^ across, z, c
+
+    pairs = perm(lambda *p: move(*p) if odd or p[-1] == 0 else p)
+    return pairs if odd else [p for p in pairs if p[0] != p[1]]
 
 
 def other_core():
@@ -80,20 +81,39 @@
         normed[rows, :] = (x * lax.rsqrt(ms + EPS) * gain[...]).astype(jnp.bfloat16)
 
 
-def gather_kernel(meta, *rest):
-    pieces, (_, w, wo, sems) = rest[:SHARDS], rest[SHARDS:]
-    copies = []
-    for i in range(SHARDS):
-        at = pl.ds(pl.multiple_of(meta[12 + i] * DEPTH, DEPTH), DEPTH)
-        for j, dst in enumerate((w, wo)):
-            cols = pl.ds(j * 3 * HALF, (3 - 2 * j) * HALF)
-            copies.append(
-                pltpu.make_async_copy(pieces[i].at[:, cols], dst.at[at, :], sems.at[i, j])
+def gather_kernel(meta, own, a, b, c, d, early, late, _, w, wo, sems):
+    core = lax.rem(lax.axis_index("dp"), NC)
+    sources = [(ref, 0) for ref in (own, a, b, c)]
+    sources += [(early, 0), (early, DEPTH), (late, 0)]
+
+    def copies(i, ref, row):
+        at = pl.multiple_of(meta[12 + i] * DEPTH, DEPTH)
+        return [
+            pltpu.make_async_copy(
+                ref.at[pl.ds(row, DEPTH), pl.ds(j * 3 * HALF, (3 - 2 * j) * HALF)],
+                dst.at[pl.ds(at, DEPTH), :],
+                sems.at[i, j],
             )
-    for copy in copies:
-        copy.start()
-    for copy in copies:
-        copy.wait()
+            for j, dst in enumerate((w, wo))
+        ]
+
+    for i, source in enumerate(sources):
+        for copy in copies(i, *source):
+            copy.start()
+
+    @pl.when(core == 0)
+    def _():
+        for copy in copies(SHARDS - 1, d, 0):
+            copy.start()
+
+    @pl.when(core != 0)
+    def _():
+        for copy in copies(SHARDS - 1, late, DEPTH):
+            copy.start()
+
+    for i, source in enumerate((*sources, (late, DEPTH))):
+        for copy in copies(i, *source):
+            copy.wait()
 
 
 def attend_kernel(meta, xa, xb, bias, w, outa, outb, q, k, v):
@@ -184,8 +204,13 @@
     lands = (there[:, :, 0] == who[:, None])[:, :, None] & (there[:, :, 1][:, :, None] == target)
     src = jnp.sum(jnp.where(lands, slot[None, :, None], 0), axis=1)
     grp = jnp.sum(jnp.where(lands, count[:, :, None], 0), axis=1)
-    steps = [(0, 0), (-1, 0), (1, 0), (0, 1), (2, 0), (-1, 1), (1, 1), (2, 1)]
-    shard = jnp.stack([((x + dx) % NX) * NYH + (yh + dy) % NYH for dx, dy in steps])
+    even = [(-1, 0), (0, 1), (-1, 1)]
+    odd = [(1, 0), (2, 0), (2, 1)]
+    orders = [
+        [((x + dx) % NX) * NYH + (yh + dy) % NYH for dx, dy in [(0, 0), *one, *two, (1, 1)]]
+        for one, two in ((even, odd), (odd, even))
+    ]
+    shard = jnp.where(rank % NC == 0, jnp.stack(orders[0]), jnp.stack(orders[1]))
     return jnp.concatenate([src[0], grp[0], grp[1], shard]).astype(jnp.int32)
 
 
@@ -195,23 +220,29 @@
     core = rank % NC
     half = core * HALF
 
-    piece = jnp.concatenate(
-        [lax.dynamic_slice_in_dim(w_qkv, j * D + half, HALF, 1) for j in range(3)]
-        + [lax.dynamic_slice_in_dim(jnp.transpose(w_proj), half, HALF, 1)],
-        axis=1,
-    )
+    def columns(at):
+        return jnp.concatenate(
+            [lax.dynamic_slice_in_dim(w_qkv, j * D + at, HALF, 1) for j in range(3)]
+            + [lax.dynamic_slice_in_dim(jnp.transpose(w_proj), at, HALF, 1)],
+            axis=1,
+        )
+
+    piece = jnp.concatenate([columns(half), columns(HALF - half)], axis=0)
     bias = jnp.concatenate(
         [lax.dynamic_slice_in_dim(b_qkv, j * D + half, HALF, 0) for j in range(3)]
     )
-    far = send(piece, by_x(2))
-    cross = send(piece, across_y())
-    plus = send(piece, by_x(1))
-    minus = send(piece, by_x(-1))
-    cross_plus = send(cross, by_x(1))
-    cross_minus = send(cross, by_x(-1))
-    cross_far = send(far, across_y())
-
+    def halves_of(*shards):
+        return jnp.concatenate([value[DEPTH:] for value in shards], axis=0)
+
+    got_b = send(piece, moves((0, 1), (2, 0)))
+    got_a = send(piece, moves((1, 0), (-1, 0)))
+    got_c = send(got_b, moves((1, 0), (0, 1)))
+    got_d = send(got_b, moves((-1, 0)))
     moved = [by_rank(patches[0, 0, RECV + m], m + 1) for m in range(SLOTS - RECV)]
+    early, moved[0] = lax.optimization_barrier((halves_of(got_a, got_b), moved[0]))
+    early = send(early, other_core())
+    late = send(halves_of(got_c, got_d), other_core())
+
 
     meta = tables(route, groups, rank, lane // NYH, lane % NYH)
 
@@ -231,11 +262,11 @@
             jax.ShapeDtypeStruct((D, 3 * HALF), jnp.bfloat16),
             jax.ShapeDtypeStruct((D, HALF), jnp.bfloat16),
         ],
-        in_specs=[SMEM] + [ANY] * (SHARDS + 1),
+        in_specs=[SMEM] + [ANY] * 8,
         out_specs=vmem(2),
         scratch_shapes=[pltpu.SemaphoreType.DMA((SHARDS, 2))],
         compiler_params=PARAMS,
-    )(meta, piece, plus, minus, cross, far, cross_plus, cross_minus, cross_far, normed_other)
+    )(meta, piece, got_a, got_b, got_c, got_d, early, late, normed_other)
     w_other = send(w_mine, other_core())
 
     att, att_theirs = pl.pallas_call(

time: 89.4 us -> 106 us (1.19)
  waiting for transfers between devices: 18.3 us -> 31.3 us
  other arithmetic: 1.19 us -> 11.2 us
  starting transfers between devices: 49.9 us -> 40.8 us
  local copies, waits for them, and re-layouts: 5.25 us -> 9.01 us
    ppermute x10 -> x9, waiting for transfers between devices: 15.2 us -> 30.6 us  [send(): return lax.ppermute(value, AXES, pairs)]
    concatenate x1 -> x4, other arithmetic: 0.06 us -> 10.1 us  [the longest x1 9.8 us: on_device(): piece = jnp.concatenate([columns(half), columns(HALF - half)], axis=0)]
    ppermute x10 -> x9, starting transfers between devices: 37.9 us -> 28.3 us  [send(): return lax.ppermute(value, AXES, pairs)]
    slice x0 -> x4, local copies, waits for them, and re-layouts: none -> 3.66 us  [halves_of(): return jnp.concatenate([value[DEPTH:] for value in shards], axis=0)]
    ppermute x3, waiting for transfers between devices: 3.12 us -> 0.66 us  [by_rank(): lax.ppermute(value, 'dp', [(i, (i + by) % devices) for i in range(devices)])]
    unnamed x21 -> x17, local copies, waits for them, and re-layouts: 2.62 us -> 0.35 us
    dynamic_slice x2, local copies, waits for them, and re-layouts: 1.3 us -> 2.56 us  [the longest x1 1.49 us: columns(): lax.dynamic_slice_in_dim(w_qkv, j * D + at, HALF, 1)]
  transfers between devices with their start and end apart: 13 -> 12, of which waited for: 6 -> 4; matrix products, arithmetic and copies ran while one was open for 3% -> 7% of each run, Pallas kernels for 8% -> 7%
where the time goes in v5:
time: 106 us; the launch traced here: 105 us
  starting transfers between devices  40.8 us (38%)
  waiting for transfers between devices  31.3 us (30%)
  Pallas kernels  12.4 us (12%)
  other arithmetic  11.2 us (11%)
  local copies, waits for them, and re-layouts  9.01 us (8%)
    ppermute x9, waiting for transfers between devices, send(): return lax.ppermute(value, AXES, pairs)  30.6 us
    ppermute x9, starting transfers between devices, send(): return lax.ppermute(value, AXES, pairs)  28.3 us
    ppermute x3, starting transfers between devices, by_rank(): lax.ppermute(value, 'dp', [(i, (i + by) % devices) for i in range(devices)])  12.6 us
    concatenate x1, other arithmetic, on_device(): piece = jnp.concatenate([columns(half), columns(HALF - half)], axis=0)  9.8 us
    pallas_call x1, Pallas kernels, on_device(): pl.pallas_call(attend_kernel, out_shape=[jax.ShapeDtypeStruct((ROWS, HALF...  5.26 us
    slice x4, local copies, waits for them, and re-layouts, halves_of(): return jnp.concatenate([value[DEPTH:] for value in shards], axis=0)  3.66 us
    pallas_call x1, Pallas kernels, on_device(): pl.pallas_call(merge_kernel, out_shape=jax.ShapeDtypeStruct((ROWS // MERG...  2.97 us
    pallas_call x1, Pallas kernels, on_device(): pl.pallas_call(gather_kernel, out_shape=[jax.ShapeDtypeStruct((D, 3 * HAL...  2.16 us
  transfers between devices with their start and end apart: 12, of which 4 were waited for; matrix products, arithmetic and copies ran while one was open for 7% of the time, Pallas kernels for 7%

profile of v5, /device:TPU:1, one launch (start us, length us, event | category | flops | bytes accessed | tf_op | source)
XLA Modules:
  0.0 105.2 jit_solution(15539846200640922204)
XLA Ops:
  0.0 1.1 %dynamic-slice_bitcast_fusion.1 = (bf16[160,640]{1,0:T(8,128)(2,1)S(1)}, bf16[160,640]{1,0:T(8,128)(2,1)S(1)}) fusion(bf16[1280,160]{0,1:T(8,128)(2,1)} %param.13, s32[]{:T(128)S(6)} %select_n.182, s32[]{:T(128)S(6)} %select_n.186), kind=kLoop, calls=%fused_computation.4 | loop fusion | bytes 819208 | tf_op jit(solution)/shard_map/dynamic_slice | solution.py:226
  1.1 1.5 %constant_dynamic-slice_fusion.5 = (bf16[160,640]{1,0:T(8,128)(2,1)S(1)}, bf16[160,640]{1,0:T(8,128)(2,1)S(1)}, bf16[160,640]{1,0:T(8,128)(2,1)S(1)}, bf16[160,6...) fusion(bf16[160,3840]{1,0:T(8,128)(2,1)} %param.11, s32[]{:T(128)S(6)} %select_n.179, ...), kind=kLoop, calls=%fused_computation.30 | loop fusion | bytes 2457624 | tf_op jit(solution)/shard_map/dynamic_slice | solution.py:225
  2.6 0.0 copy-start.7
  2.6 0.0 copy-start.6
  2.6 9.8 %maximum_maximum_fusion.own = bf16[320,2560]{1,0:T(8,128)(2,1)S(1)} fusion(bf16[160,640]{1,0:T(8,128)(2,1)S(1)} %get-tuple-element.35, bf16[160,640]{1,0:T(8,128)(2,1)S(1)} %get-tuple-element.29, bf16[160,640]{1,0:T(8,128)(2,1)S(1)} %get-tuple-element.30, bf16[160,640]{1,0:T(8,128)(2,1)S(1)} %get-tuple-element.26, bf16[160,640]{1,0:T(8,128)(2,1)S(1)} %get-tuple-element.34, ...), kind=kLoop, calls=%fused_computation | loop fusion | flops 13107200 | bytes 3276800 | tf_op jit(solution)/shard_map/concatenate | solution.py:230
  12.4 5.5 %collective-permute-start.1 = (bf16[320,2560]{1,0:T(8,128)(2,1)S(1)}, bf16[320,2560]{1,0:T(8,128)(2,1)S(1)}, u32[]{:S(2)}, u32[]{:S(2)}) collective-permute-start(bf16[320,2560]{1,0:T(8,128)(2,1)S(1)} %maximum_maximum_fusion.own), channel_id=1, source_target_pairs={{0,257},{8,12},{16,273},{24,28},{32,289},{40,44},{48,305},{56,60},... | collective-permute-start | bytes 4915208 | tf_op jit(solution)/shard_map/ppermute | solution.py:57
  17.9 2.8 %collective-permute-start = (bf16[320,2560]{1,0:T(8,128)(2,1)S(1)}, bf16[320,2560]{1,0:T(8,128)(2,1)}, u32[]{:S(2)}, u32[]{:S(2)}) collective-permute-start(bf16[320,2560]{1,0:T(8,128)(2,1)S(1)} %maximum_maximum_fusion.own), channel_id=1, source_target_pairs={{0,2},{8,14},{16,18},{24,30},{32,34},{40,46},{48,50},{56,62},{64,6... | collective-permute-start | bytes 4915208 | tf_op jit(solution)/shard_map/ppermute | solution.py:57
  20.7 27.3 %collective-permute-done.1.b = bf16[320,2560]{1,0:T(8,128)(2,1)S(1)} collective-permute-done((bf16[320,2560]{1,0:T(8,128)(2,1)S(1)}, bf16[320,2560]{1,0:T(8,128)(2,1)S(1)}, u32[]{:S(2)}, u32[]{:S(2)}) %collective-permute-start.1) | collective-permute-done | bytes 1638432 | tf_op jit(solution)/shard_map/ppermute | solution.py:57
  48.0 6.8 %collective-permute-start.6 = (bf16[320,2560]{1,0:T(8,128)(2,1)S(1)}, bf16[320,2560]{1,0:T(8,128)(2,1)}, u32[]{:S(2)}, u32[]{:S(2)}) collective-permute-start(bf16[320,2560]{1,0:T(8,128)(2,1)S(1)} %collective-permute-done.1.b), channel_id=1, source_target_pairs={{0,2},{8,265},{16,18},{24,281},{32,34},{40,297},{48,50},{56,313},{... | collective-permute-start | bytes 4915208 | tf_op jit(solution)/shard_map/ppermute | solution.py:57
  54.8 1.9 %collective-permute-start.7 = (bf16[320,2560]{1,0:T(8,128)(2,1)S(1)}, bf16[320,2560]{1,0:T(8,128)(2,1)}, u32[]{:S(2)}, u32[]{:S(2)}) collective-permute-start(bf16[320,2560]{1,0:T(8,128)(2,1)S(1)} %collective-permute-done.1.b), channel_id=1, source_target_pairs={{0,6},{16,22},{32,38},{48,54},{64,70},{80,86},{96,102},{112,118},{... | collective-permute-start | bytes 4915208 | tf_op jit(solution)/shard_map/ppermute | solution.py:57
  56.6 1.8 %slice_bitcast_fusion = (bf16[64,1280]{1,0:T(8,128)(2,1)}, bf16[64,1280]{1,0:T(8,128)(2,1)}, bf16[64,1280]{1,0:T(8,128)(2,1)}) fusion(bf16[1,1,7,64,1280]{4,3,2,1,0:T(8,128)(2,1)} %own.1), kind=kLoop, calls=%fused_computation.5 | loop fusion | bytes 983040 | tf_op jit(solution)/shard_map/squeeze | solution.py:241
  58.5 1.9 %collective-permute-start.2 = (bf16[64,1280]{1,0:T(8,128)(2,1)}, bf16[64,1280]{1,0:T(8,128)(2,1)S(1)}, u32[]{:S(2)}, u32[]{:S(2)}) collective-permute-start(bf16[64,1280]{1,0:T(8,128)(2,1)} %get-tuple-element.33), channel_id=1, source_target_pairs={{0,8},{8,16},{16,24},{24,32},{32,40},{40,48},{48,56},{56,64},{64,7... | collective-permute-start | bytes 491528 | tf_op jit(solution)/shard_map/ppermute | solution.py:62
  60.4 5.1 %collective-permute-start.3 = (bf16[64,1280]{1,0:T(8,128)(2,1)}, bf16[64,1280]{1,0:T(8,128)(2,1)}, u32[]{:S(2)}, u32[]{:S(2)}) collective-permute-start(bf16[64,1280]{1,0:T(8,128)(2,1)} %get-tuple-element.32), channel_id=1, source_target_pairs={{0,16},{8,24},{16,32},{24,40},{32,48},{40,56},{48,64},{56,72},{64,... | collective-permute-start | bytes 491528 | tf_op jit(solution)/shard_map/ppermute | solution.py:62
  65.6 0.1 stack.59
  65.7 0.1 stack.58
  65.8 0.0 copy-done.7
  65.8 0.1 pad_add_fusion
  65.9 0.1 fusion.2
  65.9 0.3 select_reduce_fusion.1
  66.2 0.1 copy.13
  66.3 0.0 copy-done.6
  66.3 0.3 select_reduce_fusion
  66.7 0.2 fusion
  66.9 0.1 slice.51
  66.9 0.0 collective-permute-done.a
  66.9 0.3 copy-done.1
  67.2 5.6 %collective-permute-start.4 = (bf16[64,1280]{1,0:T(8,128)(2,1)S(1)}, bf16[64,1280]{1,0:T(8,128)(2,1)S(1)}, u32[]{:S(2)}, u32[]{:S(2)}) collective-permute-start(bf16[64,1280]{1,0:T(8,128)(2,1)S(1)} %copy-done.1), channel_id=1, source_target_pairs={{0,24},{8,32},{16,40},{24,48},{32,56},{40,64},{48,72},{56,80},{64,... | collective-permute-start | bytes 491528 | tf_op jit(solution)/shard_map/ppermute | solution.py:62
  72.8 1.2 %slice.50 = bf16[160,2560]{1,0:T(8,128)(2,1)S(1)} slice(bf16[320,2560]{1,0:T(8,128)(2,1)} %collective-permute-done.a), slice={[160:320], [0:2560]} | slice | bytes 1638400 | tf_op jit(solution)/shard_map/slice | solution.py:235
  74.0 0.1 pad_maximum_fusion
  74.1 0.0 collective-permute-done.2.in0
  74.1 1.9 %collective-permute-start.8 = (bf16[320,2560]{1,0:T(8,128)(2,1)S(1)}, bf16[320,2560]{1,0:T(8,128)(2,1)S(1)}, u32[]{:S(2)}, u32[]{:S(2)}) collective-permute-start(bf16[320,2560]{1,0:T(8,128)(2,1)S(1)} %pad_maximum_fusion), channel_id=1, source_target_pairs={{0,8},{8,0},{16,24},{24,16},{32,40},{40,32},{48,56},{56,48},{64,72... | collective-permute-start | bytes 4915208 | tf_op jit(solution)/shard_map/ppermute | solution.py:57
  76.1 0.0 collective-permute-done.6.c
  76.1 1.2 %slice.52 = bf16[160,2560]{1,0:T(8,128)(2,1)S(1)} slice(bf16[320,2560]{1,0:T(8,128)(2,1)} %collective-permute-done.6.c), slice={[160:320], [0:2560]} | slice | bytes 1638400 | tf_op jit(solution)/shard_map/slice | solution.py:235
  77.3 0.0 collective-permute-done.7.d
  77.3 1.2 %slice.53 = bf16[160,2560]{1,0:T(8,128)(2,1)S(1)} slice(bf16[320,2560]{1,0:T(8,128)(2,1)} %collective-permute-done.7.d), slice={[160:320], [0:2560]} | slice | bytes 1638400 | tf_op jit(solution)/shard_map/slice | solution.py:235
  78.5 0.0 copy-start.3
  78.5 0.0 copy-start
  78.5 0.1 pad_maximum_fusion.1
  78.6 2.5 %collective-permute-start.9 = (bf16[320,2560]{1,0:T(8,128)(2,1)S(1)}, bf16[320,2560]{1,0:T(8,128)(2,1)S(1)}, u32[]{:S(2)}, u32[]{:S(2)}) collective-permute-start(bf16[320,2560]{1,0:T(8,128)(2,1)S(1)} %pad_maximum_fusion.1), channel_id=1, source_target_pairs={{0,8},{8,0},{16,24},{24,16},{32,40},{40,32},{48,56},{56,48},{64,72... | collective-permute-start | bytes 4915208 | tf_op jit(solution)/shard_map/ppermute | solution.py:57
  81.2 0.2 slice_reduce_fusion
  81.4 0.2 select_reduce_fusion.3
  81.6 0.0 copy-done.3
  81.6 0.1 pad_add_fusion.1.meta
  81.7 0.0 collective-permute-done.3.in1
  81.7 0.7 collective-permute-done.4.in2
  82.3 0.0 copy-done
  82.3 2.0 %shard_map.91 = (bf16[256,1280]{1,0:T(8,128)(2,1)S(1)}, bf16[256,1280]{1,0:T(8,128)(2,1)S(1)}) custom-call(s32[20]{0:T(128)S(1)} %pad_add_fusion.1.meta, bf16[1,1,7,64,1280]{4,3,2,1,0:T(8,128)(2,1)S(1)} %copy-done, bf16[64,1280]{1,0:T(8,128)(2,1)S(1)} %collective-permute-done.2.in0, bf16[64,1280]{1,0:T(8,128)(2,1)} %collective-permute-done.3.in1, ...), custom_call_target="tpu_custom_call" | custom-call | tf_op jit(solution)/shard_map/pallas_call | solution.py:249
  84.4 0.0 copy-start.2
  84.4 2.3 %collective-permute-start.5 = (bf16[256,1280]{1,0:T(8,128)(2,1)S(1)}, bf16[256,1280]{1,0:T(8,128)(2,1)S(1)}, u32[]{:S(2)}, u32[]{:S(2)}) collective-permute-start(bf16[256,1280]{1,0:T(8,128)(2,1)S(1)} %get-tuple-element.14.xa), channel_id=1, source_target_pairs={{0,8},{8,0},{16,24},{24,16},{32,40},{40,32},{48,56},{56,48},{64,72... | collective-permute-start | bytes 1966088 | tf_op jit(solution)/shard_map/ppermute | solution.py:57
  86.7 1.7 %collective-permute-done.5._.xb = bf16[256,1280]{1,0:T(8,128)(2,1)S(1)} collective-permute-done((bf16[256,1280]{1,0:T(8,128)(2,1)S(1)}, bf16[256,1280]{1,0:T(8,128)(2,1)S(1)}, u32[]{:S(2)}, u32[]{:S(2)}) %collective-permute-start.5) | collective-permute-done | bytes 655392 | tf_op jit(solution)/shard_map/ppermute | solution.py:57
  88.4 0.0 collective-permute-done.8.early
  88.4 0.0 collective-permute-done.9.late
  88.4 2.2 %shard_map.92 = (bf16[1280,1920]{1,0:T(8,128)(2,1)S(1)}, bf16[1280,640]{1,0:T(8,128)(2,1)S(1)}) custom-call(s32[20]{0:T(128)S(1)} %pad_add_fusion.1.meta, bf16[320,2560]{1,0:T(8,128)(2,1)S(1)} %maximum_maximum_fusion.own, bf16[320,2560]{1,0:T(8,128)(2,1)} %collective-permute-done.a, bf16[320,2560]{1,0:T(8,128)(2,1)S(1)} %collective-permute-done.1.b, ...), custom_call_target="tpu_custom_call" | custom-call | tf_op jit(solution)/shard_map/pallas_call | solution.py:259
  90.6 2.7 %collective-permute-start.11 = (bf16[1280,640]{1,0:T(8,128)(2,1)S(1)}, bf16[1280,640]{1,0:T(8,128)(2,1)S(1)}, u32[]{:S(2)}, u32[]{:S(2)}) collective-permute-start(bf16[1280,640]{1,0:T(8,128)(2,1)S(1)} %get-tuple-element.19.wa), channel_id=1, source_target_pairs={{0,8},{8,0},{16,24},{24,16},{32,40},{40,32},{48,56},{56,48},{64,72... | collective-permute-start | bytes 4915208 | tf_op jit(solution)/shard_map/ppermute | solution.py:57
  93.3 0.0 copy-done.2
  93.3 0.1 fusion.4
  93.4 0.0 copy-start.4
  93.4 0.0 copy-start.5
  93.5 5.3 %shard_map.93 = (bf16[256,640]{1,0:T(8,128)(2,1)S(1)}, bf16[256,640]{1,0:T(8,128)(2,1)S(1)}) custom-call(s32[20]{0:T(128)S(1)} %pad_add_fusion.1.meta, bf16[256,1280]{1,0:T(8,128)(2,1)S(1)} %get-tuple-element.14.xa, bf16[256,1280]{1,0:T(8,128)(2,1)S(1)} %collective-permute-done.5._.xb, f32[1,1920]{1,0:T(1,128)S(1)} %reshape.81.bias, ...), custom_call_target="tpu_custom_call" | custom-call | tf_op jit(solution)/shard_map/pallas_call | solution.py:272
  98.7 1.9 %collective-permute-start.10 = (bf16[256,640]{1,0:T(8,128)(2,1)S(1)}, bf16[256,640]{1,0:T(8,128)(2,1)S(1)}, u32[]{:S(2)}, u32[]{:S(2)}) collective-permute-start(bf16[256,640]{1,0:T(8,128)(2,1)S(1)} %get-tuple-element.18), channel_id=1, source_target_pairs={{0,8},{8,0},{16,24},{24,16},{32,40},{40,32},{48,56},{56,48},{64,72... | collective-permute-start | bytes 983048 | tf_op jit(solution)/shard_map/ppermute | solution.py:57
  100.7 0.0 copy-done.4
  100.7 1.5 %collective-permute-done.10.attb = bf16[256,640]{1,0:T(8,128)(2,1)S(1)} collective-permute-done((bf16[256,640]{1,0:T(8,128)(2,1)S(1)}, bf16[256,640]{1,0:T(8,128)(2,1)S(1)}, u32[]{:S(2)}, u32[]{:S(2)}) %collective-permute-start.10) | collective-permute-done | bytes 327712 | tf_op jit(solution)/shard_map/ppermute | solution.py:57
  102.2 0.0 collective-permute-done.11.wb
  102.2 3.0 %shard_map.94 = bf16[64,5120]{1,0:T(8,128)(2,1)} custom-call(s32[20]{0:T(128)S(1)} %pad_add_fusion.1.meta, bf16[256,640]{1,0:T(8,128)(2,1)S(1)} %get-tuple-element.17.atta, bf16[256,640]{1,0:T(8,128)(2,1)S(1)} %collective-permute-done.10.attb, bf16[1280,640]{1,0:T(8,128)(2,1)S(1)} %get-tuple-element.19.wa, bf16[1280,640]{1,0:T(8,128)(2,1)S(1)} %collective-permute-done.11.wb, ...), custom_call_target="tpu_custom_call" | custom-call | tf_op jit(solution)/shard_map/pallas_call | solution.py:282
  (13 shorter events, 0.1 us)
Async XLA Ops:
  2.6 63.2 %copy-start.7 = (s32[64,1,7]{0,1,2:T(1,128)S(1)}, s32[64,1,7]{0,1,2:T(1,128)}, u32[]{:S(2)}) copy-start(s32[64,1,7]{0,1,2:T(1,128)} %param.16) | copy-start | bytes 5380
  2.6 63.8 %copy-start.6 = (s32[64,1,7,2]{0,3,2,1:T(2,128)S(1)}, s32[64,1,7,2]{0,3,2,1:T(2,128)}, u32[]{:S(2)}) copy-start(s32[64,1,7,2]{0,3,2,1:T(2,128)} %param.17) | copy-start | bytes 10756
  12.4 35.6 %collective-permute-start.1 = (bf16[320,2560]{1,0:T(8,128)(2,1)S(1)}, bf16[320,2560]{1,0:T(8,128)(2,1)S(1)}, u32[]{:S(2)}, u32[]{:S(2)}) collective-permute-start(bf16[320,2560]{1,0:T(8,128)(2,1)S(1)} %maximum_maximum_fusion.own), channel_id=1, source_target_pairs={{0,257},{8,12},{16,273},{24,28},{32,289},{40,44},{48,305},{56,60},... | collective-permute-start | bytes 4915208 | tf_op jit(solution)/shard_map/ppermute | solution.py:57
  17.9 49.1 %collective-permute-start = (bf16[320,2560]{1,0:T(8,128)(2,1)S(1)}, bf16[320,2560]{1,0:T(8,128)(2,1)}, u32[]{:S(2)}, u32[]{:S(2)}) collective-permute-start(bf16[320,2560]{1,0:T(8,128)(2,1)S(1)} %maximum_maximum_fusion.own), channel_id=1, source_target_pairs={{0,2},{8,14},{16,18},{24,30},{32,34},{40,46},{48,50},{56,62},{64,6... | collective-permute-start | bytes 4915208 | tf_op jit(solution)/shard_map/ppermute | solution.py:57
  48.0 28.1 %collective-permute-start.6 = (bf16[320,2560]{1,0:T(8,128)(2,1)S(1)}, bf16[320,2560]{1,0:T(8,128)(2,1)}, u32[]{:S(2)}, u32[]{:S(2)}) collective-permute-start(bf16[320,2560]{1,0:T(8,128)(2,1)S(1)} %collective-permute-done.1.b), channel_id=1, source_target_pairs={{0,2},{8,265},{16,18},{24,281},{32,34},{40,297},{48,50},{56,313},{... | collective-permute-start | bytes 4915208 | tf_op jit(solution)/shard_map/ppermute | solution.py:57
  54.8 22.5 %collective-permute-start.7 = (bf16[320,2560]{1,0:T(8,128)(2,1)S(1)}, bf16[320,2560]{1,0:T(8,128)(2,1)}, u32[]{:S(2)}, u32[]{:S(2)}) collective-permute-start(bf16[320,2560]{1,0:T(8,128)(2,1)S(1)} %collective-permute-done.1.b), channel_id=1, source_target_pairs={{0,6},{16,22},{32,38},{48,54},{64,70},{80,86},{96,102},{112,118},{... | collective-permute-start | bytes 4915208 | tf_op jit(solution)/shard_map/ppermute | solution.py:57
  58.5 15.7 %collective-permute-start.2 = (bf16[64,1280]{1,0:T(8,128)(2,1)}, bf16[64,1280]{1,0:T(8,128)(2,1)S(1)}, u32[]{:S(2)}, u32[]{:S(2)}) collective-permute-start(bf16[64,1280]{1,0:T(8,128)(2,1)} %get-tuple-element.33), channel_id=1, source_target_pairs={{0,8},{8,16},{16,24},{24,32},{32,40},{40,48},{48,56},{56,64},{64,7... | collective-permute-start | bytes 491528 | tf_op jit(solution)/shard_map/ppermute | solution.py:62
  60.4 21.3 %collective-permute-start.3 = (bf16[64,1280]{1,0:T(8,128)(2,1)}, bf16[64,1280]{1,0:T(8,128)(2,1)}, u32[]{:S(2)}, u32[]{:S(2)}) collective-permute-start(bf16[64,1280]{1,0:T(8,128)(2,1)} %get-tuple-element.32), channel_id=1, source_target_pairs={{0,16},{8,24},{16,32},{24,40},{32,48},{40,56},{48,64},{56,72},{64,... | collective-permute-start | bytes 491528 | tf_op jit(solution)/shard_map/ppermute | solution.py:62
  66.3 0.9 copy-start.1
  67.2 15.1 %collective-permute-start.4 = (bf16[64,1280]{1,0:T(8,128)(2,1)S(1)}, bf16[64,1280]{1,0:T(8,128)(2,1)S(1)}, u32[]{:S(2)}, u32[]{:S(2)}) collective-permute-start(bf16[64,1280]{1,0:T(8,128)(2,1)S(1)} %copy-done.1), channel_id=1, source_target_pairs={{0,24},{8,32},{16,40},{24,48},{32,56},{40,64},{48,72},{56,80},{64,... | collective-permute-start | bytes 491528 | tf_op jit(solution)/shard_map/ppermute | solution.py:62
  74.1 14.3 %collective-permute-start.8 = (bf16[320,2560]{1,0:T(8,128)(2,1)S(1)}, bf16[320,2560]{1,0:T(8,128)(2,1)S(1)}, u32[]{:S(2)}, u32[]{:S(2)}) collective-permute-start(bf16[320,2560]{1,0:T(8,128)(2,1)S(1)} %pad_maximum_fusion), channel_id=1, source_target_pairs={{0,8},{8,0},{16,24},{24,16},{32,40},{40,32},{48,56},{56,48},{64,72... | collective-permute-start | bytes 4915208 | tf_op jit(solution)/shard_map/ppermute | solution.py:57
  78.5 3.1 %copy-start.3 = (f32[1280]{0:T(1024)S(1)}, f32[1280]{0:T(1024)}, u32[]{:S(2)}) copy-start(f32[1280]{0:T(1024)} %param.10) | copy-start | bytes 15364
  78.5 3.8 %copy-start = (bf16[1,1,7,64,1280]{4,3,2,1,0:T(8,128)(2,1)S(1)}, bf16[1,1,7,64,1280]{4,3,2,1,0:T(8,128)(2,1)}, u32[]{:S(2)}) copy-start(bf16[1,1,7,64,1280]{4,3,2,1,0:T(8,128)(2,1)} %own.1) | copy-start | bytes 3440644
  78.6 9.8 %collective-permute-start.9 = (bf16[320,2560]{1,0:T(8,128)(2,1)S(1)}, bf16[320,2560]{1,0:T(8,128)(2,1)S(1)}, u32[]{:S(2)}, u32[]{:S(2)}) collective-permute-start(bf16[320,2560]{1,0:T(8,128)(2,1)S(1)} %pad_maximum_fusion.1), channel_id=1, source_target_pairs={{0,8},{8,0},{16,24},{24,16},{32,40},{40,32},{48,56},{56,48},{64,72... | collective-permute-start | bytes 4915208 | tf_op jit(solution)/shard_map/ppermute | solution.py:57
  84.4 8.9 %copy-start.2 = (f32[3840]{0:T(1024)S(1)}, f32[3840]{0:T(1024)}, u32[]{:S(2)}) copy-start(f32[3840]{0:T(1024)} %param.12) | copy-start | bytes 46084
  84.4 4.0 %collective-permute-start.5 = (bf16[256,1280]{1,0:T(8,128)(2,1)S(1)}, bf16[256,1280]{1,0:T(8,128)(2,1)S(1)}, u32[]{:S(2)}, u32[]{:S(2)}) collective-permute-start(bf16[256,1280]{1,0:T(8,128)(2,1)S(1)} %get-tuple-element.14.xa), channel_id=1, source_target_pairs={{0,8},{8,0},{16,24},{24,16},{32,40},{40,32},{48,56},{56,48},{64,72... | collective-permute-start | bytes 1966088 | tf_op jit(solution)/shard_map/ppermute | solution.py:57
  90.6 11.7 %collective-permute-start.11 = (bf16[1280,640]{1,0:T(8,128)(2,1)S(1)}, bf16[1280,640]{1,0:T(8,128)(2,1)S(1)}, u32[]{:S(2)}, u32[]{:S(2)}) collective-permute-start(bf16[1280,640]{1,0:T(8,128)(2,1)S(1)} %get-tuple-element.19.wa), channel_id=1, source_target_pairs={{0,8},{8,0},{16,24},{24,16},{32,40},{40,32},{48,56},{56,48},{64,72... | collective-permute-start | bytes 4915208 | tf_op jit(solution)/shard_map/ppermute | solution.py:57
  93.4 7.2 %copy-start.4 = (f32[1280]{0:T(1024)S(1)}, f32[1280]{0:T(1024)}, u32[]{:S(2)}) copy-start(f32[1280]{0:T(1024)} %param.14) | copy-start | bytes 15364
  93.4 7.2 %copy-start.5 = (f32[1280]{0:T(1024)S(1)}, f32[1280]{0:T(1024)}, u32[]{:S(2)}) copy-start(f32[1280]{0:T(1024)} %param.15) | copy-start | bytes 15364
  98.7 3.5 %collective-permute-start.10 = (bf16[256,640]{1,0:T(8,128)(2,1)S(1)}, bf16[256,640]{1,0:T(8,128)(2,1)S(1)}, u32[]{:S(2)}, u32[]{:S(2)}) collective-permute-start(bf16[256,640]{1,0:T(8,128)(2,1)S(1)} %get-tuple-element.18), channel_id=1, source_target_pairs={{0,8},{8,0},{16,24},{24,16},{32,40},{40,32},{48,56},{56,48},{64,72... | collective-permute-start | bytes 983048 | tf_op jit(solution)/shard_map/ppermute | solution.py:57

commit v6 on v5

--- a/solution.py
+++ b/solution.py
@@ -227,7 +227,9 @@
             axis=1,
         )
 
-    piece = jnp.concatenate([columns(half), columns(HALF - half)], axis=0)
+    piece = jnp.concatenate(
+        lax.optimization_barrier([columns(half), columns(HALF - half)]), axis=0
+    )
     bias = jnp.concatenate(
         [lax.dynamic_slice_in_dim(b_qkv, j * D + half, HALF, 0) for j in range(3)]
     )
@@ -236,12 +238,11 @@
 
     got_b = send(piece, moves((0, 1), (2, 0)))
     got_a = send(piece, moves((1, 0), (-1, 0)))
+    moved = [by_rank(patches[0, 0, RECV + m], m + 1) for m in range(SLOTS - RECV)]
+    got_b, *moved = lax.optimization_barrier((got_b, *moved))
     got_c = send(got_b, moves((1, 0), (0, 1)))
     got_d = send(got_b, moves((-1, 0)))
-    moved = [by_rank(patches[0, 0, RECV + m], m + 1) for m in range(SLOTS - RECV)]
-    early, moved[0] = lax.optimization_barrier((halves_of(got_a, got_b), moved[0]))
-    early = send(early, other_core())
-    late = send(halves_of(got_c, got_d), other_core())
+    early = send(halves_of(got_a, got_b), other_core())
 
 
     meta = tables(route, groups, rank, lane // NYH, lane % NYH)
@@ -255,6 +256,8 @@
         compiler_params=SMALL,
     )(meta, patches, *moved, norm_gain.reshape(1, D))
     normed_other = send(normed, other_core())
+    late, normed_other = lax.optimization_barrier((halves_of(got_c, got_d), normed_other))
+    late = send(late, other_core())
 
     w, w_mine = pl.pallas_call(
         gather_kernel,

time: 106 us -> 92.2 us (0.87)
  the two profiles are of different devices: /device:TPU:1 before, /device:TPU:485 now
where the time goes in v6:
time: 92.2 us; the launch traced here: 91.5 us
  waiting for transfers between devices  36 us (39%)
  starting transfers between devices  31.5 us (34%)
  Pallas kernels  12.3 us (13%)
  local copies, waits for them, and re-layouts  9.64 us (10%)
  other arithmetic  1.6 us (2%)
    ppermute x9, starting transfers between devices, send(): return lax.ppermute(value, AXES, pairs)  25.7 us
    ppermute x9, waiting for transfers between devices, send(): return lax.ppermute(value, AXES, pairs)  24.4 us
    ppermute x3, waiting for transfers between devices, by_rank(): lax.ppermute(value, 'dp', [(i, (i + by) % devices) for i in range(devices)])  11.6 us
    ppermute x3, starting transfers between devices, by_rank(): lax.ppermute(value, 'dp', [(i, (i + by) % devices) for i in range(devices)])  5.75 us
    pallas_call x1, Pallas kernels, on_device(): pl.pallas_call(attend_kernel, out_shape=[jax.ShapeDtypeStruct((ROWS, HALF...  5.27 us
    pallas_call x1, Pallas kernels, on_device(): pl.pallas_call(merge_kernel, out_shape=jax.ShapeDtypeStruct((ROWS // MERG...  2.97 us
    slice x4, local copies, waits for them, and re-layouts, halves_of(): return jnp.concatenate([value[DEPTH:] for value in shards], axis=0)  2.51 us
    pallas_call x1, Pallas kernels, on_device(): pl.pallas_call(gather_kernel, out_shape=[jax.ShapeDtypeStruct((D, 3 * HAL...  2.1 us
  transfers between devices with their start and end apart: 12, of which 6 were waited for; matrix products, arithmetic and copies ran while one was open for 7% of the time, Pallas kernels for 8%

profile of v6, /device:TPU:485, one launch (start us, length us, event | category | flops | bytes accessed | tf_op | source)
XLA Modules:
  0.0 91.5 jit_solution(9817682171195919688)
XLA Ops:
  0.0 1.1 %dynamic-slice_bitcast_fusion = (bf16[160,640]{1,0:T(8,128)(2,1)S(1)}, bf16[160,640]{1,0:T(8,128)(2,1)S(1)}) fusion(bf16[1280,160]{0,1:T(8,128)(2,1)} %param.13, s32[]{:T(128)S(6)} %select_n.186, s32[]{:T(128)S(6)} %select_n.182), kind=kLoop, calls=%fused_computation.4 | loop fusion | bytes 819208 | tf_op jit(solution)/shard_map/dynamic_slice | solution.py:226
  1.1 1.5 %constant_dynamic-slice_fusion.2 = (bf16[160,640]{1,0:T(8,128)(2,1)S(1)}, bf16[160,640]{1,0:T(8,128)(2,1)S(1)}, bf16[160,640]{1,0:T(8,128)(2,1)S(1)}, bf16[160,6...) fusion(bf16[160,3840]{1,0:T(8,128)(2,1)} %param.11, s32[]{:T(128)S(6)} %select_n.183, ...), kind=kLoop, calls=%fused_computation.30 | loop fusion | bytes 2457624 | tf_op jit(solution)/shard_map/dynamic_slice | solution.py:225
  2.6 0.2 pad_maximum_fusion.2
  2.7 1.0 %constant_dynamic-update-slice_fusion.1 = bf16[320,2560]{1,0:T(8,128)(2,1)} fusion(bf16[160,2560]{1,0:T(8,128)(2,1)S(1)} %get-tuple-element.19), kind=kLoop, calls=%fused_computation.17 | loop fusion | bytes 1638400
  3.7 0.0 copy-start.6
  3.7 0.0 copy-start.2
  3.7 1.0 %constant_dynamic-update-slice_fusion.own = bf16[320,2560]{1,0:T(8,128)(2,1)} fusion(bf16[320,2560]{1,0:T(8,128)(2,1)} %constant_dynamic-update-slice_fusion.1, bf16[160,2560]{1,0:T(8,128)(2,1)S(1)} %get-tuple-element.20), kind=kLoop, calls=%fused_computation.16 | loop fusion | bytes 1638400 | tf_op jit(solution)/shard_map/concatenate | solution.py:230
  4.7 2.1 %collective-permute-start = (bf16[320,2560]{1,0:T(8,128)(2,1)}, bf16[320,2560]{1,0:T(8,128)(2,1)S(1)}, u32[]{:S(2)}, u32[]{:S(2)}) collective-permute-start(bf16[320,2560]{1,0:T(8,128)(2,1)} %constant_dynamic-update-slice_fusion.own), channel_id=1, source_target_pairs={{0,257},{8,12},{16,273},{24,28},{32,289},{40,44},{48,305},{56,60},... | collective-permute-start | bytes 4915208 | tf_op jit(solution)/shard_map/ppermute | solution.py:57
  6.8 3.8 %collective-permute-start.7 = (bf16[320,2560]{1,0:T(8,128)(2,1)}, bf16[320,2560]{1,0:T(8,128)(2,1)S(1)}, u32[]{:S(2)}, u32[]{:S(2)}) collective-permute-start(bf16[320,2560]{1,0:T(8,128)(2,1)} %constant_dynamic-update-slice_fusion.own), channel_id=1, source_target_pairs={{0,2},{8,14},{16,18},{24,30},{32,34},{40,46},{48,50},{56,62},{64,6... | collective-permute-start | bytes 4915208 | tf_op jit(solution)/shard_map/ppermute | solution.py:57
  10.6 1.9 %slice_bitcast_fusion = (bf16[64,1280]{1,0:T(8,128)(2,1)}, bf16[64,1280]{1,0:T(8,128)(2,1)}, bf16[64,1280]{1,0:T(8,128)(2,1)}) fusion(bf16[1,1,7,64,1280]{4,3,2,1,0:T(8,128)(2,1)} %own.1), kind=kLoop, calls=%fused_computation.6 | loop fusion | bytes 983040 | tf_op jit(solution)/shard_map/squeeze | solution.py:241
  12.4 1.9 %collective-permute-start.1 = (bf16[64,1280]{1,0:T(8,128)(2,1)}, bf16[64,1280]{1,0:T(8,128)(2,1)S(1)}, u32[]{:S(2)}, u32[]{:S(2)}) collective-permute-start(bf16[64,1280]{1,0:T(8,128)(2,1)} %get-tuple-element.45), channel_id=1, source_target_pairs={{0,8},{8,16},{16,24},{24,32},{32,40},{40,48},{48,56},{56,64},{64,7... | collective-permute-start | bytes 491528 | tf_op jit(solution)/shard_map/ppermute | solution.py:62
  14.4 1.9 %collective-permute-start.2 = (bf16[64,1280]{1,0:T(8,128)(2,1)}, bf16[64,1280]{1,0:T(8,128)(2,1)}, u32[]{:S(2)}, u32[]{:S(2)}) collective-permute-start(bf16[64,1280]{1,0:T(8,128)(2,1)} %get-tuple-element.44), channel_id=1, source_target_pairs={{0,16},{8,24},{16,32},{24,40},{32,48},{40,56},{48,64},{56,72},{64,... | collective-permute-start | bytes 491528 | tf_op jit(solution)/shard_map/ppermute | solution.py:62
  16.3 1.9 %collective-permute-start.3 = (bf16[64,1280]{1,0:T(8,128)(2,1)}, bf16[64,1280]{1,0:T(8,128)(2,1)}, u32[]{:S(2)}, u32[]{:S(2)}) collective-permute-start(bf16[64,1280]{1,0:T(8,128)(2,1)} %get-tuple-element.43), channel_id=1, source_target_pairs={{0,24},{8,32},{16,40},{24,48},{32,56},{40,64},{48,72},{56,80},{64,... | collective-permute-start | bytes 491528 | tf_op jit(solution)/shard_map/ppermute | solution.py:62
  18.2 0.0 copy-done.6
  18.2 0.1 pad_add_fusion
  18.3 0.1 fusion.2
  18.4 0.0 collective-permute-done.1.in0
  18.4 6.5 %collective-permute-done.2.in1 = bf16[64,1280]{1,0:T(8,128)(2,1)} collective-permute-done((bf16[64,1280]{1,0:T(8,128)(2,1)}, bf16[64,1280]{1,0:T(8,128)(2,1)}, u32[]{:S(2)}, u32[]{:S(2)}) %collective-permute-start.2) | collective-permute-done | bytes 163872 | tf_op jit(solution)/shard_map/ppermute | solution.py:62
  24.9 5.1 %collective-permute-done.3.in2 = bf16[64,1280]{1,0:T(8,128)(2,1)} collective-permute-done((bf16[64,1280]{1,0:T(8,128)(2,1)}, bf16[64,1280]{1,0:T(8,128)(2,1)}, u32[]{:S(2)}, u32[]{:S(2)}) %collective-permute-start.3) | collective-permute-done | bytes 163872 | tf_op jit(solution)/shard_map/ppermute | solution.py:62
  30.0 11.1 %collective-permute-done.b = bf16[320,2560]{1,0:T(8,128)(2,1)S(1)} collective-permute-done((bf16[320,2560]{1,0:T(8,128)(2,1)}, bf16[320,2560]{1,0:T(8,128)(2,1)S(1)}, u32[]{:S(2)}, u32[]{:S(2)}) %collective-permute-start) | collective-permute-done | bytes 1638432 | tf_op jit(solution)/shard_map/ppermute | solution.py:57
  41.2 7.4 %collective-permute-start.4 = (bf16[320,2560]{1,0:T(8,128)(2,1)S(1)}, bf16[320,2560]{1,0:T(8,128)(2,1)}, u32[]{:S(2)}, u32[]{:S(2)}) collective-permute-start(bf16[320,2560]{1,0:T(8,128)(2,1)S(1)} %collective-permute-done.b), channel_id=1, source_target_pairs={{0,2},{8,265},{16,18},{24,281},{32,34},{40,297},{48,50},{56,313},{... | collective-permute-start | bytes 4915208 | tf_op jit(solution)/shard_map/ppermute | solution.py:57
  48.6 1.8 %collective-permute-start.5 = (bf16[320,2560]{1,0:T(8,128)(2,1)S(1)}, bf16[320,2560]{1,0:T(8,128)(2,1)}, u32[]{:S(2)}, u32[]{:S(2)}) collective-permute-start(bf16[320,2560]{1,0:T(8,128)(2,1)S(1)} %collective-permute-done.b), channel_id=1, source_target_pairs={{0,6},{16,22},{32,38},{48,54},{64,70},{80,86},{96,102},{112,118},{... | collective-permute-start | bytes 4915208 | tf_op jit(solution)/shard_map/ppermute | solution.py:57
  50.4 0.3 select_reduce_fusion.1
  50.8 0.1 stack.59
  50.9 0.1 stack.58
  51.0 0.1 copy.13
  51.1 0.0 copy-done.2
  51.1 0.0 copy-done.5
  51.1 0.3 select_reduce_fusion
  51.5 0.2 slice_reduce_fusion
  51.7 0.2 fusion
  51.9 0.2 select_reduce_fusion.3
  52.1 0.1 pad_add_fusion.1.meta
  52.2 0.1 slice.47
  52.2 0.2 copy-done
  52.4 2.0 %shard_map.91 = (bf16[256,1280]{1,0:T(8,128)(2,1)S(1)}, bf16[256,1280]{1,0:T(8,128)(2,1)S(1)}) custom-call(s32[20]{0:T(128)S(1)} %pad_add_fusion.1.meta, bf16[1,1,7,64,1280]{4,3,2,1,0:T(8,128)(2,1)S(1)} %copy-done, bf16[64,1280]{1,0:T(8,128)(2,1)S(1)} %collective-permute-done.1.in0, bf16[64,1280]{1,0:T(8,128)(2,1)} %collective-permute-done.2.in1, ...), custom_call_target="tpu_custom_call" | custom-call | tf_op jit(solution)/shard_map/pallas_call | solution.py:250
  54.4 1.9 %collective-permute-start.6 = (bf16[256,1280]{1,0:T(8,128)(2,1)S(1)}, bf16[256,1280]{1,0:T(8,128)(2,1)S(1)}, u32[]{:S(2)}, u32[]{:S(2)}) collective-permute-start(bf16[256,1280]{1,0:T(8,128)(2,1)S(1)} %get-tuple-element.24.xa), channel_id=1, source_target_pairs={{0,8},{8,0},{16,24},{24,16},{32,40},{40,32},{48,56},{56,48},{64,72... | collective-permute-start | bytes 1966088 | tf_op jit(solution)/shard_map/ppermute | solution.py:57
  56.3 0.0 collective-permute-done.7.a
  56.3 0.1 slice.52
  56.4 0.1 pad_maximum_fusion.1
  56.5 2.4 %collective-permute-start.8 = (bf16[320,2560]{1,0:T(8,128)(2,1)S(1)}, bf16[320,2560]{1,0:T(8,128)(2,1)S(1)}, u32[]{:S(2)}, u32[]{:S(2)}) collective-permute-start(bf16[320,2560]{1,0:T(8,128)(2,1)S(1)} %pad_maximum_fusion.1), channel_id=1, source_target_pairs={{0,8},{8,0},{16,24},{24,16},{32,40},{40,32},{48,56},{56,48},{64,72... | collective-permute-start | bytes 4915208 | tf_op jit(solution)/shard_map/ppermute | solution.py:57
  58.9 8.3 %collective-permute-done.4.c = bf16[320,2560]{1,0:T(8,128)(2,1)} collective-permute-done((bf16[320,2560]{1,0:T(8,128)(2,1)S(1)}, bf16[320,2560]{1,0:T(8,128)(2,1)}, u32[]{:S(2)}, u32[]{:S(2)}) %collective-permute-start.4) | collective-permute-done | bytes 1638432 | tf_op jit(solution)/shard_map/ppermute | solution.py:57
  67.2 1.2 %slice.50 = bf16[160,2560]{1,0:T(8,128)(2,1)S(1)} slice(bf16[320,2560]{1,0:T(8,128)(2,1)} %collective-permute-done.4.c), slice={[160:320], [0:2560]} | slice | bytes 1638400 | tf_op jit(solution)/shard_map/slice | solution.py:237
  68.4 0.0 collective-permute-done.5.d
  68.4 1.2 %slice.51 = bf16[160,2560]{1,0:T(8,128)(2,1)S(1)} slice(bf16[320,2560]{1,0:T(8,128)(2,1)} %collective-permute-done.5.d), slice={[160:320], [0:2560]} | slice | bytes 1638400 | tf_op jit(solution)/shard_map/slice | solution.py:237
  69.6 0.1 pad_maximum_fusion
  69.7 0.0 copy-start.1
  69.8 0.0 collective-permute-done.6._.xb
  69.8 1.9 %collective-permute-start.9 = (bf16[320,2560]{1,0:T(8,128)(2,1)S(1)}, bf16[320,2560]{1,0:T(8,128)(2,1)S(1)}, u32[]{:S(2)}, u32[]{:S(2)}) collective-permute-start(bf16[320,2560]{1,0:T(8,128)(2,1)S(1)} %pad_maximum_fusion), channel_id=1, source_target_pairs={{0,8},{8,0},{16,24},{24,16},{32,40},{40,32},{48,56},{56,48},{64,72... | collective-permute-start | bytes 4915208 | tf_op jit(solution)/shard_map/ppermute | solution.py:57
  71.7 0.0 collective-permute-done.8.early
  71.7 3.5 %collective-permute-done.9.late = bf16[320,2560]{1,0:T(8,128)(2,1)S(1)} collective-permute-done((bf16[320,2560]{1,0:T(8,128)(2,1)S(1)}, bf16[320,2560]{1,0:T(8,128)(2,1)S(1)}, u32[]{:S(2)}, u32[]{:S(2)}) %collective-permute-start.9) | collective-permute-done | bytes 1638432 | tf_op jit(solution)/shard_map/ppermute | solution.py:57
  75.2 2.1 %shard_map.92 = (bf16[1280,1920]{1,0:T(8,128)(2,1)S(1)}, bf16[1280,640]{1,0:T(8,128)(2,1)S(1)}) custom-call(s32[20]{0:T(128)S(1)} %pad_add_fusion.1.meta, bf16[320,2560]{1,0:T(8,128)(2,1)} %constant_dynamic-update-slice_fusion.own, bf16[320,2560]{1,0:T(8,128)(2,1)S(1)} %collective-permute-done.7.a, bf16[320,2560]{1,0:T(8,128)(2,1)S(1)} %collective-permute-done.b, ...), custom_call_target="tpu_custom_call" | custom-call | tf_op jit(solution)/shard_map/pallas_call | solution.py:262
  77.3 2.3 %collective-permute-start.11 = (bf16[1280,640]{1,0:T(8,128)(2,1)S(1)}, bf16[1280,640]{1,0:T(8,128)(2,1)S(1)}, u32[]{:S(2)}, u32[]{:S(2)}) collective-permute-start(bf16[1280,640]{1,0:T(8,128)(2,1)S(1)} %get-tuple-element.31.wa), channel_id=1, source_target_pairs={{0,8},{8,0},{16,24},{24,16},{32,40},{40,32},{48,56},{56,48},{64,72... | collective-permute-start | bytes 4915208 | tf_op jit(solution)/shard_map/ppermute | solution.py:57
  79.6 0.0 copy-done.1
  79.6 0.1 fusion.4
  79.7 0.0 copy-start.3
  79.7 0.0 copy-start.4
  79.8 5.3 %shard_map.93 = (bf16[256,640]{1,0:T(8,128)(2,1)S(1)}, bf16[256,640]{1,0:T(8,128)(2,1)S(1)}) custom-call(s32[20]{0:T(128)S(1)} %pad_add_fusion.1.meta, bf16[256,1280]{1,0:T(8,128)(2,1)S(1)} %get-tuple-element.24.xa, bf16[256,1280]{1,0:T(8,128)(2,1)S(1)} %collective-permute-done.6._.xb, f32[1,1920]{1,0:T(1,128)S(1)} %reshape.81.bias, ...), custom_call_target="tpu_custom_call" | custom-call | tf_op jit(solution)/shard_map/pallas_call | solution.py:275
  85.0 2.0 %collective-permute-start.10 = (bf16[256,640]{1,0:T(8,128)(2,1)S(1)}, bf16[256,640]{1,0:T(8,128)(2,1)S(1)}, u32[]{:S(2)}, u32[]{:S(2)}) collective-permute-start(bf16[256,640]{1,0:T(8,128)(2,1)S(1)} %get-tuple-element.30), channel_id=1, source_target_pairs={{0,8},{8,0},{16,24},{24,16},{32,40},{40,32},{48,56},{56,48},{64,72... | collective-permute-start | bytes 983048 | tf_op jit(solution)/shard_map/ppermute | solution.py:57
  87.0 0.0 copy-done.3
  87.1 0.0 copy-done.4
  87.1 1.5 %collective-permute-done.10.attb = bf16[256,640]{1,0:T(8,128)(2,1)S(1)} collective-permute-done((bf16[256,640]{1,0:T(8,128)(2,1)S(1)}, bf16[256,640]{1,0:T(8,128)(2,1)S(1)}, u32[]{:S(2)}, u32[]{:S(2)}) %collective-permute-start.10) | collective-permute-done | bytes 327712 | tf_op jit(solution)/shard_map/ppermute | solution.py:57
  88.6 0.0 collective-permute-done.11.wb
  88.6 3.0 %shard_map.94 = bf16[64,5120]{1,0:T(8,128)(2,1)} custom-call(s32[20]{0:T(128)S(1)} %pad_add_fusion.1.meta, bf16[256,640]{1,0:T(8,128)(2,1)S(1)} %get-tuple-element.29.atta, bf16[256,640]{1,0:T(8,128)(2,1)S(1)} %collective-permute-done.10.attb, bf16[1280,640]{1,0:T(8,128)(2,1)S(1)} %get-tuple-element.31.wa, bf16[1280,640]{1,0:T(8,128)(2,1)S(1)} %collective-permute-done.11.wb, ...), custom_call_target="tpu_custom_call" | custom-call | tf_op jit(solution)/shard_map/pallas_call | solution.py:285
  (13 shorter events, 0.1 us)
Async XLA Ops:
  3.7 14.5 %copy-start.6 = (s32[64,1,7]{0,1,2:T(1,128)S(1)}, s32[64,1,7]{0,1,2:T(1,128)}, u32[]{:S(2)}) copy-start(s32[64,1,7]{0,1,2:T(1,128)} %param.16) | copy-start | bytes 5380
  3.7 47.4 %copy-start.2 = (f32[1280]{0:T(1024)S(1)}, f32[1280]{0:T(1024)}, u32[]{:S(2)}) copy-start(f32[1280]{0:T(1024)} %param.10) | copy-start | bytes 15364
  3.7 47.4 %copy-start.5 = (s32[64,1,7,2]{0,3,2,1:T(2,128)S(1)}, s32[64,1,7,2]{0,3,2,1:T(2,128)}, u32[]{:S(2)}) copy-start(s32[64,1,7,2]{0,3,2,1:T(2,128)} %param.17) | copy-start | bytes 10756
  4.7 36.5 %collective-permute-start = (bf16[320,2560]{1,0:T(8,128)(2,1)}, bf16[320,2560]{1,0:T(8,128)(2,1)S(1)}, u32[]{:S(2)}, u32[]{:S(2)}) collective-permute-start(bf16[320,2560]{1,0:T(8,128)(2,1)} %constant_dynamic-update-slice_fusion.own), channel_id=1, source_target_pairs={{0,257},{8,12},{16,273},{24,28},{32,289},{40,44},{48,305},{56,60},... | collective-permute-start | bytes 4915208 | tf_op jit(solution)/shard_map/ppermute | solution.py:57
  6.8 49.5 %collective-permute-start.7 = (bf16[320,2560]{1,0:T(8,128)(2,1)}, bf16[320,2560]{1,0:T(8,128)(2,1)S(1)}, u32[]{:S(2)}, u32[]{:S(2)}) collective-permute-start(bf16[320,2560]{1,0:T(8,128)(2,1)} %constant_dynamic-update-slice_fusion.own), channel_id=1, source_target_pairs={{0,2},{8,14},{16,18},{24,30},{32,34},{40,46},{48,50},{56,62},{64,6... | collective-permute-start | bytes 4915208 | tf_op jit(solution)/shard_map/ppermute | solution.py:57
  12.4 6.0 %collective-permute-start.1 = (bf16[64,1280]{1,0:T(8,128)(2,1)}, bf16[64,1280]{1,0:T(8,128)(2,1)S(1)}, u32[]{:S(2)}, u32[]{:S(2)}) collective-permute-start(bf16[64,1280]{1,0:T(8,128)(2,1)} %get-tuple-element.45), channel_id=1, source_target_pairs={{0,8},{8,16},{16,24},{24,32},{32,40},{40,48},{48,56},{56,64},{64,7... | collective-permute-start | bytes 491528 | tf_op jit(solution)/shard_map/ppermute | solution.py:62
  14.4 10.6 %collective-permute-start.2 = (bf16[64,1280]{1,0:T(8,128)(2,1)}, bf16[64,1280]{1,0:T(8,128)(2,1)}, u32[]{:S(2)}, u32[]{:S(2)}) collective-permute-start(bf16[64,1280]{1,0:T(8,128)(2,1)} %get-tuple-element.44), channel_id=1, source_target_pairs={{0,16},{8,24},{16,32},{24,40},{32,48},{40,56},{48,64},{56,72},{64,... | collective-permute-start | bytes 491528 | tf_op jit(solution)/shard_map/ppermute | solution.py:62
  16.3 13.8 %collective-permute-start.3 = (bf16[64,1280]{1,0:T(8,128)(2,1)}, bf16[64,1280]{1,0:T(8,128)(2,1)}, u32[]{:S(2)}, u32[]{:S(2)}) collective-permute-start(bf16[64,1280]{1,0:T(8,128)(2,1)} %get-tuple-element.43), channel_id=1, source_target_pairs={{0,24},{8,32},{16,40},{24,48},{32,56},{40,64},{48,72},{56,80},{64,... | collective-permute-start | bytes 491528 | tf_op jit(solution)/shard_map/ppermute | solution.py:62
  41.2 26.0 %collective-permute-start.4 = (bf16[320,2560]{1,0:T(8,128)(2,1)S(1)}, bf16[320,2560]{1,0:T(8,128)(2,1)}, u32[]{:S(2)}, u32[]{:S(2)}) collective-permute-start(bf16[320,2560]{1,0:T(8,128)(2,1)S(1)} %collective-permute-done.b), channel_id=1, source_target_pairs={{0,2},{8,265},{16,18},{24,281},{32,34},{40,297},{48,50},{56,313},{... | collective-permute-start | bytes 4915208 | tf_op jit(solution)/shard_map/ppermute | solution.py:57
  48.6 19.8 %collective-permute-start.5 = (bf16[320,2560]{1,0:T(8,128)(2,1)S(1)}, bf16[320,2560]{1,0:T(8,128)(2,1)}, u32[]{:S(2)}, u32[]{:S(2)}) collective-permute-start(bf16[320,2560]{1,0:T(8,128)(2,1)S(1)} %collective-permute-done.b), channel_id=1, source_target_pairs={{0,6},{16,22},{32,38},{48,54},{64,70},{80,86},{96,102},{112,118},{... | collective-permute-start | bytes 4915208 | tf_op jit(solution)/shard_map/ppermute | solution.py:57
  51.1 1.3 %copy-start = (bf16[1,1,7,64,1280]{4,3,2,1,0:T(8,128)(2,1)S(1)}, bf16[1,1,7,64,1280]{4,3,2,1,0:T(8,128)(2,1)}, u32[]{:S(2)}) copy-start(bf16[1,1,7,64,1280]{4,3,2,1,0:T(8,128)(2,1)} %own.1) | copy-start | bytes 3440644
  54.4 15.4 %collective-permute-start.6 = (bf16[256,1280]{1,0:T(8,128)(2,1)S(1)}, bf16[256,1280]{1,0:T(8,128)(2,1)S(1)}, u32[]{:S(2)}, u32[]{:S(2)}) collective-permute-start(bf16[256,1280]{1,0:T(8,128)(2,1)S(1)} %get-tuple-element.24.xa), channel_id=1, source_target_pairs={{0,8},{8,0},{16,24},{24,16},{32,40},{40,32},{48,56},{56,48},{64,72... | collective-permute-start | bytes 1966088 | tf_op jit(solution)/shard_map/ppermute | solution.py:57
  56.5 15.2 %collective-permute-start.8 = (bf16[320,2560]{1,0:T(8,128)(2,1)S(1)}, bf16[320,2560]{1,0:T(8,128)(2,1)S(1)}, u32[]{:S(2)}, u32[]{:S(2)}) collective-permute-start(bf16[320,2560]{1,0:T(8,128)(2,1)S(1)} %pad_maximum_fusion.1), channel_id=1, source_target_pairs={{0,8},{8,0},{16,24},{24,16},{32,40},{40,32},{48,56},{56,48},{64,72... | collective-permute-start | bytes 4915208 | tf_op jit(solution)/shard_map/ppermute | solution.py:57
  69.7 9.9 %copy-start.1 = (f32[3840]{0:T(1024)S(1)}, f32[3840]{0:T(1024)}, u32[]{:S(2)}) copy-start(f32[3840]{0:T(1024)} %param.12) | copy-start | bytes 46084
  69.8 5.4 %collective-permute-start.9 = (bf16[320,2560]{1,0:T(8,128)(2,1)S(1)}, bf16[320,2560]{1,0:T(8,128)(2,1)S(1)}, u32[]{:S(2)}, u32[]{:S(2)}) collective-permute-start(bf16[320,2560]{1,0:T(8,128)(2,1)S(1)} %pad_maximum_fusion), channel_id=1, source_target_pairs={{0,8},{8,0},{16,24},{24,16},{32,40},{40,32},{48,56},{56,48},{64,72... | collective-permute-start | bytes 4915208 | tf_op jit(solution)/shard_map/ppermute | solution.py:57
  77.3 11.3 %collective-permute-start.11 = (bf16[1280,640]{1,0:T(8,128)(2,1)S(1)}, bf16[1280,640]{1,0:T(8,128)(2,1)S(1)}, u32[]{:S(2)}, u32[]{:S(2)}) collective-permute-start(bf16[1280,640]{1,0:T(8,128)(2,1)S(1)} %get-tuple-element.31.wa), channel_id=1, source_target_pairs={{0,8},{8,0},{16,24},{24,16},{32,40},{40,32},{48,56},{56,48},{64,72... | collective-permute-start | bytes 4915208 | tf_op jit(solution)/shard_map/ppermute | solution.py:57
  79.7 7.3 %copy-start.3 = (f32[1280]{0:T(1024)S(1)}, f32[1280]{0:T(1024)}, u32[]{:S(2)}) copy-start(f32[1280]{0:T(1024)} %param.14) | copy-start | bytes 15364
  79.7 7.3 %copy-start.4 = (f32[1280]{0:T(1024)S(1)}, f32[1280]{0:T(1024)}, u32[]{:S(2)}) copy-start(f32[1280]{0:T(1024)} %param.15) | copy-start | bytes 15364
  85.0 3.5 %collective-permute-start.10 = (bf16[256,640]{1,0:T(8,128)(2,1)S(1)}, bf16[256,640]{1,0:T(8,128)(2,1)S(1)}, u32[]{:S(2)}, u32[]{:S(2)}) collective-permute-start(bf16[256,640]{1,0:T(8,128)(2,1)S(1)} %get-tuple-element.30), channel_id=1, source_target_pairs={{0,8},{8,0},{16,24},{24,16},{32,40},{40,32},{48,56},{56,48},{64,72... | collective-permute-start | bytes 983048 | tf_op jit(solution)/shard_map/ppermute | solution.py:57

commit v7 on v6

--- a/solution.py
+++ b/solution.py
@@ -15,6 +15,7 @@
 HEAD = D // HEADS
 SHARDS = 8
 DEPTH = D // SHARDS
+PART = DEPTH // 2
 ROWS = RECV * WIN
 NX, NYH, NYL, NZ, NC = 4, 2, 2, 16, 2
 AXES = ("dp", "fsdp")
@@ -49,6 +50,10 @@
     return pairs if odd else [p for p in pairs if p[0] != p[1]]
 
 
+def planes():
+    return perm(lambda x, yh, yl, z, c: (x, yh, yl, z - 1 if c else z + 1, c))
+
+
 def other_core():
     return perm(lambda x, yh, yl, z, c: (x, yh, yl, z, 1 - c))
 
@@ -81,17 +86,29 @@
         normed[rows, :] = (x * lax.rsqrt(ms + EPS) * gain[...]).astype(jnp.bfloat16)
 
 
-def gather_kernel(meta, own, a, b, c, d, early, late, _, w, wo, sems):
+def gather_kernel(meta, own, a, b, c, d, rest_a, early, late, _, w, wo, sems):
     core = lax.rem(lax.axis_index("dp"), NC)
-    sources = [(ref, 0) for ref in (own, a, b, c)]
-    sources += [(early, 0), (early, DEPTH), (late, 0)]
-
-    def copies(i, ref, row):
-        at = pl.multiple_of(meta[12 + i] * DEPTH, DEPTH)
+    near = lax.rem(lax.div(lax.axis_index("dp"), NC), 2) * PART
+    away = PART - near
+    sources = [
+        (0, own, 0, DEPTH, 0),
+        (1, a, 0, PART, near),
+        (1, rest_a, 0, PART, away),
+        (2, b, 0, DEPTH, 0),
+        (3, c, 0, DEPTH, 0),
+        (4, early, 0, PART, near),
+        (4, early, PART, PART, away),
+        (5, early, DEPTH, DEPTH, 0),
+        (6, late, 0, DEPTH, 0),
+    ]
+    last = len(sources)
+
+    def copies(i, shard, ref, row, rows, to):
+        at = pl.multiple_of(meta[12 + shard] * DEPTH + to, PART)
         return [
             pltpu.make_async_copy(
-                ref.at[pl.ds(row, DEPTH), pl.ds(j * 3 * HALF, (3 - 2 * j) * HALF)],
-                dst.at[pl.ds(at, DEPTH), :],
+                ref.at[pl.ds(row, rows), pl.ds(j * 3 * HALF, (3 - 2 * j) * HALF)],
+                dst.at[pl.ds(at, rows), :],
                 sems.at[i, j],
             )
             for j, dst in enumerate((w, wo))
@@ -103,15 +120,15 @@
 
     @pl.when(core == 0)
     def _():
-        for copy in copies(SHARDS - 1, d, 0):
+        for copy in copies(last, SHARDS - 1, d, 0, DEPTH, 0):
             copy.start()
 
     @pl.when(core != 0)
     def _():
-        for copy in copies(SHARDS - 1, late, DEPTH):
+        for copy in copies(last, SHARDS - 1, late, DEPTH, DEPTH, 0):
             copy.start()
 
-    for i, source in enumerate((*sources, (late, DEPTH))):
+    for i, source in enumerate((*sources, (SHARDS - 1, late, DEPTH, DEPTH, 0))):
         for copy in copies(i, *source):
             copy.wait()
 
@@ -234,16 +251,20 @@
         [lax.dynamic_slice_in_dim(b_qkv, j * D + half, HALF, 0) for j in range(3)]
     )
     def halves_of(*shards):
-        return jnp.concatenate([value[DEPTH:] for value in shards], axis=0)
+        return jnp.concatenate([value[value.shape[0] // 2 :] for value in shards], axis=0)
 
     got_b = send(piece, moves((0, 1), (2, 0)))
-    got_a = send(piece, moves((1, 0), (-1, 0)))
+    near = rank // NC % 2 * PART
+    part = jnp.concatenate(
+        [lax.dynamic_slice_in_dim(piece, i * DEPTH + near, PART, 0) for i in range(NC)], axis=0
+    )
+    got_a = send(part, moves((1, 0), (-1, 0)))
     moved = [by_rank(patches[0, 0, RECV + m], m + 1) for m in range(SLOTS - RECV)]
-    got_b, *moved = lax.optimization_barrier((got_b, *moved))
+    got_b, *moved[:2] = lax.optimization_barrier((got_b, *moved[:2]))
     got_c = send(got_b, moves((1, 0), (0, 1)))
     got_d = send(got_b, moves((-1, 0)))
-    early = send(halves_of(got_a, got_b), other_core())
-
+    rest_a = send(got_a, planes())
+    early = send(halves_of(got_a, rest_a, got_b), other_core())
 
     meta = tables(route, groups, rank, lane // NYH, lane % NYH)
 
@@ -265,11 +286,11 @@
             jax.ShapeDtypeStruct((D, 3 * HALF), jnp.bfloat16),
             jax.ShapeDtypeStruct((D, HALF), jnp.bfloat16),
         ],
-        in_specs=[SMEM] + [ANY] * 8,
+        in_specs=[SMEM] + [ANY] * 9,
         out_specs=vmem(2),
-        scratch_shapes=[pltpu.SemaphoreType.DMA((SHARDS, 2))],
+        scratch_shapes=[pltpu.SemaphoreType.DMA((SHARDS + 2, 2))],
         compiler_params=PARAMS,
-    )(meta, piece, got_a, got_b, got_c, got_d, early, late, normed_other)
+    )(meta, piece, got_a, got_b, got_c, got_d, rest_a, early, late, normed_other)
     w_other = send(w_mine, other_core())
 
     att, att_theirs = pl.pallas_call(

time: 92.2 us -> 94.6 us (1.026)
  the two profiles are of different devices: /device:TPU:485 before, /device:TPU:1 now
where the time goes in v7:
time: 94.6 us; the launch traced here: 93.8 us
  starting transfers between devices  50.3 us (53%)
  waiting for transfers between devices  18.2 us (19%)
  Pallas kernels  12.5 us (13%)
  local copies, waits for them, and re-layouts  9.89 us (10%)
  other arithmetic  2.54 us (3%)
    ppermute x10, starting transfers between devices, send(): return lax.ppermute(value, AXES, pairs)  38.2 us
    ppermute x3, starting transfers between devices, by_rank(): lax.ppermute(value, 'dp', [(i, (i + by) % devices) for i in range(devices)])  12.1 us
    ppermute x10, waiting for transfers between devices, send(): return lax.ppermute(value, AXES, pairs)  12 us
    ppermute x3, waiting for transfers between devices, by_rank(): lax.ppermute(value, 'dp', [(i, (i + by) % devices) for i in range(devices)])  6.2 us
    pallas_call x1, Pallas kernels, on_device(): pl.pallas_call(attend_kernel, out_shape=[jax.ShapeDtypeStruct((ROWS, HALF...  5.26 us
    slice x5, local copies, waits for them, and re-layouts, halves_of(): value[value.shape[0] // 2:]  4.58 us
    pallas_call x1, Pallas kernels, on_device(): pl.pallas_call(merge_kernel, out_shape=jax.ShapeDtypeStruct((ROWS // MERG...  2.97 us
    pallas_call x1, Pallas kernels, on_device(): pl.pallas_call(gather_kernel, out_shape=[jax.ShapeDtypeStruct((D, 3 * HAL...  2.23 us
  transfers between devices with their start and end apart: 13, of which 5 were waited for; matrix products, arithmetic and copies ran while one was open for 10% of the time, Pallas kernels for 8%

profile of v7, /device:TPU:1, one launch (start us, length us, event | category | flops | bytes accessed | tf_op | source)
XLA Modules:
  0.0 93.8 jit_solution(16297349044563776852)
XLA Ops:
  0.0 1.1 %dynamic-slice_bitcast_fusion = (bf16[160,640]{1,0:T(8,128)(2,1)S(1)}, bf16[160,640]{1,0:T(8,128)(2,1)S(1)}) fusion(bf16[1280,160]{0,1:T(8,128)(2,1)} %param.13, s32[]{:T(128)S(6)} %select_n.199, s32[]{:T(128)S(6)} %select_n.195), kind=kLoop, calls=%fused_computation.5 | loop fusion | bytes 819208 | tf_op jit(solution)/shard_map/dynamic_slice | solution.py:243
  1.1 1.5 %constant_dynamic-slice_fusion.4 = (bf16[160,640]{1,0:T(8,128)(2,1)S(1)}, bf16[160,640]{1,0:T(8,128)(2,1)S(1)}, bf16[160,640]{1,0:T(8,128)(2,1)S(1)}, bf16[160,6...) fusion(bf16[160,3840]{1,0:T(8,128)(2,1)} %param.11, s32[]{:T(128)S(6)} %select_n.196, ...), kind=kLoop, calls=%fused_computation.33 | loop fusion | bytes 2457624 | tf_op jit(solution)/shard_map/dynamic_slice | solution.py:242
  2.6 0.2 pad_maximum_fusion.2
  2.7 0.1 constant_dynamic-update-slice_fusion.1
  2.8 0.1 constant_dynamic-update-slice_fusion.own
  2.9 5.5 %collective-permute-start = (bf16[320,2560]{1,0:T(8,128)(2,1)S(1)}, bf16[320,2560]{1,0:T(8,128)(2,1)S(1)}, u32[]{:S(2)}, u32[]{:S(2)}) collective-permute-start(bf16[320,2560]{1,0:T(8,128)(2,1)S(1)} %constant_dynamic-update-slice_fusion.own), channel_id=1, source_target_pairs={{0,257},{8,12},{16,273},{24,28},{32,289},{40,44},{48,305},{56,60},... | collective-permute-start | bytes 4915208 | tf_op jit(solution)/shard_map/ppermute | solution.py:62
  8.4 0.1 constant_dynamic-slice_fusion.1
  8.4 0.0 copy-start.6
  8.5 0.0 copy-start.5
  8.5 0.0 copy-start.2
  8.5 0.9 %pad_maximum_fusion.4 = bf16[160,2560]{1,0:T(8,128)(2,1)} fusion(bf16[80,2560]{1,0:T(8,128)(2,1)S(1)} %get-tuple-element.36, bf16[80,2560]{1,0:T(8,128)(2,1)S(1)} %get-tuple-element.35), kind=kLoop, calls=%fused_computation.4 | loop fusion | flops 1638400 | bytes 1638400 | tf_op jit(solution)/shard_map/concatenate | solution.py:258
  9.4 2.8 %collective-permute-start.7 = (bf16[160,2560]{1,0:T(8,128)(2,1)}, bf16[160,2560]{1,0:T(8,128)(2,1)}, u32[]{:S(2)}, u32[]{:S(2)}) collective-permute-start(bf16[160,2560]{1,0:T(8,128)(2,1)} %pad_maximum_fusion.4), channel_id=1, source_target_pairs={{0,2},{8,14},{16,18},{24,30},{32,34},{40,46},{48,50},{56,62},{64,6... | collective-permute-start | bytes 2457608 | tf_op jit(solution)/shard_map/ppermute | solution.py:62
  12.2 1.9 %slice_bitcast_fusion = (bf16[64,1280]{1,0:T(8,128)(2,1)}, bf16[64,1280]{1,0:T(8,128)(2,1)}, bf16[64,1280]{1,0:T(8,128)(2,1)}) fusion(bf16[1,1,7,64,1280]{4,3,2,1,0:T(8,128)(2,1)} %own.1), kind=kLoop, calls=%fused_computation.7 | loop fusion | bytes 983040 | tf_op jit(solution)/shard_map/squeeze | solution.py:262
  14.1 5.0 %collective-permute-start.1 = (bf16[64,1280]{1,0:T(8,128)(2,1)}, bf16[64,1280]{1,0:T(8,128)(2,1)S(1)}, u32[]{:S(2)}, u32[]{:S(2)}) collective-permute-start(bf16[64,1280]{1,0:T(8,128)(2,1)} %get-tuple-element.45), channel_id=1, source_target_pairs={{0,8},{8,16},{16,24},{24,32},{32,40},{40,48},{48,56},{56,64},{64,7... | collective-permute-start | bytes 491528 | tf_op jit(solution)/shard_map/ppermute | solution.py:67
  19.1 3.5 %collective-permute-start.2 = (bf16[64,1280]{1,0:T(8,128)(2,1)}, bf16[64,1280]{1,0:T(8,128)(2,1)}, u32[]{:S(2)}, u32[]{:S(2)}) collective-permute-start(bf16[64,1280]{1,0:T(8,128)(2,1)} %get-tuple-element.44), channel_id=1, source_target_pairs={{0,16},{8,24},{16,32},{24,40},{32,48},{40,56},{48,64},{56,72},{64,... | collective-permute-start | bytes 491528 | tf_op jit(solution)/shard_map/ppermute | solution.py:67
  22.6 3.6 %collective-permute-start.3 = (bf16[64,1280]{1,0:T(8,128)(2,1)}, bf16[64,1280]{1,0:T(8,128)(2,1)}, u32[]{:S(2)}, u32[]{:S(2)}) collective-permute-start(bf16[64,1280]{1,0:T(8,128)(2,1)} %get-tuple-element.43), channel_id=1, source_target_pairs={{0,24},{8,32},{16,40},{24,48},{32,56},{40,64},{48,72},{56,80},{64,... | collective-permute-start | bytes 491528 | tf_op jit(solution)/shard_map/ppermute | solution.py:67
  26.2 0.1 pad_add_fusion
  26.3 0.1 fusion.2
  26.3 0.0 collective-permute-done.1.in0
  26.3 6.2 %collective-permute-done.2.in1 = bf16[64,1280]{1,0:T(8,128)(2,1)} collective-permute-done((bf16[64,1280]{1,0:T(8,128)(2,1)}, bf16[64,1280]{1,0:T(8,128)(2,1)}, u32[]{:S(2)}, u32[]{:S(2)}) %collective-permute-start.2) | collective-permute-done | bytes 163872 | tf_op jit(solution)/shard_map/ppermute | solution.py:67
  32.5 3.5 %collective-permute-done.b = bf16[320,2560]{1,0:T(8,128)(2,1)S(1)} collective-permute-done((bf16[320,2560]{1,0:T(8,128)(2,1)S(1)}, bf16[320,2560]{1,0:T(8,128)(2,1)S(1)}, u32[]{:S(2)}, u32[]{:S(2)}) %collective-permute-start) | collective-permute-done | bytes 1638432 | tf_op jit(solution)/shard_map/ppermute | solution.py:62
  36.0 4.9 %collective-permute-start.4 = (bf16[320,2560]{1,0:T(8,128)(2,1)S(1)}, bf16[320,2560]{1,0:T(8,128)(2,1)}, u32[]{:S(2)}, u32[]{:S(2)}) collective-permute-start(bf16[320,2560]{1,0:T(8,128)(2,1)S(1)} %collective-permute-done.b), channel_id=1, source_target_pairs={{0,2},{8,265},{16,18},{24,281},{32,34},{40,297},{48,50},{56,313},{... | collective-permute-start | bytes 4915208 | tf_op jit(solution)/shard_map/ppermute | solution.py:62
  40.9 1.8 %collective-permute-start.5 = (bf16[320,2560]{1,0:T(8,128)(2,1)S(1)}, bf16[320,2560]{1,0:T(8,128)(2,1)}, u32[]{:S(2)}, u32[]{:S(2)}) collective-permute-start(bf16[320,2560]{1,0:T(8,128)(2,1)S(1)} %collective-permute-done.b), channel_id=1, source_target_pairs={{0,6},{16,22},{32,38},{48,54},{64,70},{80,86},{96,102},{112,118},{... | collective-permute-start | bytes 4915208 | tf_op jit(solution)/shard_map/ppermute | solution.py:62
  42.8 0.3 select_reduce_fusion.1
  43.0 0.1 copy.13
  43.1 0.3 select_reduce_fusion
  43.5 0.2 slice_reduce_fusion
  43.7 0.2 fusion
  43.9 0.0 collective-permute-done.7.a
  43.9 12.5 %collective-permute-start.8 = (bf16[160,2560]{1,0:T(8,128)(2,1)}, bf16[160,2560]{1,0:T(8,128)(2,1)}, u32[]{:S(2)}, u32[]{:S(2)}) collective-permute-start(bf16[160,2560]{1,0:T(8,128)(2,1)} %collective-permute-done.7.a), channel_id=1, source_target_pairs={{0,16},{8,248},{16,32},{24,8},{32,48},{40,24},{48,64},{56,40},{64,... | collective-permute-start | bytes 2457608 | tf_op jit(solution)/shard_map/ppermute | solution.py:62
  56.4 0.1 select_reduce_fusion.3
  56.6 0.1 stack.59
  56.7 0.1 stack.58
  56.9 0.1 pad_add_fusion.1.meta
  56.9 1.1 %slice.56 = bf16[80,2560]{1,0:T(8,128)(2,1)S(1)} slice(bf16[160,2560]{1,0:T(8,128)(2,1)} %collective-permute-done.7.a), slice={[80:160], [0:2560]} | slice | bytes 819200 | tf_op jit(solution)/shard_map/slice | solution.py:254
  58.0 0.1 slice.51
  58.1 0.0 collective-permute-done.3.in2
  58.1 0.1 copy-done
  58.2 2.0 %shard_map.91 = (bf16[256,1280]{1,0:T(8,128)(2,1)S(1)}, bf16[256,1280]{1,0:T(8,128)(2,1)S(1)}) custom-call(s32[20]{0:T(128)S(1)} %pad_add_fusion.1.meta, bf16[1,1,7,64,1280]{4,3,2,1,0:T(8,128)(2,1)S(1)} %copy-done, bf16[64,1280]{1,0:T(8,128)(2,1)S(1)} %collective-permute-done.1.in0, bf16[64,1280]{1,0:T(8,128)(2,1)} %collective-permute-done.2.in1, ...), custom_call_target="tpu_custom_call" | custom-call | tf_op jit(solution)/shard_map/pallas_call | solution.py:271
  60.2 1.9 %collective-permute-start.6 = (bf16[256,1280]{1,0:T(8,128)(2,1)S(1)}, bf16[256,1280]{1,0:T(8,128)(2,1)S(1)}, u32[]{:S(2)}, u32[]{:S(2)}) collective-permute-start(bf16[256,1280]{1,0:T(8,128)(2,1)S(1)} %get-tuple-element.22.xa), channel_id=1, source_target_pairs={{0,8},{8,0},{16,24},{24,16},{32,40},{40,32},{48,56},{56,48},{64,72... | collective-permute-start | bytes 1966088 | tf_op jit(solution)/shard_map/ppermute | solution.py:62
  62.1 3.8 %collective-permute-done.8.rest_a = bf16[160,2560]{1,0:T(8,128)(2,1)} collective-permute-done((bf16[160,2560]{1,0:T(8,128)(2,1)}, bf16[160,2560]{1,0:T(8,128)(2,1)}, u32[]{:S(2)}, u32[]{:S(2)}) %collective-permute-start.8) | collective-permute-done | bytes 819232 | tf_op jit(solution)/shard_map/ppermute | solution.py:62
  66.0 1.0 %slice.57 = bf16[80,2560]{1,0:T(8,128)(2,1)S(1)} slice(bf16[160,2560]{1,0:T(8,128)(2,1)} %collective-permute-done.8.rest_a), slice={[80:160], [0:2560]} | slice | bytes 819200 | tf_op jit(solution)/shard_map/slice | solution.py:254
  67.0 0.1 pad_maximum_fusion.1
  67.1 1.9 %collective-permute-start.9 = (bf16[320,2560]{1,0:T(8,128)(2,1)S(1)}, bf16[320,2560]{1,0:T(8,128)(2,1)S(1)}, u32[]{:S(2)}, u32[]{:S(2)}) collective-permute-start(bf16[320,2560]{1,0:T(8,128)(2,1)S(1)} %pad_maximum_fusion.1), channel_id=1, source_target_pairs={{0,8},{8,0},{16,24},{24,16},{32,40},{40,32},{48,56},{56,48},{64,72... | collective-permute-start | bytes 4915208 | tf_op jit(solution)/shard_map/ppermute | solution.py:62
  69.0 0.0 collective-permute-done.4.c
  69.0 1.2 %slice.54 = bf16[160,2560]{1,0:T(8,128)(2,1)S(1)} slice(bf16[320,2560]{1,0:T(8,128)(2,1)} %collective-permute-done.4.c), slice={[160:320], [0:2560]} | slice | bytes 1638400 | tf_op jit(solution)/shard_map/slice | solution.py:254
  70.2 0.0 collective-permute-done.5.d
  70.3 1.2 %slice.55 = bf16[160,2560]{1,0:T(8,128)(2,1)S(1)} slice(bf16[320,2560]{1,0:T(8,128)(2,1)} %collective-permute-done.5.d), slice={[160:320], [0:2560]} | slice | bytes 1638400 | tf_op jit(solution)/shard_map/slice | solution.py:254
  71.5 0.1 pad_maximum_fusion
  71.6 0.0 copy-start.1
  71.6 0.0 collective-permute-done.6._.xb
  71.6 2.4 %collective-permute-start.10 = (bf16[320,2560]{1,0:T(8,128)(2,1)S(1)}, bf16[320,2560]{1,0:T(8,128)(2,1)S(1)}, u32[]{:S(2)}, u32[]{:S(2)}) collective-permute-start(bf16[320,2560]{1,0:T(8,128)(2,1)S(1)} %pad_maximum_fusion), channel_id=1, source_target_pairs={{0,8},{8,0},{16,24},{24,16},{32,40},{40,32},{48,56},{56,48},{64,72... | collective-permute-start | bytes 4915208 | tf_op jit(solution)/shard_map/ppermute | solution.py:62
  74.0 0.0 collective-permute-done.9.early
  74.0 3.1 %collective-permute-done.10.late = bf16[320,2560]{1,0:T(8,128)(2,1)S(1)} collective-permute-done((bf16[320,2560]{1,0:T(8,128)(2,1)S(1)}, bf16[320,2560]{1,0:T(8,128)(2,1)S(1)}, u32[]{:S(2)}, u32[]{:S(2)}) %collective-permute-start.10) | collective-permute-done | bytes 1638432 | tf_op jit(solution)/shard_map/ppermute | solution.py:62
  77.1 2.2 %shard_map.92 = (bf16[1280,1920]{1,0:T(8,128)(2,1)S(1)}, bf16[1280,640]{1,0:T(8,128)(2,1)S(1)}) custom-call(s32[20]{0:T(128)S(1)} %pad_add_fusion.1.meta, bf16[320,2560]{1,0:T(8,128)(2,1)S(1)} %constant_dynamic-update-slice_fusion.own, bf16[160,2560]{1,0:T(8,128)(2,1)} %collective-permute-done.7.a, bf16[320,2560]{1,0:T(8,128)(2,1)S(1)} %collective-permute-done.b, ...), custom_call_target="tpu_custom_call" | custom-call | tf_op jit(solution)/shard_map/pallas_call | solution.py:283
  79.4 2.6 %collective-permute-start.12 = (bf16[1280,640]{1,0:T(8,128)(2,1)S(1)}, bf16[1280,640]{1,0:T(8,128)(2,1)S(1)}, u32[]{:S(2)}, u32[]{:S(2)}) collective-permute-start(bf16[1280,640]{1,0:T(8,128)(2,1)S(1)} %get-tuple-element.29.wa), channel_id=1, source_target_pairs={{0,8},{8,0},{16,24},{24,16},{32,40},{40,32},{48,56},{56,48},{64,72... | collective-permute-start | bytes 4915208 | tf_op jit(solution)/shard_map/ppermute | solution.py:62
  81.9 0.1 fusion.4
  82.1 0.0 copy-start.3
  82.1 0.0 copy-start.4
  82.1 5.3 %shard_map.93 = (bf16[256,640]{1,0:T(8,128)(2,1)S(1)}, bf16[256,640]{1,0:T(8,128)(2,1)S(1)}) custom-call(s32[20]{0:T(128)S(1)} %pad_add_fusion.1.meta, bf16[256,1280]{1,0:T(8,128)(2,1)S(1)} %get-tuple-element.22.xa, bf16[256,1280]{1,0:T(8,128)(2,1)S(1)} %collective-permute-done.6._.xb, f32[1,1920]{1,0:T(1,128)S(1)} %reshape.81.bias, ...), custom_call_target="tpu_custom_call" | custom-call | tf_op jit(solution)/shard_map/pallas_call | solution.py:296
  87.3 1.9 %collective-permute-start.11 = (bf16[256,640]{1,0:T(8,128)(2,1)S(1)}, bf16[256,640]{1,0:T(8,128)(2,1)S(1)}, u32[]{:S(2)}, u32[]{:S(2)}) collective-permute-start(bf16[256,640]{1,0:T(8,128)(2,1)S(1)} %get-tuple-element.28), channel_id=1, source_target_pairs={{0,8},{8,0},{16,24},{24,16},{32,40},{40,32},{48,56},{56,48},{64,72... | collective-permute-start | bytes 983048 | tf_op jit(solution)/shard_map/ppermute | solution.py:62
  89.3 1.5 %collective-permute-done.11.attb = bf16[256,640]{1,0:T(8,128)(2,1)S(1)} collective-permute-done((bf16[256,640]{1,0:T(8,128)(2,1)S(1)}, bf16[256,640]{1,0:T(8,128)(2,1)S(1)}, u32[]{:S(2)}, u32[]{:S(2)}) %collective-permute-start.11) | collective-permute-done | bytes 327712 | tf_op jit(solution)/shard_map/ppermute | solution.py:62
  90.9 0.0 collective-permute-done.12.wb
  90.9 3.0 %shard_map.94 = bf16[64,5120]{1,0:T(8,128)(2,1)} custom-call(s32[20]{0:T(128)S(1)} %pad_add_fusion.1.meta, bf16[256,640]{1,0:T(8,128)(2,1)S(1)} %get-tuple-element.27.atta, bf16[256,640]{1,0:T(8,128)(2,1)S(1)} %collective-permute-done.11.attb, bf16[1280,640]{1,0:T(8,128)(2,1)S(1)} %get-tuple-element.29.wa, bf16[1280,640]{1,0:T(8,128)(2,1)S(1)} %collective-permute-done.12.wb, ...), custom_call_target="tpu_custom_call" | custom-call | tf_op jit(solution)/shard_map/pallas_call | solution.py:306
  (18 shorter events, 0.1 us)
Async XLA Ops:
  2.9 33.2 %collective-permute-start = (bf16[320,2560]{1,0:T(8,128)(2,1)S(1)}, bf16[320,2560]{1,0:T(8,128)(2,1)S(1)}, u32[]{:S(2)}, u32[]{:S(2)}) collective-permute-start(bf16[320,2560]{1,0:T(8,128)(2,1)S(1)} %constant_dynamic-update-slice_fusion.own), channel_id=1, source_target_pairs={{0,257},{8,12},{16,273},{24,28},{32,289},{40,44},{48,305},{56,60},... | collective-permute-start | bytes 4915208 | tf_op jit(solution)/shard_map/ppermute | solution.py:62
  8.4 17.8 %copy-start.6 = (s32[64,1,7]{0,1,2:T(1,128)S(1)}, s32[64,1,7]{0,1,2:T(1,128)}, u32[]{:S(2)}) copy-start(s32[64,1,7]{0,1,2:T(1,128)} %param.16) | copy-start | bytes 5380
  8.5 34.7 %copy-start.5 = (s32[64,1,7,2]{0,3,2,1:T(2,128)S(1)}, s32[64,1,7,2]{0,3,2,1:T(2,128)}, u32[]{:S(2)}) copy-start(s32[64,1,7,2]{0,3,2,1:T(2,128)} %param.17) | copy-start | bytes 10756
  8.5 48.4 %copy-start.2 = (f32[1280]{0:T(1024)S(1)}, f32[1280]{0:T(1024)}, u32[]{:S(2)}) copy-start(f32[1280]{0:T(1024)} %param.10) | copy-start | bytes 15364
  9.4 34.5 %collective-permute-start.7 = (bf16[160,2560]{1,0:T(8,128)(2,1)}, bf16[160,2560]{1,0:T(8,128)(2,1)}, u32[]{:S(2)}, u32[]{:S(2)}) collective-permute-start(bf16[160,2560]{1,0:T(8,128)(2,1)} %pad_maximum_fusion.4), channel_id=1, source_target_pairs={{0,2},{8,14},{16,18},{24,30},{32,34},{40,46},{48,50},{56,62},{64,6... | collective-permute-start | bytes 2457608 | tf_op jit(solution)/shard_map/ppermute | solution.py:62
  14.1 12.3 %collective-permute-start.1 = (bf16[64,1280]{1,0:T(8,128)(2,1)}, bf16[64,1280]{1,0:T(8,128)(2,1)S(1)}, u32[]{:S(2)}, u32[]{:S(2)}) collective-permute-start(bf16[64,1280]{1,0:T(8,128)(2,1)} %get-tuple-element.45), channel_id=1, source_target_pairs={{0,8},{8,16},{16,24},{24,32},{32,40},{40,48},{48,56},{56,64},{64,7... | collective-permute-start | bytes 491528 | tf_op jit(solution)/shard_map/ppermute | solution.py:67
  19.1 13.5 %collective-permute-start.2 = (bf16[64,1280]{1,0:T(8,128)(2,1)}, bf16[64,1280]{1,0:T(8,128)(2,1)}, u32[]{:S(2)}, u32[]{:S(2)}) collective-permute-start(bf16[64,1280]{1,0:T(8,128)(2,1)} %get-tuple-element.44), channel_id=1, source_target_pairs={{0,16},{8,24},{16,32},{24,40},{32,48},{40,56},{48,64},{56,72},{64,... | collective-permute-start | bytes 491528 | tf_op jit(solution)/shard_map/ppermute | solution.py:67
  22.6 35.5 %collective-permute-start.3 = (bf16[64,1280]{1,0:T(8,128)(2,1)}, bf16[64,1280]{1,0:T(8,128)(2,1)}, u32[]{:S(2)}, u32[]{:S(2)}) collective-permute-start(bf16[64,1280]{1,0:T(8,128)(2,1)} %get-tuple-element.43), channel_id=1, source_target_pairs={{0,24},{8,32},{16,40},{24,48},{32,56},{40,64},{48,72},{56,80},{64,... | collective-permute-start | bytes 491528 | tf_op jit(solution)/shard_map/ppermute | solution.py:67
  36.0 33.0 %collective-permute-start.4 = (bf16[320,2560]{1,0:T(8,128)(2,1)S(1)}, bf16[320,2560]{1,0:T(8,128)(2,1)}, u32[]{:S(2)}, u32[]{:S(2)}) collective-permute-start(bf16[320,2560]{1,0:T(8,128)(2,1)S(1)} %collective-permute-done.b), channel_id=1, source_target_pairs={{0,2},{8,265},{16,18},{24,281},{32,34},{40,297},{48,50},{56,313},{... | collective-permute-start | bytes 4915208 | tf_op jit(solution)/shard_map/ppermute | solution.py:62
  40.9 29.3 %collective-permute-start.5 = (bf16[320,2560]{1,0:T(8,128)(2,1)S(1)}, bf16[320,2560]{1,0:T(8,128)(2,1)}, u32[]{:S(2)}, u32[]{:S(2)}) collective-permute-start(bf16[320,2560]{1,0:T(8,128)(2,1)S(1)} %collective-permute-done.b), channel_id=1, source_target_pairs={{0,6},{16,22},{32,38},{48,54},{64,70},{80,86},{96,102},{112,118},{... | collective-permute-start | bytes 4915208 | tf_op jit(solution)/shard_map/ppermute | solution.py:62
  43.9 22.0 %collective-permute-start.8 = (bf16[160,2560]{1,0:T(8,128)(2,1)}, bf16[160,2560]{1,0:T(8,128)(2,1)}, u32[]{:S(2)}, u32[]{:S(2)}) collective-permute-start(bf16[160,2560]{1,0:T(8,128)(2,1)} %collective-permute-done.7.a), channel_id=1, source_target_pairs={{0,16},{8,248},{16,32},{24,8},{32,48},{40,24},{48,64},{56,40},{64,... | collective-permute-start | bytes 2457608 | tf_op jit(solution)/shard_map/ppermute | solution.py:62
  56.8 1.4 %copy-start = (bf16[1,1,7,64,1280]{4,3,2,1,0:T(8,128)(2,1)S(1)}, bf16[1,1,7,64,1280]{4,3,2,1,0:T(8,128)(2,1)}, u32[]{:S(2)}) copy-start(bf16[1,1,7,64,1280]{4,3,2,1,0:T(8,128)(2,1)} %own.1) | copy-start | bytes 3440644
  60.2 11.4 %collective-permute-start.6 = (bf16[256,1280]{1,0:T(8,128)(2,1)S(1)}, bf16[256,1280]{1,0:T(8,128)(2,1)S(1)}, u32[]{:S(2)}, u32[]{:S(2)}) collective-permute-start(bf16[256,1280]{1,0:T(8,128)(2,1)S(1)} %get-tuple-element.22.xa), channel_id=1, source_target_pairs={{0,8},{8,0},{16,24},{24,16},{32,40},{40,32},{48,56},{56,48},{64,72... | collective-permute-start | bytes 1966088 | tf_op jit(solution)/shard_map/ppermute | solution.py:62
  67.1 6.9 %collective-permute-start.9 = (bf16[320,2560]{1,0:T(8,128)(2,1)S(1)}, bf16[320,2560]{1,0:T(8,128)(2,1)S(1)}, u32[]{:S(2)}, u32[]{:S(2)}) collective-permute-start(bf16[320,2560]{1,0:T(8,128)(2,1)S(1)} %pad_maximum_fusion.1), channel_id=1, source_target_pairs={{0,8},{8,0},{16,24},{24,16},{32,40},{40,32},{48,56},{56,48},{64,72... | collective-permute-start | bytes 4915208 | tf_op jit(solution)/shard_map/ppermute | solution.py:62
  71.6 10.4 %copy-start.1 = (f32[3840]{0:T(1024)S(1)}, f32[3840]{0:T(1024)}, u32[]{:S(2)}) copy-start(f32[3840]{0:T(1024)} %param.12) | copy-start | bytes 46084
  71.6 5.5 %collective-permute-start.10 = (bf16[320,2560]{1,0:T(8,128)(2,1)S(1)}, bf16[320,2560]{1,0:T(8,128)(2,1)S(1)}, u32[]{:S(2)}, u32[]{:S(2)}) collective-permute-start(bf16[320,2560]{1,0:T(8,128)(2,1)S(1)} %pad_maximum_fusion), channel_id=1, source_target_pairs={{0,8},{8,0},{16,24},{24,16},{32,40},{40,32},{48,56},{56,48},{64,72... | collective-permute-start | bytes 4915208 | tf_op jit(solution)/shard_map/ppermute | solution.py:62
  79.4 11.5 %collective-permute-start.12 = (bf16[1280,640]{1,0:T(8,128)(2,1)S(1)}, bf16[1280,640]{1,0:T(8,128)(2,1)S(1)}, u32[]{:S(2)}, u32[]{:S(2)}) collective-permute-start(bf16[1280,640]{1,0:T(8,128)(2,1)S(1)} %get-tuple-element.29.wa), channel_id=1, source_target_pairs={{0,8},{8,0},{16,24},{24,16},{32,40},{40,32},{48,56},{56,48},{64,72... | collective-permute-start | bytes 4915208 | tf_op jit(solution)/shard_map/ppermute | solution.py:62
  82.1 7.2 %copy-start.3 = (f32[1280]{0:T(1024)S(1)}, f32[1280]{0:T(1024)}, u32[]{:S(2)}) copy-start(f32[1280]{0:T(1024)} %param.14) | copy-start | bytes 15364
  82.1 7.2 %copy-start.4 = (f32[1280]{0:T(1024)S(1)}, f32[1280]{0:T(1024)}, u32[]{:S(2)}) copy-start(f32[1280]{0:T(1024)} %param.15) | copy-start | bytes 15364
  87.3 3.5 %collective-permute-start.11 = (bf16[256,640]{1,0:T(8,128)(2,1)S(1)}, bf16[256,640]{1,0:T(8,128)(2,1)S(1)}, u32[]{:S(2)}, u32[]{:S(2)}) collective-permute-start(bf16[256,640]{1,0:T(8,128)(2,1)S(1)} %get-tuple-element.28), channel_id=1, source_target_pairs={{0,8},{8,0},{16,24},{24,16},{32,40},{40,32},{48,56},{56,48},{64,72... | collective-permute-start | bytes 983048 | tf_op jit(solution)/shard_map/ppermute | solution.py:62

commit v8 on v7

--- a/solution.py
+++ b/solution.py
@@ -84,6 +84,23 @@
         x = placed[rows, :].astype(jnp.float32)
         ms = jnp.mean(x * x, axis=-1, keepdims=True)
         normed[rows, :] = (x * lax.rsqrt(ms + EPS) * gain[...]).astype(jnp.bfloat16)
+
+
+def halves_kernel(*refs):
+    sources, out, sems = refs[:-2], refs[-2], refs[-1]
+    copies, at = [], 0
+    for i, ref in enumerate(sources):
+        rows = ref.shape[0] // 2
+        copies.append(
+            pltpu.make_async_copy(
+                ref.at[pl.ds(rows, rows), :], out.at[pl.ds(at, rows), :], sems.at[i]
+            )
+        )
+        at += rows
+    for copy in copies:
+        copy.start()
+    for copy in copies:
+        copy.wait()
 
 
 def gather_kernel(meta, own, a, b, c, d, rest_a, early, late, _, w, wo, sems):
@@ -197,6 +214,9 @@
             out[:, pl.ds(i * D + n * 128, 128)] = jnp.where(live, part, 0.0).astype(jnp.bfloat16)
 
 
+COST = 2 * 10**10
+
+
 def vmem(n):
     return [pl.BlockSpec(memory_space=pltpu.VMEM)] * n
 
@@ -205,6 +225,20 @@
 SMALL = pltpu.CompilerParams(vmem_limit_bytes=4 * 1024 * 1024)
 SMEM = pl.BlockSpec(memory_space=pltpu.SMEM)
 PARAMS = pltpu.CompilerParams(vmem_limit_bytes=20 * 1024 * 1024)
+
+
+def gather_halves(*shards):
+    return pl.pallas_call(
+        halves_kernel,
+        out_shape=jax.ShapeDtypeStruct((NC * DEPTH, 4 * HALF), jnp.bfloat16),
+        in_specs=[ANY] * len(shards),
+        out_specs=vmem(1)[0],
+        scratch_shapes=[pltpu.SemaphoreType.DMA((len(shards),))],
+        cost_estimate=pl.CostEstimate(
+            flops=COST, bytes_accessed=4 * DEPTH * D, transcendentals=0
+        ),
+        compiler_params=SMALL,
+    )(*shards)
 
 
 def tables(route, groups, rank, x, yh):
@@ -250,9 +284,6 @@
     bias = jnp.concatenate(
         [lax.dynamic_slice_in_dim(b_qkv, j * D + half, HALF, 0) for j in range(3)]
     )
-    def halves_of(*shards):
-        return jnp.concatenate([value[value.shape[0] // 2 :] for value in shards], axis=0)
-
     got_b = send(piece, moves((0, 1), (2, 0)))
     near = rank // NC % 2 * PART
     part = jnp.concatenate(
@@ -264,7 +295,7 @@
     got_c = send(got_b, moves((1, 0), (0, 1)))
     got_d = send(got_b, moves((-1, 0)))
     rest_a = send(got_a, planes())
-    early = send(halves_of(got_a, rest_a, got_b), other_core())
+    early = send(gather_halves(got_a, rest_a, got_b), other_core())
 
     meta = tables(route, groups, rank, lane // NYH, lane % NYH)
 
@@ -277,7 +308,7 @@
         compiler_params=SMALL,
     )(meta, patches, *moved, norm_gain.reshape(1, D))
     normed_other = send(normed, other_core())
-    late, normed_other = lax.optimization_barrier((halves_of(got_c, got_d), normed_other))
+    late, normed_other = lax.optimization_barrier((gather_halves(got_c, got_d), normed_other))
     late = send(late, other_core())
 
     w, w_mine = pl.pallas_call(

time: 94.6 us -> 93.6 us (0.989)
  local copies, waits for them, and re-layouts: 9.89 us -> 4.13 us
  waiting for transfers between devices: 18.2 us -> 23.9 us
  starting transfers between devices: 50.3 us -> 47.9 us
  Pallas kernels: 12.5 us -> 14.3 us
    ppermute x10, waiting for transfers between devices: 12 us -> 23.9 us  [send(): return lax.ppermute(value, AXES, pairs)]
    ppermute x3, waiting for transfers between devices: 6.2 us -> 0.01 us  [by_rank(): lax.ppermute(value, 'dp', [(i, (i + by) % devices) for i in range(devices)])]
    slice x5 -> x0, local copies, waits for them, and re-layouts: 4.58 us -> none  [halves_of(): value[value.shape[0] // 2:]]
    ppermute x10, starting transfers between devices: 38.2 us -> 35.8 us  [send(): return lax.ppermute(value, AXES, pairs)]
    pallas_call x0 -> x2, Pallas kernels: none -> 1.63 us  [gather_halves(): pl.pallas_call(halves_kernel, out_shape=jax.ShapeDtypeStruct((NC * DEPTH,...]
    squeeze x1, local copies, waits for them, and re-layouts: 1.86 us -> 0.75 us  [on_device(): patches[0, 0, RECV + m]]
  transfers between devices with their start and end apart: 13 -> 13, of which waited for: 5 -> 5; matrix products, arithmetic and copies ran while one was open for 10% -> 4% of each run, Pallas kernels for 8% -> 10%
where the time goes in v8:
time: 93.6 us; the launch traced here: 93.1 us
  starting transfers between devices  47.9 us (51%)
  waiting for transfers between devices  23.9 us (26%)
  Pallas kernels  14.3 us (15%)
  local copies, waits for them, and re-layouts  4.13 us (4%)
  other arithmetic  2.35 us (3%)
    ppermute x10, starting transfers between devices, send(): return lax.ppermute(value, AXES, pairs)  35.8 us
    ppermute x10, waiting for transfers between devices, send(): return lax.ppermute(value, AXES, pairs)  23.9 us
    ppermute x3, starting transfers between devices, by_rank(): lax.ppermute(value, 'dp', [(i, (i + by) % devices) for i in range(devices)])  12.1 us
    pallas_call x1, Pallas kernels, on_device(): pl.pallas_call(attend_kernel, out_shape=[jax.ShapeDtypeStruct((ROWS, HALF...  5.38 us
    pallas_call x1, Pallas kernels, on_device(): pl.pallas_call(merge_kernel, out_shape=jax.ShapeDtypeStruct((ROWS // MERG...  2.97 us
    pallas_call x1, Pallas kernels, on_device(): pl.pallas_call(gather_kernel, out_shape=[jax.ShapeDtypeStruct((D, 3 * HAL...  2.21 us
    pallas_call x1, Pallas kernels, on_device(): pl.pallas_call(place_kernel, out_shape=[jax.ShapeDtypeStruct((ROWS, D), j...  2.07 us
  transfers between devices with their start and end apart: 13, of which 5 were waited for; matrix products, arithmetic and copies ran while one was open for 4% of the time, Pallas kernels for 10%

profile of v8, /device:TPU:1, one launch (start us, length us, event | category | flops | bytes accessed | tf_op | source)
XLA Modules:
  0.0 93.1 jit_solution(11864865111159368076)
XLA Ops:
  0.0 1.1 %dynamic-slice_bitcast_fusion = (bf16[160,640]{1,0:T(8,128)(2,1)S(1)}, bf16[160,640]{1,0:T(8,128)(2,1)S(1)}) fusion(bf16[1280,160]{0,1:T(8,128)(2,1)} %param.13, s32[]{:T(128)S(6)} %select_n.199, s32[]{:T(128)S(6)} %select_n.195), kind=kLoop, calls=%fused_computation.3 | loop fusion | bytes 819208 | tf_op jit(solution)/shard_map/dynamic_slice | solution.py:277
  1.1 1.5 %constant_dynamic-slice_fusion.4 = (bf16[160,640]{1,0:T(8,128)(2,1)S(1)}, bf16[160,640]{1,0:T(8,128)(2,1)S(1)}, bf16[160,640]{1,0:T(8,128)(2,1)S(1)}, bf16[160,6...) fusion(bf16[160,3840]{1,0:T(8,128)(2,1)} %param.11, s32[]{:T(128)S(6)} %select_n.196, ...), kind=kLoop, calls=%fused_computation.31 | loop fusion | bytes 2457624 | tf_op jit(solution)/shard_map/dynamic_slice | solution.py:276
  2.6 0.2 pad_maximum_fusion
  2.7 0.1 constant_dynamic-update-slice_fusion.1
  2.8 0.1 constant_dynamic-update-slice_fusion.own
  2.9 5.5 %collective-permute-start = (bf16[320,2560]{1,0:T(8,128)(2,1)S(1)}, bf16[320,2560]{1,0:T(8,128)(2,1)}, u32[]{:S(2)}, u32[]{:S(2)}) collective-permute-start(bf16[320,2560]{1,0:T(8,128)(2,1)S(1)} %constant_dynamic-update-slice_fusion.own), channel_id=1, source_target_pairs={{0,257},{8,12},{16,273},{24,28},{32,289},{40,44},{48,305},{56,60},... | collective-permute-start | bytes 4915208 | tf_op jit(solution)/shard_map/ppermute | solution.py:62
  8.4 0.0 copy-start
  8.4 0.1 constant_dynamic-slice_fusion.1
  8.5 0.0 copy-start.6
  8.5 0.0 copy-start.5
  8.5 0.0 copy-start.2
  8.5 1.0 %pad_maximum_fusion.2 = bf16[160,2560]{1,0:T(8,128)(2,1)} fusion(bf16[80,2560]{1,0:T(8,128)(2,1)S(1)} %get-tuple-element.36, bf16[80,2560]{1,0:T(8,128)(2,1)S(1)} %get-tuple-element.35), kind=kLoop, calls=%fused_computation.2 | loop fusion | flops 1638400 | bytes 1638400 | tf_op jit(solution)/shard_map/concatenate | solution.py:289
  9.5 2.8 %collective-permute-start.7 = (bf16[160,2560]{1,0:T(8,128)(2,1)}, bf16[160,2560]{1,0:T(8,128)(2,1)}, u32[]{:S(2)}, u32[]{:S(2)}) collective-permute-start(bf16[160,2560]{1,0:T(8,128)(2,1)} %pad_maximum_fusion.2), channel_id=1, source_target_pairs={{0,2},{8,14},{16,18},{24,30},{32,34},{40,46},{48,50},{56,62},{64,6... | collective-permute-start | bytes 2457608 | tf_op jit(solution)/shard_map/ppermute | solution.py:62
  12.2 0.0 copy-done
  12.2 0.8 slice_bitcast_fusion
  13.0 5.0 %collective-permute-start.1 = (bf16[64,1280]{1,0:T(8,128)(2,1)}, bf16[64,1280]{1,0:T(8,128)(2,1)S(1)}, u32[]{:S(2)}, u32[]{:S(2)}) collective-permute-start(bf16[64,1280]{1,0:T(8,128)(2,1)} %get-tuple-element.45), channel_id=1, source_target_pairs={{0,8},{8,16},{16,24},{24,32},{32,40},{40,48},{48,56},{56,64},{64,7... | collective-permute-start | bytes 491528 | tf_op jit(solution)/shard_map/ppermute | solution.py:67
  18.0 3.5 %collective-permute-start.2 = (bf16[64,1280]{1,0:T(8,128)(2,1)}, bf16[64,1280]{1,0:T(8,128)(2,1)S(1)}, u32[]{:S(2)}, u32[]{:S(2)}) collective-permute-start(bf16[64,1280]{1,0:T(8,128)(2,1)} %get-tuple-element.44), channel_id=1, source_target_pairs={{0,16},{8,24},{16,32},{24,40},{32,48},{40,56},{48,64},{56,72},{64,... | collective-permute-start | bytes 491528 | tf_op jit(solution)/shard_map/ppermute | solution.py:67
  21.6 3.6 %collective-permute-start.3 = (bf16[64,1280]{1,0:T(8,128)(2,1)S(1)}, bf16[64,1280]{1,0:T(8,128)(2,1)S(1)}, u32[]{:S(2)}, u32[]{:S(2)}) collective-permute-start(bf16[64,1280]{1,0:T(8,128)(2,1)S(1)} %get-tuple-element.43), channel_id=1, source_target_pairs={{0,24},{8,32},{16,40},{24,48},{32,56},{40,64},{48,72},{56,80},{64,... | collective-permute-start | bytes 491528 | tf_op jit(solution)/shard_map/ppermute | solution.py:67
  25.1 0.1 pad_add_fusion
  25.2 0.0 copy-done.6
  25.2 0.1 fusion.2
  25.3 0.3 select_reduce_fusion.1
  25.6 0.1 copy.13
  25.7 0.0 copy-done.5
  25.7 0.3 select_reduce_fusion
  26.0 0.2 slice_reduce_fusion
  26.2 0.2 fusion
  26.4 9.9 %collective-permute-done.7.refs_0_.a = bf16[160,2560]{1,0:T(8,128)(2,1)} collective-permute-done((bf16[160,2560]{1,0:T(8,128)(2,1)}, bf16[160,2560]{1,0:T(8,128)(2,1)}, u32[]{:S(2)}, u32[]{:S(2)}) %collective-permute-start.7) | collective-permute-done | bytes 819232 | tf_op jit(solution)/shard_map/ppermute | solution.py:62
  36.4 10.8 %collective-permute-start.8 = (bf16[160,2560]{1,0:T(8,128)(2,1)}, bf16[160,2560]{1,0:T(8,128)(2,1)}, u32[]{:S(2)}, u32[]{:S(2)}) collective-permute-start(bf16[160,2560]{1,0:T(8,128)(2,1)} %collective-permute-done.7.refs_0_.a), channel_id=1, source_target_pairs={{0,16},{8,248},{16,32},{24,8},{32,48},{40,24},{48,64},{56,40},{64,... | collective-permute-start | bytes 2457608 | tf_op jit(solution)/shard_map/ppermute | solution.py:62
  47.2 0.1 select_reduce_fusion.3
  47.4 0.1 stack.59
  47.5 0.1 stack.58
  47.6 0.0 copy-done.2
  47.7 0.1 pad_add_fusion.1.meta
  47.7 0.0 collective-permute-done.1.in0
  47.7 0.0 collective-permute-done.2.in1
  47.7 0.0 collective-permute-done.refs_2_.b
  47.8 4.6 %collective-permute-start.4 = (bf16[320,2560]{1,0:T(8,128)(2,1)}, bf16[320,2560]{1,0:T(8,128)(2,1)S(1)}, u32[]{:S(2)}, u32[]{:S(2)}) collective-permute-start(bf16[320,2560]{1,0:T(8,128)(2,1)} %collective-permute-done.refs_2_.b), channel_id=1, source_target_pairs={{0,2},{8,265},{16,18},{24,281},{32,34},{40,297},{48,50},{56,313},{... | collective-permute-start | bytes 4915208 | tf_op jit(solution)/shard_map/ppermute | solution.py:62
  52.4 0.8 collective-permute-start.5
  53.2 3.6 %collective-permute-done.8.refs_1_.rest_a = bf16[160,2560]{1,0:T(8,128)(2,1)} collective-permute-done((bf16[160,2560]{1,0:T(8,128)(2,1)}, bf16[160,2560]{1,0:T(8,128)(2,1)}, u32[]{:S(2)}, u32[]{:S(2)}) %collective-permute-start.8) | collective-permute-done | bytes 819232 | tf_op jit(solution)/shard_map/ppermute | solution.py:62
  56.8 1.4 %shard_map.93 = bf16[320,2560]{1,0:T(8,128)(2,1)S(1)} custom-call(bf16[160,2560]{1,0:T(8,128)(2,1)} %collective-permute-done.7.refs_0_.a, bf16[160,2560]{1,0:T(8,128)(2,1)} %collective-permute-done.8.refs_1_.rest_a, bf16[320,2560]{1,0:T(8,128)(2,1)} %collective-permute-done.refs_2_.b), custom_call_target="tpu_custom_call" | custom-call | flops 20000000000 | bytes 819200 | tf_op jit(solution)/shard_map/pallas_call | solution.py:231
  58.2 3.2 %collective-permute-start.9 = (bf16[320,2560]{1,0:T(8,128)(2,1)S(1)}, bf16[320,2560]{1,0:T(8,128)(2,1)S(1)}, u32[]{:S(2)}, u32[]{:S(2)}) collective-permute-start(bf16[320,2560]{1,0:T(8,128)(2,1)S(1)} %shard_map.93), channel_id=1, source_target_pairs={{0,8},{8,0},{16,24},{24,16},{32,40},{40,32},{48,56},{56,48},{64,72... | collective-permute-start | bytes 4915208 | tf_op jit(solution)/shard_map/ppermute | solution.py:62
  61.4 0.0 collective-permute-done.3.in2
  61.4 2.1 %shard_map.91 = (bf16[256,1280]{1,0:T(8,128)(2,1)S(1)}, bf16[256,1280]{1,0:T(8,128)(2,1)S(1)}) custom-call(s32[20]{0:T(128)S(1)} %pad_add_fusion.1.meta, bf16[1,1,7,64,1280]{4,3,2,1,0:T(8,128)(2,1)S(1)} %copy-done, bf16[64,1280]{1,0:T(8,128)(2,1)S(1)} %collective-permute-done.1.in0, bf16[64,1280]{1,0:T(8,128)(2,1)S(1)} %collective-permute-done.2.in1, ...), custom_call_target="tpu_custom_call" | custom-call | tf_op jit(solution)/shard_map/pallas_call | solution.py:302
  63.4 1.9 %collective-permute-start.6 = (bf16[256,1280]{1,0:T(8,128)(2,1)S(1)}, bf16[256,1280]{1,0:T(8,128)(2,1)S(1)}, u32[]{:S(2)}, u32[]{:S(2)}) collective-permute-start(bf16[256,1280]{1,0:T(8,128)(2,1)S(1)} %get-tuple-element.22.xa), channel_id=1, source_target_pairs={{0,8},{8,0},{16,24},{24,16},{32,40},{40,32},{48,56},{56,48},{64,72... | collective-permute-start | bytes 1966088 | tf_op jit(solution)/shard_map/ppermute | solution.py:62
  65.4 5.7 %collective-permute-done.4.refs_0_.c = bf16[320,2560]{1,0:T(8,128)(2,1)S(1)} collective-permute-done((bf16[320,2560]{1,0:T(8,128)(2,1)}, bf16[320,2560]{1,0:T(8,128)(2,1)S(1)}, u32[]{:S(2)}, u32[]{:S(2)}) %collective-permute-start.4) | collective-permute-done | bytes 1638432 | tf_op jit(solution)/shard_map/ppermute | solution.py:62
  71.1 0.0 collective-permute-done.5.refs_1_.d
  71.1 0.2 shard_map.92
  71.3 0.0 copy-start.1
  71.3 0.0 collective-permute-done.6._.xb
  71.3 1.9 %collective-permute-start.10 = (bf16[320,2560]{1,0:T(8,128)(2,1)S(1)}, bf16[320,2560]{1,0:T(8,128)(2,1)S(1)}, u32[]{:S(2)}, u32[]{:S(2)}) collective-permute-start(bf16[320,2560]{1,0:T(8,128)(2,1)S(1)} %shard_map.92), channel_id=1, source_target_pairs={{0,8},{8,0},{16,24},{24,16},{32,40},{40,32},{48,56},{56,48},{64,72... | collective-permute-start | bytes 4915208 | tf_op jit(solution)/shard_map/ppermute | solution.py:62
  73.3 0.0 collective-permute-done.9.early
  73.3 3.5 %collective-permute-done.10.late = bf16[320,2560]{1,0:T(8,128)(2,1)S(1)} collective-permute-done((bf16[320,2560]{1,0:T(8,128)(2,1)S(1)}, bf16[320,2560]{1,0:T(8,128)(2,1)S(1)}, u32[]{:S(2)}, u32[]{:S(2)}) %collective-permute-start.10) | collective-permute-done | bytes 1638432 | tf_op jit(solution)/shard_map/ppermute | solution.py:62
  76.7 2.2 %shard_map.94 = (bf16[1280,1920]{1,0:T(8,128)(2,1)S(1)}, bf16[1280,640]{1,0:T(8,128)(2,1)S(1)}) custom-call(s32[20]{0:T(128)S(1)} %pad_add_fusion.1.meta, bf16[320,2560]{1,0:T(8,128)(2,1)S(1)} %constant_dynamic-update-slice_fusion.own, bf16[160,2560]{1,0:T(8,128)(2,1)} %collective-permute-done.7.refs_0_.a, bf16[320,2560]{1,0:T(8,128)(2,1)} %collective-permute-done.refs_2_.b, ...), custom_call_target="tpu_custom_call" | custom-call | tf_op jit(solution)/shard_map/pallas_call | solution.py:314
  79.0 2.0 %collective-permute-start.12 = (bf16[1280,640]{1,0:T(8,128)(2,1)S(1)}, bf16[1280,640]{1,0:T(8,128)(2,1)S(1)}, u32[]{:S(2)}, u32[]{:S(2)}) collective-permute-start(bf16[1280,640]{1,0:T(8,128)(2,1)S(1)} %get-tuple-element.29.wa), channel_id=1, source_target_pairs={{0,8},{8,0},{16,24},{24,16},{32,40},{40,32},{48,56},{56,48},{64,72... | collective-permute-start | bytes 4915208 | tf_op jit(solution)/shard_map/ppermute | solution.py:62
  81.0 0.0 copy-done.1
  81.0 0.1 fusion.4
  81.1 0.0 copy-start.3
  81.2 0.0 copy-start.4
  81.2 5.4 %shard_map.95 = (bf16[256,640]{1,0:T(8,128)(2,1)S(1)}, bf16[256,640]{1,0:T(8,128)(2,1)S(1)}) custom-call(s32[20]{0:T(128)S(1)} %pad_add_fusion.1.meta, bf16[256,1280]{1,0:T(8,128)(2,1)S(1)} %get-tuple-element.22.xa, bf16[256,1280]{1,0:T(8,128)(2,1)S(1)} %collective-permute-done.6._.xb, f32[1,1920]{1,0:T(1,128)S(1)} %reshape.81.bias, ...), custom_call_target="tpu_custom_call" | custom-call | tf_op jit(solution)/shard_map/pallas_call | solution.py:327
  86.6 2.3 %collective-permute-start.11 = (bf16[256,640]{1,0:T(8,128)(2,1)S(1)}, bf16[256,640]{1,0:T(8,128)(2,1)S(1)}, u32[]{:S(2)}, u32[]{:S(2)}) collective-permute-start(bf16[256,640]{1,0:T(8,128)(2,1)S(1)} %get-tuple-element.28), channel_id=1, source_target_pairs={{0,8},{8,0},{16,24},{24,16},{32,40},{40,32},{48,56},{56,48},{64,72... | collective-permute-start | bytes 983048 | tf_op jit(solution)/shard_map/ppermute | solution.py:62
  88.9 1.2 %collective-permute-done.11.attb = bf16[256,640]{1,0:T(8,128)(2,1)S(1)} collective-permute-done((bf16[256,640]{1,0:T(8,128)(2,1)S(1)}, bf16[256,640]{1,0:T(8,128)(2,1)S(1)}, u32[]{:S(2)}, u32[]{:S(2)}) %collective-permute-start.11) | collective-permute-done | bytes 327712 | tf_op jit(solution)/shard_map/ppermute | solution.py:62
  90.1 0.0 collective-permute-done.12.wb
  90.1 3.0 %shard_map.96 = bf16[64,5120]{1,0:T(8,128)(2,1)} custom-call(s32[20]{0:T(128)S(1)} %pad_add_fusion.1.meta, bf16[256,640]{1,0:T(8,128)(2,1)S(1)} %get-tuple-element.27.atta, bf16[256,640]{1,0:T(8,128)(2,1)S(1)} %collective-permute-done.11.attb, bf16[1280,640]{1,0:T(8,128)(2,1)S(1)} %get-tuple-element.29.wa, bf16[1280,640]{1,0:T(8,128)(2,1)S(1)} %collective-permute-done.12.wb, ...), custom_call_target="tpu_custom_call" | custom-call | tf_op jit(solution)/shard_map/pallas_call | solution.py:337
  (13 shorter events, 0.1 us)
Async XLA Ops:
  2.9 44.9 %collective-permute-start = (bf16[320,2560]{1,0:T(8,128)(2,1)S(1)}, bf16[320,2560]{1,0:T(8,128)(2,1)}, u32[]{:S(2)}, u32[]{:S(2)}) collective-permute-start(bf16[320,2560]{1,0:T(8,128)(2,1)S(1)} %constant_dynamic-update-slice_fusion.own), channel_id=1, source_target_pairs={{0,257},{8,12},{16,273},{24,28},{32,289},{40,44},{48,305},{56,60},... | collective-permute-start | bytes 4915208 | tf_op jit(solution)/shard_map/ppermute | solution.py:62
  8.4 3.9 %copy-start = (bf16[1,1,7,64,1280]{4,3,2,1,0:T(8,128)(2,1)S(1)}, bf16[1,1,7,64,1280]{4,3,2,1,0:T(8,128)(2,1)}, u32[]{:S(2)}) copy-start(bf16[1,1,7,64,1280]{4,3,2,1,0:T(8,128)(2,1)} %own.1) | copy-start | bytes 3440644
  8.5 16.7 %copy-start.6 = (s32[64,1,7]{0,1,2:T(1,128)S(1)}, s32[64,1,7]{0,1,2:T(1,128)}, u32[]{:S(2)}) copy-start(s32[64,1,7]{0,1,2:T(1,128)} %param.16) | copy-start | bytes 5380
  8.5 17.2 %copy-start.5 = (s32[64,1,7,2]{0,3,2,1:T(2,128)S(1)}, s32[64,1,7,2]{0,3,2,1:T(2,128)}, u32[]{:S(2)}) copy-start(s32[64,1,7,2]{0,3,2,1:T(2,128)} %param.17) | copy-start | bytes 10756
  8.5 39.2 %copy-start.2 = (f32[1280]{0:T(1024)S(1)}, f32[1280]{0:T(1024)}, u32[]{:S(2)}) copy-start(f32[1280]{0:T(1024)} %param.10) | copy-start | bytes 15364
  9.5 26.9 %collective-permute-start.7 = (bf16[160,2560]{1,0:T(8,128)(2,1)}, bf16[160,2560]{1,0:T(8,128)(2,1)}, u32[]{:S(2)}, u32[]{:S(2)}) collective-permute-start(bf16[160,2560]{1,0:T(8,128)(2,1)} %pad_maximum_fusion.2), channel_id=1, source_target_pairs={{0,2},{8,14},{16,18},{24,30},{32,34},{40,46},{48,50},{56,62},{64,6... | collective-permute-start | bytes 2457608 | tf_op jit(solution)/shard_map/ppermute | solution.py:62
  13.0 34.7 %collective-permute-start.1 = (bf16[64,1280]{1,0:T(8,128)(2,1)}, bf16[64,1280]{1,0:T(8,128)(2,1)S(1)}, u32[]{:S(2)}, u32[]{:S(2)}) collective-permute-start(bf16[64,1280]{1,0:T(8,128)(2,1)} %get-tuple-element.45), channel_id=1, source_target_pairs={{0,8},{8,16},{16,24},{24,32},{32,40},{40,48},{48,56},{56,64},{64,7... | collective-permute-start | bytes 491528 | tf_op jit(solution)/shard_map/ppermute | solution.py:67
  18.0 29.7 %collective-permute-start.2 = (bf16[64,1280]{1,0:T(8,128)(2,1)}, bf16[64,1280]{1,0:T(8,128)(2,1)S(1)}, u32[]{:S(2)}, u32[]{:S(2)}) collective-permute-start(bf16[64,1280]{1,0:T(8,128)(2,1)} %get-tuple-element.44), channel_id=1, source_target_pairs={{0,16},{8,24},{16,32},{24,40},{32,48},{40,56},{48,64},{56,72},{64,... | collective-permute-start | bytes 491528 | tf_op jit(solution)/shard_map/ppermute | solution.py:67
  21.6 39.8 %collective-permute-start.3 = (bf16[64,1280]{1,0:T(8,128)(2,1)S(1)}, bf16[64,1280]{1,0:T(8,128)(2,1)S(1)}, u32[]{:S(2)}, u32[]{:S(2)}) collective-permute-start(bf16[64,1280]{1,0:T(8,128)(2,1)S(1)} %get-tuple-element.43), channel_id=1, source_target_pairs={{0,24},{8,32},{16,40},{24,48},{32,56},{40,64},{48,72},{56,80},{64,... | collective-permute-start | bytes 491528 | tf_op jit(solution)/shard_map/ppermute | solution.py:67
  36.4 20.4 %collective-permute-start.8 = (bf16[160,2560]{1,0:T(8,128)(2,1)}, bf16[160,2560]{1,0:T(8,128)(2,1)}, u32[]{:S(2)}, u32[]{:S(2)}) collective-permute-start(bf16[160,2560]{1,0:T(8,128)(2,1)} %collective-permute-done.7.refs_0_.a), channel_id=1, source_target_pairs={{0,16},{8,248},{16,32},{24,8},{32,48},{40,24},{48,64},{56,40},{64,... | collective-permute-start | bytes 2457608 | tf_op jit(solution)/shard_map/ppermute | solution.py:62
  47.8 23.4 %collective-permute-start.4 = (bf16[320,2560]{1,0:T(8,128)(2,1)}, bf16[320,2560]{1,0:T(8,128)(2,1)S(1)}, u32[]{:S(2)}, u32[]{:S(2)}) collective-permute-start(bf16[320,2560]{1,0:T(8,128)(2,1)} %collective-permute-done.refs_2_.b), channel_id=1, source_target_pairs={{0,2},{8,265},{16,18},{24,281},{32,34},{40,297},{48,50},{56,313},{... | collective-permute-start | bytes 4915208 | tf_op jit(solution)/shard_map/ppermute | solution.py:62
  52.4 18.7 %collective-permute-start.5 = (bf16[320,2560]{1,0:T(8,128)(2,1)}, bf16[320,2560]{1,0:T(8,128)(2,1)S(1)}, u32[]{:S(2)}, u32[]{:S(2)}) collective-permute-start(bf16[320,2560]{1,0:T(8,128)(2,1)} %collective-permute-done.refs_2_.b), channel_id=1, source_target_pairs={{0,6},{16,22},{32,38},{48,54},{64,70},{80,86},{96,102},{112,118},{... | collective-permute-start | bytes 4915208 | tf_op jit(solution)/shard_map/ppermute | solution.py:62
  58.2 15.1 %collective-permute-start.9 = (bf16[320,2560]{1,0:T(8,128)(2,1)S(1)}, bf16[320,2560]{1,0:T(8,128)(2,1)S(1)}, u32[]{:S(2)}, u32[]{:S(2)}) collective-permute-start(bf16[320,2560]{1,0:T(8,128)(2,1)S(1)} %shard_map.93), channel_id=1, source_target_pairs={{0,8},{8,0},{16,24},{24,16},{32,40},{40,32},{48,56},{56,48},{64,72... | collective-permute-start | bytes 4915208 | tf_op jit(solution)/shard_map/ppermute | solution.py:62
  63.4 7.9 %collective-permute-start.6 = (bf16[256,1280]{1,0:T(8,128)(2,1)S(1)}, bf16[256,1280]{1,0:T(8,128)(2,1)S(1)}, u32[]{:S(2)}, u32[]{:S(2)}) collective-permute-start(bf16[256,1280]{1,0:T(8,128)(2,1)S(1)} %get-tuple-element.22.xa), channel_id=1, source_target_pairs={{0,8},{8,0},{16,24},{24,16},{32,40},{40,32},{48,56},{56,48},{64,72... | collective-permute-start | bytes 1966088 | tf_op jit(solution)/shard_map/ppermute | solution.py:62
  71.3 9.7 %copy-start.1 = (f32[3840]{0:T(1024)S(1)}, f32[3840]{0:T(1024)}, u32[]{:S(2)}) copy-start(f32[3840]{0:T(1024)} %param.12) | copy-start | bytes 46084
  71.3 5.4 %collective-permute-start.10 = (bf16[320,2560]{1,0:T(8,128)(2,1)S(1)}, bf16[320,2560]{1,0:T(8,128)(2,1)S(1)}, u32[]{:S(2)}, u32[]{:S(2)}) collective-permute-start(bf16[320,2560]{1,0:T(8,128)(2,1)S(1)} %shard_map.92), channel_id=1, source_target_pairs={{0,8},{8,0},{16,24},{24,16},{32,40},{40,32},{48,56},{56,48},{64,72... | collective-permute-start | bytes 4915208 | tf_op jit(solution)/shard_map/ppermute | solution.py:62
  79.0 11.1 %collective-permute-start.12 = (bf16[1280,640]{1,0:T(8,128)(2,1)S(1)}, bf16[1280,640]{1,0:T(8,128)(2,1)S(1)}, u32[]{:S(2)}, u32[]{:S(2)}) collective-permute-start(bf16[1280,640]{1,0:T(8,128)(2,1)S(1)} %get-tuple-element.29.wa), channel_id=1, source_target_pairs={{0,8},{8,0},{16,24},{24,16},{32,40},{40,32},{48,56},{56,48},{64,72... | collective-permute-start | bytes 4915208 | tf_op jit(solution)/shard_map/ppermute | solution.py:62
  81.1 7.7 %copy-start.3 = (f32[1280]{0:T(1024)S(1)}, f32[1280]{0:T(1024)}, u32[]{:S(2)}) copy-start(f32[1280]{0:T(1024)} %param.14) | copy-start | bytes 15364
  81.2 7.7 %copy-start.4 = (f32[1280]{0:T(1024)S(1)}, f32[1280]{0:T(1024)}, u32[]{:S(2)}) copy-start(f32[1280]{0:T(1024)} %param.15) | copy-start | bytes 15364
  86.6 3.5 %collective-permute-start.11 = (bf16[256,640]{1,0:T(8,128)(2,1)S(1)}, bf16[256,640]{1,0:T(8,128)(2,1)S(1)}, u32[]{:S(2)}, u32[]{:S(2)}) collective-permute-start(bf16[256,640]{1,0:T(8,128)(2,1)S(1)} %get-tuple-element.28), channel_id=1, source_target_pairs={{0,8},{8,0},{16,24},{24,16},{32,40},{40,32},{48,56},{56,48},{64,72... | collective-permute-start | bytes 983048 | tf_op jit(solution)/shard_map/ppermute | solution.py:62

commit v9 on v8

--- a/solution.py
+++ b/solution.py
@@ -51,7 +51,7 @@
 
 
 def planes():
-    return perm(lambda x, yh, yl, z, c: (x, yh, yl, z - 1 if c else z + 1, c))
+    return perm(lambda x, yh, yl, z, c: (x, yh, yl, z - 1, c))
 
 
 def other_core():

time: 93.6 us -> 97.6 us (1.043)
  waiting for transfers between devices: 23.9 us -> 28.4 us
    ppermute x10, waiting for transfers between devices: 23.9 us -> 28.3 us  [send(): return lax.ppermute(value, AXES, pairs)]
  transfers between devices with their start and end apart: 13 -> 13, of which waited for: 5 -> 5; matrix products, arithmetic and copies ran while one was open for 4% -> 4% of each run, Pallas kernels for 10% -> 9%
where the time goes in v9:
time: 97.6 us; the launch traced here: 97.1 us
  starting transfers between devices  47.4 us (49%)
  waiting for transfers between devices  28.4 us (29%)
  Pallas kernels  14.3 us (15%)
  local copies, waits for them, and re-layouts  4.13 us (4%)
  other arithmetic  2.35 us (2%)
    ppermute x10, starting transfers between devices, send(): return lax.ppermute(value, AXES, pairs)  35.3 us
    ppermute x10, waiting for transfers between devices, send(): return lax.ppermute(value, AXES, pairs)  28.3 us
    ppermute x3, starting transfers between devices, by_rank(): lax.ppermute(value, 'dp', [(i, (i + by) % devices) for i in range(devices)])  12.1 us
    pallas_call x1, Pallas kernels, on_device(): pl.pallas_call(attend_kernel, out_shape=[jax.ShapeDtypeStruct((ROWS, HALF...  5.38 us
    pallas_call x1, Pallas kernels, on_device(): pl.pallas_call(merge_kernel, out_shape=jax.ShapeDtypeStruct((ROWS // MERG...  2.98 us
    pallas_call x1, Pallas kernels, on_device(): pl.pallas_call(gather_kernel, out_shape=[jax.ShapeDtypeStruct((D, 3 * HAL...  2.21 us
    pallas_call x1, Pallas kernels, on_device(): pl.pallas_call(place_kernel, out_shape=[jax.ShapeDtypeStruct((ROWS, D), j...  2.07 us
  transfers between devices with their start and end apart: 13, of which 5 were waited for; matrix products, arithmetic and copies ran while one was open for 4% of the time, Pallas kernels for 9%

profile of v9, /device:TPU:1, one launch (start us, length us, event | category | flops | bytes accessed | tf_op | source)
XLA Modules:
  0.0 97.1 jit_solution(11495337574091872121)
XLA Ops:
  0.0 1.1 %dynamic-slice_bitcast_fusion = (bf16[160,640]{1,0:T(8,128)(2,1)S(1)}, bf16[160,640]{1,0:T(8,128)(2,1)S(1)}) fusion(bf16[1280,160]{0,1:T(8,128)(2,1)} %param.13, s32[]{:T(128)S(6)} %select_n.199, s32[]{:T(128)S(6)} %select_n.195), kind=kLoop, calls=%fused_computation.3 | loop fusion | bytes 819208 | tf_op jit(solution)/shard_map/dynamic_slice | solution.py:277
  1.1 1.5 %constant_dynamic-slice_fusion.4 = (bf16[160,640]{1,0:T(8,128)(2,1)S(1)}, bf16[160,640]{1,0:T(8,128)(2,1)S(1)}, bf16[160,640]{1,0:T(8,128)(2,1)S(1)}, bf16[160,6...) fusion(bf16[160,3840]{1,0:T(8,128)(2,1)} %param.11, s32[]{:T(128)S(6)} %select_n.196, ...), kind=kLoop, calls=%fused_computation.31 | loop fusion | bytes 2457624 | tf_op jit(solution)/shard_map/dynamic_slice | solution.py:276
  2.6 0.2 pad_maximum_fusion
  2.7 0.1 constant_dynamic-update-slice_fusion.1
  2.8 0.1 constant_dynamic-update-slice_fusion.own
  2.9 5.5 %collective-permute-start = (bf16[320,2560]{1,0:T(8,128)(2,1)S(1)}, bf16[320,2560]{1,0:T(8,128)(2,1)}, u32[]{:S(2)}, u32[]{:S(2)}) collective-permute-start(bf16[320,2560]{1,0:T(8,128)(2,1)S(1)} %constant_dynamic-update-slice_fusion.own), channel_id=1, source_target_pairs={{0,257},{8,12},{16,273},{24,28},{32,289},{40,44},{48,305},{56,60},... | collective-permute-start | bytes 4915208 | tf_op jit(solution)/shard_map/ppermute | solution.py:62
  8.4 0.0 copy-start
  8.4 0.1 constant_dynamic-slice_fusion.1
  8.5 0.0 copy-start.6
  8.5 0.0 copy-start.5
  8.5 0.0 copy-start.2
  8.5 1.0 pad_maximum_fusion.2
  9.5 2.8 %collective-permute-start.7 = (bf16[160,2560]{1,0:T(8,128)(2,1)}, bf16[160,2560]{1,0:T(8,128)(2,1)}, u32[]{:S(2)}, u32[]{:S(2)}) collective-permute-start(bf16[160,2560]{1,0:T(8,128)(2,1)} %pad_maximum_fusion.2), channel_id=1, source_target_pairs={{0,2},{8,14},{16,18},{24,30},{32,34},{40,46},{48,50},{56,62},{64,6... | collective-permute-start | bytes 2457608 | tf_op jit(solution)/shard_map/ppermute | solution.py:62
  12.2 0.0 copy-done
  12.2 0.8 slice_bitcast_fusion
  13.0 5.0 %collective-permute-start.1 = (bf16[64,1280]{1,0:T(8,128)(2,1)}, bf16[64,1280]{1,0:T(8,128)(2,1)S(1)}, u32[]{:S(2)}, u32[]{:S(2)}) collective-permute-start(bf16[64,1280]{1,0:T(8,128)(2,1)} %get-tuple-element.45), channel_id=1, source_target_pairs={{0,8},{8,16},{16,24},{24,32},{32,40},{40,48},{48,56},{56,64},{64,7... | collective-permute-start | bytes 491528 | tf_op jit(solution)/shard_map/ppermute | solution.py:67
  18.0 3.5 %collective-permute-start.2 = (bf16[64,1280]{1,0:T(8,128)(2,1)}, bf16[64,1280]{1,0:T(8,128)(2,1)S(1)}, u32[]{:S(2)}, u32[]{:S(2)}) collective-permute-start(bf16[64,1280]{1,0:T(8,128)(2,1)} %get-tuple-element.44), channel_id=1, source_target_pairs={{0,16},{8,24},{16,32},{24,40},{32,48},{40,56},{48,64},{56,72},{64,... | collective-permute-start | bytes 491528 | tf_op jit(solution)/shard_map/ppermute | solution.py:67
  21.6 3.6 %collective-permute-start.3 = (bf16[64,1280]{1,0:T(8,128)(2,1)S(1)}, bf16[64,1280]{1,0:T(8,128)(2,1)S(1)}, u32[]{:S(2)}, u32[]{:S(2)}) collective-permute-start(bf16[64,1280]{1,0:T(8,128)(2,1)S(1)} %get-tuple-element.43), channel_id=1, source_target_pairs={{0,24},{8,32},{16,40},{24,48},{32,56},{40,64},{48,72},{56,80},{64,... | collective-permute-start | bytes 491528 | tf_op jit(solution)/shard_map/ppermute | solution.py:67
  25.1 0.1 pad_add_fusion
  25.2 0.0 copy-done.6
  25.2 0.1 fusion.2
  25.3 0.3 select_reduce_fusion.1
  25.6 0.1 copy.13
  25.7 0.0 copy-done.5
  25.7 0.3 select_reduce_fusion
  26.0 0.2 slice_reduce_fusion
  26.2 0.2 fusion
  26.4 9.9 %collective-permute-done.7.refs_0_.a = bf16[160,2560]{1,0:T(8,128)(2,1)} collective-permute-done((bf16[160,2560]{1,0:T(8,128)(2,1)}, bf16[160,2560]{1,0:T(8,128)(2,1)}, u32[]{:S(2)}, u32[]{:S(2)}) %collective-permute-start.7) | collective-permute-done | bytes 819232 | tf_op jit(solution)/shard_map/ppermute | solution.py:62
  36.4 10.8 %collective-permute-start.8 = (bf16[160,2560]{1,0:T(8,128)(2,1)}, bf16[160,2560]{1,0:T(8,128)(2,1)}, u32[]{:S(2)}, u32[]{:S(2)}) collective-permute-start(bf16[160,2560]{1,0:T(8,128)(2,1)} %collective-permute-done.7.refs_0_.a), channel_id=1, source_target_pairs={{0,240},{8,248},{16,0},{24,8},{32,16},{40,24},{48,32},{56,40},{64,... | collective-permute-start | bytes 2457608 | tf_op jit(solution)/shard_map/ppermute | solution.py:62
  47.2 0.1 select_reduce_fusion.3
  47.4 0.1 stack.59
  47.5 0.1 stack.58
  47.6 0.0 copy-done.2
  47.7 0.1 pad_add_fusion.1.meta
  47.7 0.0 collective-permute-done.1.in0
  47.7 0.0 collective-permute-done.2.in1
  47.7 0.0 collective-permute-done.refs_2_.b
  47.8 4.6 %collective-permute-start.4 = (bf16[320,2560]{1,0:T(8,128)(2,1)}, bf16[320,2560]{1,0:T(8,128)(2,1)S(1)}, u32[]{:S(2)}, u32[]{:S(2)}) collective-permute-start(bf16[320,2560]{1,0:T(8,128)(2,1)} %collective-permute-done.refs_2_.b), channel_id=1, source_target_pairs={{0,2},{8,265},{16,18},{24,281},{32,34},{40,297},{48,50},{56,313},{... | collective-permute-start | bytes 4915208 | tf_op jit(solution)/shard_map/ppermute | solution.py:62
  52.4 0.8 collective-permute-start.5
  53.2 12.1 %collective-permute-done.8.refs_1_.rest_a = bf16[160,2560]{1,0:T(8,128)(2,1)} collective-permute-done((bf16[160,2560]{1,0:T(8,128)(2,1)}, bf16[160,2560]{1,0:T(8,128)(2,1)}, u32[]{:S(2)}, u32[]{:S(2)}) %collective-permute-start.8) | collective-permute-done | bytes 819232 | tf_op jit(solution)/shard_map/ppermute | solution.py:62
  65.2 1.4 %shard_map.93 = bf16[320,2560]{1,0:T(8,128)(2,1)S(1)} custom-call(bf16[160,2560]{1,0:T(8,128)(2,1)} %collective-permute-done.7.refs_0_.a, bf16[160,2560]{1,0:T(8,128)(2,1)} %collective-permute-done.8.refs_1_.rest_a, bf16[320,2560]{1,0:T(8,128)(2,1)} %collective-permute-done.refs_2_.b), custom_call_target="tpu_custom_call" | custom-call | flops 20000000000 | bytes 819200 | tf_op jit(solution)/shard_map/pallas_call | solution.py:231
  66.7 2.6 %collective-permute-start.9 = (bf16[320,2560]{1,0:T(8,128)(2,1)S(1)}, bf16[320,2560]{1,0:T(8,128)(2,1)S(1)}, u32[]{:S(2)}, u32[]{:S(2)}) collective-permute-start(bf16[320,2560]{1,0:T(8,128)(2,1)S(1)} %shard_map.93), channel_id=1, source_target_pairs={{0,8},{8,0},{16,24},{24,16},{32,40},{40,32},{48,56},{56,48},{64,72... | collective-permute-start | bytes 4915208 | tf_op jit(solution)/shard_map/ppermute | solution.py:62
  69.3 0.0 collective-permute-done.3.in2
  69.3 2.1 %shard_map.91 = (bf16[256,1280]{1,0:T(8,128)(2,1)S(1)}, bf16[256,1280]{1,0:T(8,128)(2,1)S(1)}) custom-call(s32[20]{0:T(128)S(1)} %pad_add_fusion.1.meta, bf16[1,1,7,64,1280]{4,3,2,1,0:T(8,128)(2,1)S(1)} %copy-done, bf16[64,1280]{1,0:T(8,128)(2,1)S(1)} %collective-permute-done.1.in0, bf16[64,1280]{1,0:T(8,128)(2,1)S(1)} %collective-permute-done.2.in1, ...), custom_call_target="tpu_custom_call" | custom-call | tf_op jit(solution)/shard_map/pallas_call | solution.py:302
  71.4 1.9 %collective-permute-start.6 = (bf16[256,1280]{1,0:T(8,128)(2,1)S(1)}, bf16[256,1280]{1,0:T(8,128)(2,1)S(1)}, u32[]{:S(2)}, u32[]{:S(2)}) collective-permute-start(bf16[256,1280]{1,0:T(8,128)(2,1)S(1)} %get-tuple-element.22.xa), channel_id=1, source_target_pairs={{0,8},{8,0},{16,24},{24,16},{32,40},{40,32},{48,56},{56,48},{64,72... | collective-permute-start | bytes 1966088 | tf_op jit(solution)/shard_map/ppermute | solution.py:62
  73.3 0.0 collective-permute-done.4.refs_0_.c
  73.3 0.0 collective-permute-done.5.refs_1_.d
  73.3 0.2 shard_map.92
  73.5 0.0 copy-start.1
  73.6 1.8 %collective-permute-done.6._.xb = bf16[256,1280]{1,0:T(8,128)(2,1)S(1)} collective-permute-done((bf16[256,1280]{1,0:T(8,128)(2,1)S(1)}, bf16[256,1280]{1,0:T(8,128)(2,1)S(1)}, u32[]{:S(2)}, u32[]{:S(2)}) %collective-permute-start.6) | collective-permute-done | bytes 655392 | tf_op jit(solution)/shard_map/ppermute | solution.py:62
  75.4 2.0 %collective-permute-start.10 = (bf16[320,2560]{1,0:T(8,128)(2,1)S(1)}, bf16[320,2560]{1,0:T(8,128)(2,1)S(1)}, u32[]{:S(2)}, u32[]{:S(2)}) collective-permute-start(bf16[320,2560]{1,0:T(8,128)(2,1)S(1)} %shard_map.92), channel_id=1, source_target_pairs={{0,8},{8,0},{16,24},{24,16},{32,40},{40,32},{48,56},{56,48},{64,72... | collective-permute-start | bytes 4915208 | tf_op jit(solution)/shard_map/ppermute | solution.py:62
  77.4 0.0 collective-permute-done.9.early
  77.4 3.3 %collective-permute-done.10.late = bf16[320,2560]{1,0:T(8,128)(2,1)S(1)} collective-permute-done((bf16[320,2560]{1,0:T(8,128)(2,1)S(1)}, bf16[320,2560]{1,0:T(8,128)(2,1)S(1)}, u32[]{:S(2)}, u32[]{:S(2)}) %collective-permute-start.10) | collective-permute-done | bytes 1638432 | tf_op jit(solution)/shard_map/ppermute | solution.py:62
  80.7 2.2 %shard_map.94 = (bf16[1280,1920]{1,0:T(8,128)(2,1)S(1)}, bf16[1280,640]{1,0:T(8,128)(2,1)S(1)}) custom-call(s32[20]{0:T(128)S(1)} %pad_add_fusion.1.meta, bf16[320,2560]{1,0:T(8,128)(2,1)S(1)} %constant_dynamic-update-slice_fusion.own, bf16[160,2560]{1,0:T(8,128)(2,1)} %collective-permute-done.7.refs_0_.a, bf16[320,2560]{1,0:T(8,128)(2,1)} %collective-permute-done.refs_2_.b, ...), custom_call_target="tpu_custom_call" | custom-call | tf_op jit(solution)/shard_map/pallas_call | solution.py:314
  83.0 2.0 %collective-permute-start.12 = (bf16[1280,640]{1,0:T(8,128)(2,1)S(1)}, bf16[1280,640]{1,0:T(8,128)(2,1)S(1)}, u32[]{:S(2)}, u32[]{:S(2)}) collective-permute-start(bf16[1280,640]{1,0:T(8,128)(2,1)S(1)} %get-tuple-element.29.wa), channel_id=1, source_target_pairs={{0,8},{8,0},{16,24},{24,16},{32,40},{40,32},{48,56},{56,48},{64,72... | collective-permute-start | bytes 4915208 | tf_op jit(solution)/shard_map/ppermute | solution.py:62
  85.0 0.0 copy-done.1
  85.0 0.1 fusion.4
  85.1 0.0 copy-start.3
  85.2 0.0 copy-start.4
  85.2 5.4 %shard_map.95 = (bf16[256,640]{1,0:T(8,128)(2,1)S(1)}, bf16[256,640]{1,0:T(8,128)(2,1)S(1)}) custom-call(s32[20]{0:T(128)S(1)} %pad_add_fusion.1.meta, bf16[256,1280]{1,0:T(8,128)(2,1)S(1)} %get-tuple-element.22.xa, bf16[256,1280]{1,0:T(8,128)(2,1)S(1)} %collective-permute-done.6._.xb, f32[1,1920]{1,0:T(1,128)S(1)} %reshape.81.bias, ...), custom_call_target="tpu_custom_call" | custom-call | tf_op jit(solution)/shard_map/pallas_call | solution.py:327
  90.5 2.3 %collective-permute-start.11 = (bf16[256,640]{1,0:T(8,128)(2,1)S(1)}, bf16[256,640]{1,0:T(8,128)(2,1)S(1)}, u32[]{:S(2)}, u32[]{:S(2)}) collective-permute-start(bf16[256,640]{1,0:T(8,128)(2,1)S(1)} %get-tuple-element.28), channel_id=1, source_target_pairs={{0,8},{8,0},{16,24},{24,16},{32,40},{40,32},{48,56},{56,48},{64,72... | collective-permute-start | bytes 983048 | tf_op jit(solution)/shard_map/ppermute | solution.py:62
  92.9 1.2 %collective-permute-done.11.attb = bf16[256,640]{1,0:T(8,128)(2,1)S(1)} collective-permute-done((bf16[256,640]{1,0:T(8,128)(2,1)S(1)}, bf16[256,640]{1,0:T(8,128)(2,1)S(1)}, u32[]{:S(2)}, u32[]{:S(2)}) %collective-permute-start.11) | collective-permute-done | bytes 327712 | tf_op jit(solution)/shard_map/ppermute | solution.py:62
  94.1 0.0 collective-permute-done.12.wb
  94.1 3.0 %shard_map.96 = bf16[64,5120]{1,0:T(8,128)(2,1)} custom-call(s32[20]{0:T(128)S(1)} %pad_add_fusion.1.meta, bf16[256,640]{1,0:T(8,128)(2,1)S(1)} %get-tuple-element.27.atta, bf16[256,640]{1,0:T(8,128)(2,1)S(1)} %collective-permute-done.11.attb, bf16[1280,640]{1,0:T(8,128)(2,1)S(1)} %get-tuple-element.29.wa, bf16[1280,640]{1,0:T(8,128)(2,1)S(1)} %collective-permute-done.12.wb, ...), custom_call_target="tpu_custom_call" | custom-call | tf_op jit(solution)/shard_map/pallas_call | solution.py:337
  (13 shorter events, 0.1 us)
Async XLA Ops:
  2.9 44.9 %collective-permute-start = (bf16[320,2560]{1,0:T(8,128)(2,1)S(1)}, bf16[320,2560]{1,0:T(8,128)(2,1)}, u32[]{:S(2)}, u32[]{:S(2)}) collective-permute-start(bf16[320,2560]{1,0:T(8,128)(2,1)S(1)} %constant_dynamic-update-slice_fusion.own), channel_id=1, source_target_pairs={{0,257},{8,12},{16,273},{24,28},{32,289},{40,44},{48,305},{56,60},... | collective-permute-start | bytes 4915208 | tf_op jit(solution)/shard_map/ppermute | solution.py:62
  8.4 3.9 %copy-start = (bf16[1,1,7,64,1280]{4,3,2,1,0:T(8,128)(2,1)S(1)}, bf16[1,1,7,64,1280]{4,3,2,1,0:T(8,128)(2,1)}, u32[]{:S(2)}) copy-start(bf16[1,1,7,64,1280]{4,3,2,1,0:T(8,128)(2,1)} %own.1) | copy-start | bytes 3440644
  8.5 16.7 %copy-start.6 = (s32[64,1,7]{0,1,2:T(1,128)S(1)}, s32[64,1,7]{0,1,2:T(1,128)}, u32[]{:S(2)}) copy-start(s32[64,1,7]{0,1,2:T(1,128)} %param.16) | copy-start | bytes 5380
  8.5 17.2 %copy-start.5 = (s32[64,1,7,2]{0,3,2,1:T(2,128)S(1)}, s32[64,1,7,2]{0,3,2,1:T(2,128)}, u32[]{:S(2)}) copy-start(s32[64,1,7,2]{0,3,2,1:T(2,128)} %param.17) | copy-start | bytes 10756
  8.5 39.2 %copy-start.2 = (f32[1280]{0:T(1024)S(1)}, f32[1280]{0:T(1024)}, u32[]{:S(2)}) copy-start(f32[1280]{0:T(1024)} %param.10) | copy-start | bytes 15364
  9.5 26.9 %collective-permute-start.7 = (bf16[160,2560]{1,0:T(8,128)(2,1)}, bf16[160,2560]{1,0:T(8,128)(2,1)}, u32[]{:S(2)}, u32[]{:S(2)}) collective-permute-start(bf16[160,2560]{1,0:T(8,128)(2,1)} %pad_maximum_fusion.2), channel_id=1, source_target_pairs={{0,2},{8,14},{16,18},{24,30},{32,34},{40,46},{48,50},{56,62},{64,6... | collective-permute-start | bytes 2457608 | tf_op jit(solution)/shard_map/ppermute | solution.py:62
  13.0 34.7 %collective-permute-start.1 = (bf16[64,1280]{1,0:T(8,128)(2,1)}, bf16[64,1280]{1,0:T(8,128)(2,1)S(1)}, u32[]{:S(2)}, u32[]{:S(2)}) collective-permute-start(bf16[64,1280]{1,0:T(8,128)(2,1)} %get-tuple-element.45), channel_id=1, source_target_pairs={{0,8},{8,16},{16,24},{24,32},{32,40},{40,48},{48,56},{56,64},{64,7... | collective-permute-start | bytes 491528 | tf_op jit(solution)/shard_map/ppermute | solution.py:67
  18.0 29.7 %collective-permute-start.2 = (bf16[64,1280]{1,0:T(8,128)(2,1)}, bf16[64,1280]{1,0:T(8,128)(2,1)S(1)}, u32[]{:S(2)}, u32[]{:S(2)}) collective-permute-start(bf16[64,1280]{1,0:T(8,128)(2,1)} %get-tuple-element.44), channel_id=1, source_target_pairs={{0,16},{8,24},{16,32},{24,40},{32,48},{40,56},{48,64},{56,72},{64,... | collective-permute-start | bytes 491528 | tf_op jit(solution)/shard_map/ppermute | solution.py:67
  21.6 47.7 %collective-permute-start.3 = (bf16[64,1280]{1,0:T(8,128)(2,1)S(1)}, bf16[64,1280]{1,0:T(8,128)(2,1)S(1)}, u32[]{:S(2)}, u32[]{:S(2)}) collective-permute-start(bf16[64,1280]{1,0:T(8,128)(2,1)S(1)} %get-tuple-element.43), channel_id=1, source_target_pairs={{0,24},{8,32},{16,40},{24,48},{32,56},{40,64},{48,72},{56,80},{64,... | collective-permute-start | bytes 491528 | tf_op jit(solution)/shard_map/ppermute | solution.py:67
  36.4 28.9 %collective-permute-start.8 = (bf16[160,2560]{1,0:T(8,128)(2,1)}, bf16[160,2560]{1,0:T(8,128)(2,1)}, u32[]{:S(2)}, u32[]{:S(2)}) collective-permute-start(bf16[160,2560]{1,0:T(8,128)(2,1)} %collective-permute-done.7.refs_0_.a), channel_id=1, source_target_pairs={{0,240},{8,248},{16,0},{24,8},{32,16},{40,24},{48,32},{56,40},{64,... | collective-permute-start | bytes 2457608 | tf_op jit(solution)/shard_map/ppermute | solution.py:62
  47.8 25.5 %collective-permute-start.4 = (bf16[320,2560]{1,0:T(8,128)(2,1)}, bf16[320,2560]{1,0:T(8,128)(2,1)S(1)}, u32[]{:S(2)}, u32[]{:S(2)}) collective-permute-start(bf16[320,2560]{1,0:T(8,128)(2,1)} %collective-permute-done.refs_2_.b), channel_id=1, source_target_pairs={{0,2},{8,265},{16,18},{24,281},{32,34},{40,297},{48,50},{56,313},{... | collective-permute-start | bytes 4915208 | tf_op jit(solution)/shard_map/ppermute | solution.py:62
  52.4 20.9 %collective-permute-start.5 = (bf16[320,2560]{1,0:T(8,128)(2,1)}, bf16[320,2560]{1,0:T(8,128)(2,1)S(1)}, u32[]{:S(2)}, u32[]{:S(2)}) collective-permute-start(bf16[320,2560]{1,0:T(8,128)(2,1)} %collective-permute-done.refs_2_.b), channel_id=1, source_target_pairs={{0,6},{16,22},{32,38},{48,54},{64,70},{80,86},{96,102},{112,118},{... | collective-permute-start | bytes 4915208 | tf_op jit(solution)/shard_map/ppermute | solution.py:62
  66.7 10.7 %collective-permute-start.9 = (bf16[320,2560]{1,0:T(8,128)(2,1)S(1)}, bf16[320,2560]{1,0:T(8,128)(2,1)S(1)}, u32[]{:S(2)}, u32[]{:S(2)}) collective-permute-start(bf16[320,2560]{1,0:T(8,128)(2,1)S(1)} %shard_map.93), channel_id=1, source_target_pairs={{0,8},{8,0},{16,24},{24,16},{32,40},{40,32},{48,56},{56,48},{64,72... | collective-permute-start | bytes 4915208 | tf_op jit(solution)/shard_map/ppermute | solution.py:62
  71.4 4.0 %collective-permute-start.6 = (bf16[256,1280]{1,0:T(8,128)(2,1)S(1)}, bf16[256,1280]{1,0:T(8,128)(2,1)S(1)}, u32[]{:S(2)}, u32[]{:S(2)}) collective-permute-start(bf16[256,1280]{1,0:T(8,128)(2,1)S(1)} %get-tuple-element.22.xa), channel_id=1, source_target_pairs={{0,8},{8,0},{16,24},{24,16},{32,40},{40,32},{48,56},{56,48},{64,72... | collective-permute-start | bytes 1966088 | tf_op jit(solution)/shard_map/ppermute | solution.py:62
  73.5 11.5 %copy-start.1 = (f32[3840]{0:T(1024)S(1)}, f32[3840]{0:T(1024)}, u32[]{:S(2)}) copy-start(f32[3840]{0:T(1024)} %param.12) | copy-start | bytes 46084
  75.4 5.4 %collective-permute-start.10 = (bf16[320,2560]{1,0:T(8,128)(2,1)S(1)}, bf16[320,2560]{1,0:T(8,128)(2,1)S(1)}, u32[]{:S(2)}, u32[]{:S(2)}) collective-permute-start(bf16[320,2560]{1,0:T(8,128)(2,1)S(1)} %shard_map.92), channel_id=1, source_target_pairs={{0,8},{8,0},{16,24},{24,16},{32,40},{40,32},{48,56},{56,48},{64,72... | collective-permute-start | bytes 4915208 | tf_op jit(solution)/shard_map/ppermute | solution.py:62
  83.0 11.1 %collective-permute-start.12 = (bf16[1280,640]{1,0:T(8,128)(2,1)S(1)}, bf16[1280,640]{1,0:T(8,128)(2,1)S(1)}, u32[]{:S(2)}, u32[]{:S(2)}) collective-permute-start(bf16[1280,640]{1,0:T(8,128)(2,1)S(1)} %get-tuple-element.29.wa), channel_id=1, source_target_pairs={{0,8},{8,0},{16,24},{24,16},{32,40},{40,32},{48,56},{56,48},{64,72... | collective-permute-start | bytes 4915208 | tf_op jit(solution)/shard_map/ppermute | solution.py:62
  85.1 7.7 %copy-start.3 = (f32[1280]{0:T(1024)S(1)}, f32[1280]{0:T(1024)}, u32[]{:S(2)}) copy-start(f32[1280]{0:T(1024)} %param.14) | copy-start | bytes 15364
  85.2 7.7 %copy-start.4 = (f32[1280]{0:T(1024)S(1)}, f32[1280]{0:T(1024)}, u32[]{:S(2)}) copy-start(f32[1280]{0:T(1024)} %param.15) | copy-start | bytes 15364
  90.5 3.5 %collective-permute-start.11 = (bf16[256,640]{1,0:T(8,128)(2,1)S(1)}, bf16[256,640]{1,0:T(8,128)(2,1)S(1)}, u32[]{:S(2)}, u32[]{:S(2)}) collective-permute-start(bf16[256,640]{1,0:T(8,128)(2,1)S(1)} %get-tuple-element.28), channel_id=1, source_target_pairs={{0,8},{8,0},{16,24},{24,16},{32,40},{40,32},{48,56},{56,48},{64,72... | collective-permute-start | bytes 983048 | tf_op jit(solution)/shard_map/ppermute | solution.py:62

commit v10 on v9

--- a/solution.py
+++ b/solution.py
@@ -51,7 +51,7 @@
 
 
 def planes():
-    return perm(lambda x, yh, yl, z, c: (x, yh, yl, z - 1, c))
+    return perm(lambda x, yh, yl, z, c: (x, yh, yl, z ^ 1, c))
 
 
 def other_core():

time: 97.6 us -> 90.9 us (0.931)
  starting transfers between devices: 47.4 us -> 40.6 us
    ppermute x10, starting transfers between devices: 35.3 us -> 28.5 us  [send(): return lax.ppermute(value, AXES, pairs)]
  transfers between devices with their start and end apart: 13 -> 13, of which waited for: 5 -> 5; matrix products, arithmetic and copies ran while one was open for 4% -> 4% of each run, Pallas kernels for 9% -> 10%
where the time goes in v10:
time: 90.9 us; the launch traced here: 90.3 us
  starting transfers between devices  40.6 us (45%)
  waiting for transfers between devices  28.5 us (31%)
  Pallas kernels  14.3 us (16%)
  local copies, waits for them, and re-layouts  4.13 us (5%)
  other arithmetic  2.35 us (3%)
    ppermute x10, waiting for transfers between devices, send(): return lax.ppermute(value, AXES, pairs)  28.5 us
    ppermute x10, starting transfers between devices, send(): return lax.ppermute(value, AXES, pairs)  28.5 us
    ppermute x3, starting transfers between devices, by_rank(): lax.ppermute(value, 'dp', [(i, (i + by) % devices) for i in range(devices)])  12.1 us
    pallas_call x1, Pallas kernels, on_device(): pl.pallas_call(attend_kernel, out_shape=[jax.ShapeDtypeStruct((ROWS, HALF...  5.38 us
    pallas_call x1, Pallas kernels, on_device(): pl.pallas_call(merge_kernel, out_shape=jax.ShapeDtypeStruct((ROWS // MERG...  2.97 us
    pallas_call x1, Pallas kernels, on_device(): pl.pallas_call(gather_kernel, out_shape=[jax.ShapeDtypeStruct((D, 3 * HAL...  2.21 us
    pallas_call x1, Pallas kernels, on_device(): pl.pallas_call(place_kernel, out_shape=[jax.ShapeDtypeStruct((ROWS, D), j...  2.07 us
  transfers between devices with their start and end apart: 13, of which 5 were waited for; matrix products, arithmetic and copies ran while one was open for 4% of the time, Pallas kernels for 10%

profile of v10, /device:TPU:1, one launch (start us, length us, event | category | flops | bytes accessed | tf_op | source)
XLA Modules:
  0.0 90.3 jit_solution(16397393854510851212)
XLA Ops:
  0.0 1.1 %dynamic-slice_bitcast_fusion = (bf16[160,640]{1,0:T(8,128)(2,1)S(1)}, bf16[160,640]{1,0:T(8,128)(2,1)S(1)}) fusion(bf16[1280,160]{0,1:T(8,128)(2,1)} %param.13, s32[]{:T(128)S(6)} %select_n.199, s32[]{:T(128)S(6)} %select_n.195), kind=kLoop, calls=%fused_computation.3 | loop fusion | bytes 819208 | tf_op jit(solution)/shard_map/dynamic_slice | solution.py:277
  1.1 1.5 %constant_dynamic-slice_fusion.4 = (bf16[160,640]{1,0:T(8,128)(2,1)S(1)}, bf16[160,640]{1,0:T(8,128)(2,1)S(1)}, bf16[160,640]{1,0:T(8,128)(2,1)S(1)}, bf16[160,6...) fusion(bf16[160,3840]{1,0:T(8,128)(2,1)} %param.11, s32[]{:T(128)S(6)} %select_n.196, ...), kind=kLoop, calls=%fused_computation.31 | loop fusion | bytes 2457624 | tf_op jit(solution)/shard_map/dynamic_slice | solution.py:276
  2.6 0.2 pad_maximum_fusion
  2.7 0.1 constant_dynamic-update-slice_fusion.1
  2.8 0.1 constant_dynamic-update-slice_fusion.own
  2.9 5.5 %collective-permute-start = (bf16[320,2560]{1,0:T(8,128)(2,1)S(1)}, bf16[320,2560]{1,0:T(8,128)(2,1)}, u32[]{:S(2)}, u32[]{:S(2)}) collective-permute-start(bf16[320,2560]{1,0:T(8,128)(2,1)S(1)} %constant_dynamic-update-slice_fusion.own), channel_id=1, source_target_pairs={{0,257},{8,12},{16,273},{24,28},{32,289},{40,44},{48,305},{56,60},... | collective-permute-start | bytes 4915208 | tf_op jit(solution)/shard_map/ppermute | solution.py:62
  8.4 0.0 copy-start
  8.4 0.1 constant_dynamic-slice_fusion.1
  8.5 0.0 copy-start.6
  8.5 0.0 copy-start.5
  8.5 0.0 copy-start.2
  8.5 1.0 %pad_maximum_fusion.2 = bf16[160,2560]{1,0:T(8,128)(2,1)} fusion(bf16[80,2560]{1,0:T(8,128)(2,1)S(1)} %get-tuple-element.36, bf16[80,2560]{1,0:T(8,128)(2,1)S(1)} %get-tuple-element.35), kind=kLoop, calls=%fused_computation.2 | loop fusion | flops 1638400 | bytes 1638400 | tf_op jit(solution)/shard_map/concatenate | solution.py:289
  9.5 2.8 %collective-permute-start.7 = (bf16[160,2560]{1,0:T(8,128)(2,1)}, bf16[160,2560]{1,0:T(8,128)(2,1)}, u32[]{:S(2)}, u32[]{:S(2)}) collective-permute-start(bf16[160,2560]{1,0:T(8,128)(2,1)} %pad_maximum_fusion.2), channel_id=1, source_target_pairs={{0,2},{8,14},{16,18},{24,30},{32,34},{40,46},{48,50},{56,62},{64,6... | collective-permute-start | bytes 2457608 | tf_op jit(solution)/shard_map/ppermute | solution.py:62
  12.2 0.0 copy-done
  12.2 0.8 slice_bitcast_fusion
  13.0 5.0 %collective-permute-start.1 = (bf16[64,1280]{1,0:T(8,128)(2,1)}, bf16[64,1280]{1,0:T(8,128)(2,1)S(1)}, u32[]{:S(2)}, u32[]{:S(2)}) collective-permute-start(bf16[64,1280]{1,0:T(8,128)(2,1)} %get-tuple-element.45), channel_id=1, source_target_pairs={{0,8},{8,16},{16,24},{24,32},{32,40},{40,48},{48,56},{56,64},{64,7... | collective-permute-start | bytes 491528 | tf_op jit(solution)/shard_map/ppermute | solution.py:67
  18.0 3.5 %collective-permute-start.2 = (bf16[64,1280]{1,0:T(8,128)(2,1)}, bf16[64,1280]{1,0:T(8,128)(2,1)S(1)}, u32[]{:S(2)}, u32[]{:S(2)}) collective-permute-start(bf16[64,1280]{1,0:T(8,128)(2,1)} %get-tuple-element.44), channel_id=1, source_target_pairs={{0,16},{8,24},{16,32},{24,40},{32,48},{40,56},{48,64},{56,72},{64,... | collective-permute-start | bytes 491528 | tf_op jit(solution)/shard_map/ppermute | solution.py:67
  21.6 3.6 %collective-permute-start.3 = (bf16[64,1280]{1,0:T(8,128)(2,1)S(1)}, bf16[64,1280]{1,0:T(8,128)(2,1)S(1)}, u32[]{:S(2)}, u32[]{:S(2)}) collective-permute-start(bf16[64,1280]{1,0:T(8,128)(2,1)S(1)} %get-tuple-element.43), channel_id=1, source_target_pairs={{0,24},{8,32},{16,40},{24,48},{32,56},{40,64},{48,72},{56,80},{64,... | collective-permute-start | bytes 491528 | tf_op jit(solution)/shard_map/ppermute | solution.py:67
  25.1 0.1 pad_add_fusion
  25.2 0.0 copy-done.6
  25.2 0.1 fusion.2
  25.3 0.3 select_reduce_fusion.1
  25.6 0.1 copy.13
  25.7 0.0 copy-done.5
  25.7 0.3 select_reduce_fusion
  26.0 0.2 slice_reduce_fusion
  26.2 0.2 fusion
  26.4 9.9 %collective-permute-done.7.refs_0_.a = bf16[160,2560]{1,0:T(8,128)(2,1)} collective-permute-done((bf16[160,2560]{1,0:T(8,128)(2,1)}, bf16[160,2560]{1,0:T(8,128)(2,1)}, u32[]{:S(2)}, u32[]{:S(2)}) %collective-permute-start.7) | collective-permute-done | bytes 819232 | tf_op jit(solution)/shard_map/ppermute | solution.py:62
  36.4 3.4 %collective-permute-start.8 = (bf16[160,2560]{1,0:T(8,128)(2,1)}, bf16[160,2560]{1,0:T(8,128)(2,1)}, u32[]{:S(2)}, u32[]{:S(2)}) collective-permute-start(bf16[160,2560]{1,0:T(8,128)(2,1)} %collective-permute-done.7.refs_0_.a), channel_id=1, source_target_pairs={{0,16},{8,24},{16,0},{24,8},{32,48},{40,56},{48,32},{56,40},{64,80... | collective-permute-start | bytes 2457608 | tf_op jit(solution)/shard_map/ppermute | solution.py:62
  39.7 0.1 select_reduce_fusion.3
  40.0 0.1 stack.59
  40.1 0.1 stack.58
  40.2 0.0 copy-done.2
  40.2 0.1 pad_add_fusion.1.meta
  40.3 0.0 collective-permute-done.1.in0
  40.3 0.0 collective-permute-done.2.in1
  40.3 0.0 collective-permute-done.refs_2_.b
  40.3 4.5 %collective-permute-start.4 = (bf16[320,2560]{1,0:T(8,128)(2,1)}, bf16[320,2560]{1,0:T(8,128)(2,1)S(1)}, u32[]{:S(2)}, u32[]{:S(2)}) collective-permute-start(bf16[320,2560]{1,0:T(8,128)(2,1)} %collective-permute-done.refs_2_.b), channel_id=1, source_target_pairs={{0,2},{8,265},{16,18},{24,281},{32,34},{40,297},{48,50},{56,313},{... | collective-permute-start | bytes 4915208 | tf_op jit(solution)/shard_map/ppermute | solution.py:62
  44.8 0.8 collective-permute-start.5
  45.6 12.2 %collective-permute-done.8.refs_1_.rest_a = bf16[160,2560]{1,0:T(8,128)(2,1)} collective-permute-done((bf16[160,2560]{1,0:T(8,128)(2,1)}, bf16[160,2560]{1,0:T(8,128)(2,1)}, u32[]{:S(2)}, u32[]{:S(2)}) %collective-permute-start.8) | collective-permute-done | bytes 819232 | tf_op jit(solution)/shard_map/ppermute | solution.py:62
  57.8 1.4 %shard_map.93 = bf16[320,2560]{1,0:T(8,128)(2,1)S(1)} custom-call(bf16[160,2560]{1,0:T(8,128)(2,1)} %collective-permute-done.7.refs_0_.a, bf16[160,2560]{1,0:T(8,128)(2,1)} %collective-permute-done.8.refs_1_.rest_a, bf16[320,2560]{1,0:T(8,128)(2,1)} %collective-permute-done.refs_2_.b), custom_call_target="tpu_custom_call" | custom-call | flops 20000000000 | bytes 819200 | tf_op jit(solution)/shard_map/pallas_call | solution.py:231
  59.3 3.3 %collective-permute-start.9 = (bf16[320,2560]{1,0:T(8,128)(2,1)S(1)}, bf16[320,2560]{1,0:T(8,128)(2,1)S(1)}, u32[]{:S(2)}, u32[]{:S(2)}) collective-permute-start(bf16[320,2560]{1,0:T(8,128)(2,1)S(1)} %shard_map.93), channel_id=1, source_target_pairs={{0,8},{8,0},{16,24},{24,16},{32,40},{40,32},{48,56},{56,48},{64,72... | collective-permute-start | bytes 4915208 | tf_op jit(solution)/shard_map/ppermute | solution.py:62
  62.6 0.0 collective-permute-done.3.in2
  62.6 2.1 %shard_map.91 = (bf16[256,1280]{1,0:T(8,128)(2,1)S(1)}, bf16[256,1280]{1,0:T(8,128)(2,1)S(1)}) custom-call(s32[20]{0:T(128)S(1)} %pad_add_fusion.1.meta, bf16[1,1,7,64,1280]{4,3,2,1,0:T(8,128)(2,1)S(1)} %copy-done, bf16[64,1280]{1,0:T(8,128)(2,1)S(1)} %collective-permute-done.1.in0, bf16[64,1280]{1,0:T(8,128)(2,1)S(1)} %collective-permute-done.2.in1, ...), custom_call_target="tpu_custom_call" | custom-call | tf_op jit(solution)/shard_map/pallas_call | solution.py:302
  64.7 1.9 %collective-permute-start.6 = (bf16[256,1280]{1,0:T(8,128)(2,1)S(1)}, bf16[256,1280]{1,0:T(8,128)(2,1)S(1)}, u32[]{:S(2)}, u32[]{:S(2)}) collective-permute-start(bf16[256,1280]{1,0:T(8,128)(2,1)S(1)} %get-tuple-element.22.xa), channel_id=1, source_target_pairs={{0,8},{8,0},{16,24},{24,16},{32,40},{40,32},{48,56},{56,48},{64,72... | collective-permute-start | bytes 1966088 | tf_op jit(solution)/shard_map/ppermute | solution.py:62
  66.6 0.0 collective-permute-done.4.refs_0_.c
  66.6 0.0 collective-permute-done.5.refs_1_.d
  66.6 0.2 shard_map.92
  66.8 0.0 copy-start.1
  66.8 1.8 %collective-permute-done.6._.xb = bf16[256,1280]{1,0:T(8,128)(2,1)S(1)} collective-permute-done((bf16[256,1280]{1,0:T(8,128)(2,1)S(1)}, bf16[256,1280]{1,0:T(8,128)(2,1)S(1)}, u32[]{:S(2)}, u32[]{:S(2)}) %collective-permute-start.6) | collective-permute-done | bytes 655392 | tf_op jit(solution)/shard_map/ppermute | solution.py:62
  68.7 2.0 %collective-permute-start.10 = (bf16[320,2560]{1,0:T(8,128)(2,1)S(1)}, bf16[320,2560]{1,0:T(8,128)(2,1)S(1)}, u32[]{:S(2)}, u32[]{:S(2)}) collective-permute-start(bf16[320,2560]{1,0:T(8,128)(2,1)S(1)} %shard_map.92), channel_id=1, source_target_pairs={{0,8},{8,0},{16,24},{24,16},{32,40},{40,32},{48,56},{56,48},{64,72... | collective-permute-start | bytes 4915208 | tf_op jit(solution)/shard_map/ppermute | solution.py:62
  70.7 0.0 collective-permute-done.9.early
  70.7 3.3 %collective-permute-done.10.late = bf16[320,2560]{1,0:T(8,128)(2,1)S(1)} collective-permute-done((bf16[320,2560]{1,0:T(8,128)(2,1)S(1)}, bf16[320,2560]{1,0:T(8,128)(2,1)S(1)}, u32[]{:S(2)}, u32[]{:S(2)}) %collective-permute-start.10) | collective-permute-done | bytes 1638432 | tf_op jit(solution)/shard_map/ppermute | solution.py:62
  74.0 2.2 %shard_map.94 = (bf16[1280,1920]{1,0:T(8,128)(2,1)S(1)}, bf16[1280,640]{1,0:T(8,128)(2,1)S(1)}) custom-call(s32[20]{0:T(128)S(1)} %pad_add_fusion.1.meta, bf16[320,2560]{1,0:T(8,128)(2,1)S(1)} %constant_dynamic-update-slice_fusion.own, bf16[160,2560]{1,0:T(8,128)(2,1)} %collective-permute-done.7.refs_0_.a, bf16[320,2560]{1,0:T(8,128)(2,1)} %collective-permute-done.refs_2_.b, ...), custom_call_target="tpu_custom_call" | custom-call | tf_op jit(solution)/shard_map/pallas_call | solution.py:314
  76.3 2.0 %collective-permute-start.12 = (bf16[1280,640]{1,0:T(8,128)(2,1)S(1)}, bf16[1280,640]{1,0:T(8,128)(2,1)S(1)}, u32[]{:S(2)}, u32[]{:S(2)}) collective-permute-start(bf16[1280,640]{1,0:T(8,128)(2,1)S(1)} %get-tuple-element.29.wa), channel_id=1, source_target_pairs={{0,8},{8,0},{16,24},{24,16},{32,40},{40,32},{48,56},{56,48},{64,72... | collective-permute-start | bytes 4915208 | tf_op jit(solution)/shard_map/ppermute | solution.py:62
  78.3 0.0 copy-done.1
  78.3 0.1 fusion.4
  78.4 0.0 copy-start.3
  78.4 0.0 copy-start.4
  78.5 5.4 %shard_map.95 = (bf16[256,640]{1,0:T(8,128)(2,1)S(1)}, bf16[256,640]{1,0:T(8,128)(2,1)S(1)}) custom-call(s32[20]{0:T(128)S(1)} %pad_add_fusion.1.meta, bf16[256,1280]{1,0:T(8,128)(2,1)S(1)} %get-tuple-element.22.xa, bf16[256,1280]{1,0:T(8,128)(2,1)S(1)} %collective-permute-done.6._.xb, f32[1,1920]{1,0:T(1,128)S(1)} %reshape.81.bias, ...), custom_call_target="tpu_custom_call" | custom-call | tf_op jit(solution)/shard_map/pallas_call | solution.py:327
  83.8 2.3 %collective-permute-start.11 = (bf16[256,640]{1,0:T(8,128)(2,1)S(1)}, bf16[256,640]{1,0:T(8,128)(2,1)S(1)}, u32[]{:S(2)}, u32[]{:S(2)}) collective-permute-start(bf16[256,640]{1,0:T(8,128)(2,1)S(1)} %get-tuple-element.28), channel_id=1, source_target_pairs={{0,8},{8,0},{16,24},{24,16},{32,40},{40,32},{48,56},{56,48},{64,72... | collective-permute-start | bytes 983048 | tf_op jit(solution)/shard_map/ppermute | solution.py:62
  86.2 1.2 %collective-permute-done.11.attb = bf16[256,640]{1,0:T(8,128)(2,1)S(1)} collective-permute-done((bf16[256,640]{1,0:T(8,128)(2,1)S(1)}, bf16[256,640]{1,0:T(8,128)(2,1)S(1)}, u32[]{:S(2)}, u32[]{:S(2)}) %collective-permute-start.11) | collective-permute-done | bytes 327712 | tf_op jit(solution)/shard_map/ppermute | solution.py:62
  87.4 0.0 collective-permute-done.12.wb
  87.4 3.0 %shard_map.96 = bf16[64,5120]{1,0:T(8,128)(2,1)} custom-call(s32[20]{0:T(128)S(1)} %pad_add_fusion.1.meta, bf16[256,640]{1,0:T(8,128)(2,1)S(1)} %get-tuple-element.27.atta, bf16[256,640]{1,0:T(8,128)(2,1)S(1)} %collective-permute-done.11.attb, bf16[1280,640]{1,0:T(8,128)(2,1)S(1)} %get-tuple-element.29.wa, bf16[1280,640]{1,0:T(8,128)(2,1)S(1)} %collective-permute-done.12.wb, ...), custom_call_target="tpu_custom_call" | custom-call | tf_op jit(solution)/shard_map/pallas_call | solution.py:337
  (13 shorter events, 0.1 us)
Async XLA Ops:
  2.9 37.4 %collective-permute-start = (bf16[320,2560]{1,0:T(8,128)(2,1)S(1)}, bf16[320,2560]{1,0:T(8,128)(2,1)}, u32[]{:S(2)}, u32[]{:S(2)}) collective-permute-start(bf16[320,2560]{1,0:T(8,128)(2,1)S(1)} %constant_dynamic-update-slice_fusion.own), channel_id=1, source_target_pairs={{0,257},{8,12},{16,273},{24,28},{32,289},{40,44},{48,305},{56,60},... | collective-permute-start | bytes 4915208 | tf_op jit(solution)/shard_map/ppermute | solution.py:62
  8.4 3.9 %copy-start = (bf16[1,1,7,64,1280]{4,3,2,1,0:T(8,128)(2,1)S(1)}, bf16[1,1,7,64,1280]{4,3,2,1,0:T(8,128)(2,1)}, u32[]{:S(2)}) copy-start(bf16[1,1,7,64,1280]{4,3,2,1,0:T(8,128)(2,1)} %own.1) | copy-start | bytes 3440644
  8.5 16.7 %copy-start.6 = (s32[64,1,7]{0,1,2:T(1,128)S(1)}, s32[64,1,7]{0,1,2:T(1,128)}, u32[]{:S(2)}) copy-start(s32[64,1,7]{0,1,2:T(1,128)} %param.16) | copy-start | bytes 5380
  8.5 17.2 %copy-start.5 = (s32[64,1,7,2]{0,3,2,1:T(2,128)S(1)}, s32[64,1,7,2]{0,3,2,1:T(2,128)}, u32[]{:S(2)}) copy-start(s32[64,1,7,2]{0,3,2,1:T(2,128)} %param.17) | copy-start | bytes 10756
  8.5 31.7 %copy-start.2 = (f32[1280]{0:T(1024)S(1)}, f32[1280]{0:T(1024)}, u32[]{:S(2)}) copy-start(f32[1280]{0:T(1024)} %param.10) | copy-start | bytes 15364
  9.5 26.9 %collective-permute-start.7 = (bf16[160,2560]{1,0:T(8,128)(2,1)}, bf16[160,2560]{1,0:T(8,128)(2,1)}, u32[]{:S(2)}, u32[]{:S(2)}) collective-permute-start(bf16[160,2560]{1,0:T(8,128)(2,1)} %pad_maximum_fusion.2), channel_id=1, source_target_pairs={{0,2},{8,14},{16,18},{24,30},{32,34},{40,46},{48,50},{56,62},{64,6... | collective-permute-start | bytes 2457608 | tf_op jit(solution)/shard_map/ppermute | solution.py:62
  13.0 27.3 %collective-permute-start.1 = (bf16[64,1280]{1,0:T(8,128)(2,1)}, bf16[64,1280]{1,0:T(8,128)(2,1)S(1)}, u32[]{:S(2)}, u32[]{:S(2)}) collective-permute-start(bf16[64,1280]{1,0:T(8,128)(2,1)} %get-tuple-element.45), channel_id=1, source_target_pairs={{0,8},{8,16},{16,24},{24,32},{32,40},{40,48},{48,56},{56,64},{64,7... | collective-permute-start | bytes 491528 | tf_op jit(solution)/shard_map/ppermute | solution.py:67
  18.0 22.3 %collective-permute-start.2 = (bf16[64,1280]{1,0:T(8,128)(2,1)}, bf16[64,1280]{1,0:T(8,128)(2,1)S(1)}, u32[]{:S(2)}, u32[]{:S(2)}) collective-permute-start(bf16[64,1280]{1,0:T(8,128)(2,1)} %get-tuple-element.44), channel_id=1, source_target_pairs={{0,16},{8,24},{16,32},{24,40},{32,48},{40,56},{48,64},{56,72},{64,... | collective-permute-start | bytes 491528 | tf_op jit(solution)/shard_map/ppermute | solution.py:67
  21.6 41.0 %collective-permute-start.3 = (bf16[64,1280]{1,0:T(8,128)(2,1)S(1)}, bf16[64,1280]{1,0:T(8,128)(2,1)S(1)}, u32[]{:S(2)}, u32[]{:S(2)}) collective-permute-start(bf16[64,1280]{1,0:T(8,128)(2,1)S(1)} %get-tuple-element.43), channel_id=1, source_target_pairs={{0,24},{8,32},{16,40},{24,48},{32,56},{40,64},{48,72},{56,80},{64,... | collective-permute-start | bytes 491528 | tf_op jit(solution)/shard_map/ppermute | solution.py:67
  36.4 21.5 %collective-permute-start.8 = (bf16[160,2560]{1,0:T(8,128)(2,1)}, bf16[160,2560]{1,0:T(8,128)(2,1)}, u32[]{:S(2)}, u32[]{:S(2)}) collective-permute-start(bf16[160,2560]{1,0:T(8,128)(2,1)} %collective-permute-done.7.refs_0_.a), channel_id=1, source_target_pairs={{0,16},{8,24},{16,0},{24,8},{32,48},{40,56},{48,32},{56,40},{64,80... | collective-permute-start | bytes 2457608 | tf_op jit(solution)/shard_map/ppermute | solution.py:62
  40.3 26.3 %collective-permute-start.4 = (bf16[320,2560]{1,0:T(8,128)(2,1)}, bf16[320,2560]{1,0:T(8,128)(2,1)S(1)}, u32[]{:S(2)}, u32[]{:S(2)}) collective-permute-start(bf16[320,2560]{1,0:T(8,128)(2,1)} %collective-permute-done.refs_2_.b), channel_id=1, source_target_pairs={{0,2},{8,265},{16,18},{24,281},{32,34},{40,297},{48,50},{56,313},{... | collective-permute-start | bytes 4915208 | tf_op jit(solution)/shard_map/ppermute | solution.py:62
  44.8 21.8 %collective-permute-start.5 = (bf16[320,2560]{1,0:T(8,128)(2,1)}, bf16[320,2560]{1,0:T(8,128)(2,1)S(1)}, u32[]{:S(2)}, u32[]{:S(2)}) collective-permute-start(bf16[320,2560]{1,0:T(8,128)(2,1)} %collective-permute-done.refs_2_.b), channel_id=1, source_target_pairs={{0,6},{16,22},{32,38},{48,54},{64,70},{80,86},{96,102},{112,118},{... | collective-permute-start | bytes 4915208 | tf_op jit(solution)/shard_map/ppermute | solution.py:62
  59.3 11.4 %collective-permute-start.9 = (bf16[320,2560]{1,0:T(8,128)(2,1)S(1)}, bf16[320,2560]{1,0:T(8,128)(2,1)S(1)}, u32[]{:S(2)}, u32[]{:S(2)}) collective-permute-start(bf16[320,2560]{1,0:T(8,128)(2,1)S(1)} %shard_map.93), channel_id=1, source_target_pairs={{0,8},{8,0},{16,24},{24,16},{32,40},{40,32},{48,56},{56,48},{64,72... | collective-permute-start | bytes 4915208 | tf_op jit(solution)/shard_map/ppermute | solution.py:62
  64.7 4.0 %collective-permute-start.6 = (bf16[256,1280]{1,0:T(8,128)(2,1)S(1)}, bf16[256,1280]{1,0:T(8,128)(2,1)S(1)}, u32[]{:S(2)}, u32[]{:S(2)}) collective-permute-start(bf16[256,1280]{1,0:T(8,128)(2,1)S(1)} %get-tuple-element.22.xa), channel_id=1, source_target_pairs={{0,8},{8,0},{16,24},{24,16},{32,40},{40,32},{48,56},{56,48},{64,72... | collective-permute-start | bytes 1966088 | tf_op jit(solution)/shard_map/ppermute | solution.py:62
  66.8 11.5 %copy-start.1 = (f32[3840]{0:T(1024)S(1)}, f32[3840]{0:T(1024)}, u32[]{:S(2)}) copy-start(f32[3840]{0:T(1024)} %param.12) | copy-start | bytes 46084
  68.7 5.4 %collective-permute-start.10 = (bf16[320,2560]{1,0:T(8,128)(2,1)S(1)}, bf16[320,2560]{1,0:T(8,128)(2,1)S(1)}, u32[]{:S(2)}, u32[]{:S(2)}) collective-permute-start(bf16[320,2560]{1,0:T(8,128)(2,1)S(1)} %shard_map.92), channel_id=1, source_target_pairs={{0,8},{8,0},{16,24},{24,16},{32,40},{40,32},{48,56},{56,48},{64,72... | collective-permute-start | bytes 4915208 | tf_op jit(solution)/shard_map/ppermute | solution.py:62
  76.3 11.1 %collective-permute-start.12 = (bf16[1280,640]{1,0:T(8,128)(2,1)S(1)}, bf16[1280,640]{1,0:T(8,128)(2,1)S(1)}, u32[]{:S(2)}, u32[]{:S(2)}) collective-permute-start(bf16[1280,640]{1,0:T(8,128)(2,1)S(1)} %get-tuple-element.29.wa), channel_id=1, source_target_pairs={{0,8},{8,0},{16,24},{24,16},{32,40},{40,32},{48,56},{56,48},{64,72... | collective-permute-start | bytes 4915208 | tf_op jit(solution)/shard_map/ppermute | solution.py:62
  78.4 7.7 %copy-start.3 = (f32[1280]{0:T(1024)S(1)}, f32[1280]{0:T(1024)}, u32[]{:S(2)}) copy-start(f32[1280]{0:T(1024)} %param.14) | copy-start | bytes 15364
  78.4 7.7 %copy-start.4 = (f32[1280]{0:T(1024)S(1)}, f32[1280]{0:T(1024)}, u32[]{:S(2)}) copy-start(f32[1280]{0:T(1024)} %param.15) | copy-start | bytes 15364
  83.8 3.5 %collective-permute-start.11 = (bf16[256,640]{1,0:T(8,128)(2,1)S(1)}, bf16[256,640]{1,0:T(8,128)(2,1)S(1)}, u32[]{:S(2)}, u32[]{:S(2)}) collective-permute-start(bf16[256,640]{1,0:T(8,128)(2,1)S(1)} %get-tuple-element.28), channel_id=1, source_target_pairs={{0,8},{8,0},{16,24},{24,16},{32,40},{40,32},{48,56},{56,48},{64,72... | collective-permute-start | bytes 983048 | tf_op jit(solution)/shard_map/ppermute | solution.py:62

commit v11 on v10

--- a/solution.py
+++ b/solution.py
@@ -308,7 +308,7 @@
         compiler_params=SMALL,
     )(meta, patches, *moved, norm_gain.reshape(1, D))
     normed_other = send(normed, other_core())
-    late, normed_other = lax.optimization_barrier((gather_halves(got_c, got_d), normed_other))
+    late = gather_halves(got_c, got_d)
     late = send(late, other_core())
 
     w, w_mine = pl.pallas_call(

time: 90.9 us -> 97.4 us (1.072)
  starting transfers between devices: 40.6 us -> 54.1 us
  waiting for transfers between devices: 28.5 us -> 22.2 us
    ppermute x10, starting transfers between devices: 28.5 us -> 41.4 us  [send(): return lax.ppermute(value, AXES, pairs)]
    ppermute x10, waiting for transfers between devices: 28.5 us -> 22.2 us  [send(): return lax.ppermute(value, AXES, pairs)]
  transfers between devices with their start and end apart: 13 -> 13, of which waited for: 5 -> 5; matrix products, arithmetic and copies ran while one was open for 4% -> 3% of each run, Pallas kernels for 10% -> 9%
where the time goes in v11:
time: 97.4 us; the launch traced here: 96.7 us
  starting transfers between devices  54.1 us (56%)
  waiting for transfers between devices  22.2 us (23%)
  Pallas kernels  14.3 us (15%)
  local copies, waits for them, and re-layouts  4.13 us (4%)
  other arithmetic  1.45 us (1%)
    ppermute x10, starting transfers between devices, send(): return lax.ppermute(value, AXES, pairs)  41.4 us
    ppermute x10, waiting for transfers between devices, send(): return lax.ppermute(value, AXES, pairs)  22.2 us
    ppermute x3, starting transfers between devices, by_rank(): lax.ppermute(value, 'dp', [(i, (i + by) % devices) for i in range(devices)])  12.7 us
    pallas_call x1, Pallas kernels, on_device(): pl.pallas_call(attend_kernel, out_shape=[jax.ShapeDtypeStruct((ROWS, HALF...  5.38 us
    pallas_call x1, Pallas kernels, on_device(): pl.pallas_call(merge_kernel, out_shape=jax.ShapeDtypeStruct((ROWS // MERG...  2.97 us
    pallas_call x1, Pallas kernels, on_device(): pl.pallas_call(gather_kernel, out_shape=[jax.ShapeDtypeStruct((D, 3 * HAL...  2.21 us
    pallas_call x1, Pallas kernels, on_device(): pl.pallas_call(place_kernel, out_shape=[jax.ShapeDtypeStruct((ROWS, D), j...  2.07 us
  transfers between devices with their start and end apart: 13, of which 5 were waited for; matrix products, arithmetic and copies ran while one was open for 3% of the time, Pallas kernels for 9%

profile of v11, /device:TPU:1, one launch (start us, length us, event | category | flops | bytes accessed | tf_op | source)
XLA Modules:
  0.0 96.7 jit_solution(2266560049073328579)
XLA Ops:
  0.0 1.1 %dynamic-slice_bitcast_fusion = (bf16[160,640]{1,0:T(8,128)(2,1)S(1)}, bf16[160,640]{1,0:T(8,128)(2,1)S(1)}) fusion(bf16[1280,160]{0,1:T(8,128)(2,1)} %param.13, s32[]{:T(128)S(6)} %select_n.199, s32[]{:T(128)S(6)} %select_n.195), kind=kLoop, calls=%fused_computation.3 | loop fusion | bytes 819208 | tf_op jit(solution)/shard_map/dynamic_slice | solution.py:277
  1.1 1.5 %constant_dynamic-slice_fusion.4 = (bf16[160,640]{1,0:T(8,128)(2,1)S(1)}, bf16[160,640]{1,0:T(8,128)(2,1)S(1)}, bf16[160,640]{1,0:T(8,128)(2,1)S(1)}, bf16[160,6...) fusion(bf16[160,3840]{1,0:T(8,128)(2,1)} %param.11, s32[]{:T(128)S(6)} %select_n.196, ...), kind=kLoop, calls=%fused_computation.31 | loop fusion | bytes 2457624 | tf_op jit(solution)/shard_map/dynamic_slice | solution.py:276
  2.6 0.2 pad_maximum_fusion
  2.7 0.1 constant_dynamic-update-slice_fusion.1
  2.8 0.1 constant_dynamic-update-slice_fusion.own
  2.9 0.0 copy-start
  2.9 0.1 constant_dynamic-slice_fusion.1
  3.0 0.0 copy-start.6
  3.0 0.0 copy-start.5
  3.0 0.1 pad_maximum_fusion.2
  3.0 5.3 %collective-permute-start.5 = (bf16[160,2560]{1,0:T(8,128)(2,1)S(1)}, bf16[160,2560]{1,0:T(8,128)(2,1)}, u32[]{:S(2)}, u32[]{:S(2)}) collective-permute-start(bf16[160,2560]{1,0:T(8,128)(2,1)S(1)} %pad_maximum_fusion.2), channel_id=1, source_target_pairs={{0,2},{8,14},{16,18},{24,30},{32,34},{40,46},{48,50},{56,62},{64,6... | collective-permute-start | bytes 2457608 | tf_op jit(solution)/shard_map/ppermute | solution.py:62
  8.4 2.4 %collective-permute-start = (bf16[320,2560]{1,0:T(8,128)(2,1)S(1)}, bf16[320,2560]{1,0:T(8,128)(2,1)}, u32[]{:S(2)}, u32[]{:S(2)}) collective-permute-start(bf16[320,2560]{1,0:T(8,128)(2,1)S(1)} %constant_dynamic-update-slice_fusion.own), channel_id=1, source_target_pairs={{0,257},{8,12},{16,273},{24,28},{32,289},{40,44},{48,305},{56,60},... | collective-permute-start | bytes 4915208 | tf_op jit(solution)/shard_map/ppermute | solution.py:62
  10.8 0.0 copy-done
  10.8 0.8 slice_bitcast_fusion
  11.6 5.6 %collective-permute-start.1 = (bf16[64,1280]{1,0:T(8,128)(2,1)}, bf16[64,1280]{1,0:T(8,128)(2,1)S(1)}, u32[]{:S(2)}, u32[]{:S(2)}) collective-permute-start(bf16[64,1280]{1,0:T(8,128)(2,1)} %get-tuple-element.41), channel_id=1, source_target_pairs={{0,8},{8,16},{16,24},{24,32},{32,40},{40,48},{48,56},{56,64},{64,7... | collective-permute-start | bytes 491528 | tf_op jit(solution)/shard_map/ppermute | solution.py:67
  17.2 3.5 %collective-permute-start.2 = (bf16[64,1280]{1,0:T(8,128)(2,1)}, bf16[64,1280]{1,0:T(8,128)(2,1)S(1)}, u32[]{:S(2)}, u32[]{:S(2)}) collective-permute-start(bf16[64,1280]{1,0:T(8,128)(2,1)} %get-tuple-element.40), channel_id=1, source_target_pairs={{0,16},{8,24},{16,32},{24,40},{32,48},{40,56},{48,64},{56,72},{64,... | collective-permute-start | bytes 491528 | tf_op jit(solution)/shard_map/ppermute | solution.py:67
  20.8 3.6 %collective-permute-start.3 = (bf16[64,1280]{1,0:T(8,128)(2,1)S(1)}, bf16[64,1280]{1,0:T(8,128)(2,1)S(1)}, u32[]{:S(2)}, u32[]{:S(2)}) collective-permute-start(bf16[64,1280]{1,0:T(8,128)(2,1)S(1)} %get-tuple-element.39), channel_id=1, source_target_pairs={{0,24},{8,32},{16,40},{24,48},{32,56},{40,64},{48,72},{56,80},{64,... | collective-permute-start | bytes 491528 | tf_op jit(solution)/shard_map/ppermute | solution.py:67
  24.3 10.9 %collective-permute-done.5.refs_0_.a = bf16[160,2560]{1,0:T(8,128)(2,1)} collective-permute-done((bf16[160,2560]{1,0:T(8,128)(2,1)S(1)}, bf16[160,2560]{1,0:T(8,128)(2,1)}, u32[]{:S(2)}, u32[]{:S(2)}) %collective-permute-start.5) | collective-permute-done | bytes 819232 | tf_op jit(solution)/shard_map/ppermute | solution.py:62
  35.2 3.5 %collective-permute-start.8 = (bf16[160,2560]{1,0:T(8,128)(2,1)}, bf16[160,2560]{1,0:T(8,128)(2,1)}, u32[]{:S(2)}, u32[]{:S(2)}) collective-permute-start(bf16[160,2560]{1,0:T(8,128)(2,1)} %collective-permute-done.5.refs_0_.a), channel_id=1, source_target_pairs={{0,16},{8,24},{16,0},{24,8},{32,48},{40,56},{48,32},{56,40},{64,80... | collective-permute-start | bytes 2457608 | tf_op jit(solution)/shard_map/ppermute | solution.py:62
  38.8 0.0 copy-done.6
  38.8 0.1 pad_add_fusion
  38.9 0.1 fusion.2
  38.9 0.3 select_reduce_fusion.1
  39.2 0.0 copy-done.5
  39.3 0.3 select_reduce_fusion
  39.7 0.1 stack.59
  39.8 0.1 stack.58
  39.9 0.1 copy.13
  39.9 0.2 fusion
  40.2 0.0 collective-permute-done.1.in0
  40.2 0.0 collective-permute-done.2.in1
  40.2 0.0 collective-permute-done.refs_2_.b
  40.2 4.6 %collective-permute-start.6 = (bf16[320,2560]{1,0:T(8,128)(2,1)}, bf16[320,2560]{1,0:T(8,128)(2,1)S(1)}, u32[]{:S(2)}, u32[]{:S(2)}) collective-permute-start(bf16[320,2560]{1,0:T(8,128)(2,1)} %collective-permute-done.refs_2_.b), channel_id=1, source_target_pairs={{0,2},{8,265},{16,18},{24,281},{32,34},{40,297},{48,50},{56,313},{... | collective-permute-start | bytes 4915208 | tf_op jit(solution)/shard_map/ppermute | solution.py:62
  44.8 0.8 collective-permute-start.7
  45.6 5.8 %collective-permute-done.8.refs_1_.rest_a = bf16[160,2560]{1,0:T(8,128)(2,1)} collective-permute-done((bf16[160,2560]{1,0:T(8,128)(2,1)}, bf16[160,2560]{1,0:T(8,128)(2,1)}, u32[]{:S(2)}, u32[]{:S(2)}) %collective-permute-start.8) | collective-permute-done | bytes 819232 | tf_op jit(solution)/shard_map/ppermute | solution.py:62
  51.4 1.4 %shard_map.92 = bf16[320,2560]{1,0:T(8,128)(2,1)S(1)} custom-call(bf16[160,2560]{1,0:T(8,128)(2,1)} %collective-permute-done.5.refs_0_.a, bf16[160,2560]{1,0:T(8,128)(2,1)} %collective-permute-done.8.refs_1_.rest_a, bf16[320,2560]{1,0:T(8,128)(2,1)} %collective-permute-done.refs_2_.b), custom_call_target="tpu_custom_call" | custom-call | flops 20000000000 | bytes 819200 | tf_op jit(solution)/shard_map/pallas_call | solution.py:231
  52.9 0.0 copy-start.2
  52.9 8.7 %collective-permute-start.9 = (bf16[320,2560]{1,0:T(8,128)(2,1)S(1)}, bf16[320,2560]{1,0:T(8,128)(2,1)S(1)}, u32[]{:S(2)}, u32[]{:S(2)}) collective-permute-start(bf16[320,2560]{1,0:T(8,128)(2,1)S(1)} %shard_map.92), channel_id=1, source_target_pairs={{0,8},{8,0},{16,24},{24,16},{32,40},{40,32},{48,56},{56,48},{64,72... | collective-permute-start | bytes 4915208 | tf_op jit(solution)/shard_map/ppermute | solution.py:62
  61.6 2.2 %collective-permute-done.6.refs_0_.c = bf16[320,2560]{1,0:T(8,128)(2,1)S(1)} collective-permute-done((bf16[320,2560]{1,0:T(8,128)(2,1)}, bf16[320,2560]{1,0:T(8,128)(2,1)S(1)}, u32[]{:S(2)}, u32[]{:S(2)}) %collective-permute-start.6) | collective-permute-done | bytes 1638432 | tf_op jit(solution)/shard_map/ppermute | solution.py:62
  63.8 0.0 collective-permute-done.7.refs_1_.d
  63.8 0.2 shard_map.93
  64.1 9.7 %collective-permute-start.10 = (bf16[320,2560]{1,0:T(8,128)(2,1)S(1)}, bf16[320,2560]{1,0:T(8,128)(2,1)S(1)}, u32[]{:S(2)}, u32[]{:S(2)}) collective-permute-start(bf16[320,2560]{1,0:T(8,128)(2,1)S(1)} %shard_map.93), channel_id=1, source_target_pairs={{0,8},{8,0},{16,24},{24,16},{32,40},{40,32},{48,56},{56,48},{64,72... | collective-permute-start | bytes 4915208 | tf_op jit(solution)/shard_map/ppermute | solution.py:62
  73.8 0.2 slice_reduce_fusion
  74.0 0.2 select_reduce_fusion.3
  74.2 0.0 copy-done.2
  74.2 0.1 pad_add_fusion.1.meta
  74.3 0.0 collective-permute-done.3.in2
  74.3 2.1 %shard_map.91 = (bf16[256,1280]{1,0:T(8,128)(2,1)S(1)}, bf16[256,1280]{1,0:T(8,128)(2,1)S(1)}) custom-call(s32[20]{0:T(128)S(1)} %pad_add_fusion.1.meta, bf16[1,1,7,64,1280]{4,3,2,1,0:T(8,128)(2,1)S(1)} %copy-done, bf16[64,1280]{1,0:T(8,128)(2,1)S(1)} %collective-permute-done.1.in0, bf16[64,1280]{1,0:T(8,128)(2,1)S(1)} %collective-permute-done.2.in1, ...), custom_call_target="tpu_custom_call" | custom-call | tf_op jit(solution)/shard_map/pallas_call | solution.py:302
  76.3 0.0 copy-start.1
  76.4 1.9 %collective-permute-start.4 = (bf16[256,1280]{1,0:T(8,128)(2,1)S(1)}, bf16[256,1280]{1,0:T(8,128)(2,1)S(1)}, u32[]{:S(2)}, u32[]{:S(2)}) collective-permute-start(bf16[256,1280]{1,0:T(8,128)(2,1)S(1)} %get-tuple-element.20.xa), channel_id=1, source_target_pairs={{0,8},{8,0},{16,24},{24,16},{32,40},{40,32},{48,56},{56,48},{64,72... | collective-permute-start | bytes 1966088 | tf_op jit(solution)/shard_map/ppermute | solution.py:62
  78.3 2.1 %collective-permute-done.4._.xb = bf16[256,1280]{1,0:T(8,128)(2,1)S(1)} collective-permute-done((bf16[256,1280]{1,0:T(8,128)(2,1)S(1)}, bf16[256,1280]{1,0:T(8,128)(2,1)S(1)}, u32[]{:S(2)}, u32[]{:S(2)}) %collective-permute-start.4) | collective-permute-done | bytes 655392 | tf_op jit(solution)/shard_map/ppermute | solution.py:62
  80.4 0.0 collective-permute-done.9.early
  80.4 0.0 collective-permute-done.10.late
  80.4 2.2 %shard_map.94 = (bf16[1280,1920]{1,0:T(8,128)(2,1)S(1)}, bf16[1280,640]{1,0:T(8,128)(2,1)S(1)}) custom-call(s32[20]{0:T(128)S(1)} %pad_add_fusion.1.meta, bf16[320,2560]{1,0:T(8,128)(2,1)S(1)} %constant_dynamic-update-slice_fusion.own, bf16[160,2560]{1,0:T(8,128)(2,1)} %collective-permute-done.5.refs_0_.a, bf16[320,2560]{1,0:T(8,128)(2,1)} %collective-permute-done.refs_2_.b, ...), custom_call_target="tpu_custom_call" | custom-call | tf_op jit(solution)/shard_map/pallas_call | solution.py:314
  82.6 2.0 %collective-permute-start.12 = (bf16[1280,640]{1,0:T(8,128)(2,1)S(1)}, bf16[1280,640]{1,0:T(8,128)(2,1)S(1)}, u32[]{:S(2)}, u32[]{:S(2)}) collective-permute-start(bf16[1280,640]{1,0:T(8,128)(2,1)S(1)} %get-tuple-element.25.wa), channel_id=1, source_target_pairs={{0,8},{8,0},{16,24},{24,16},{32,40},{40,32},{48,56},{56,48},{64,72... | collective-permute-start | bytes 4915208 | tf_op jit(solution)/shard_map/ppermute | solution.py:62
  84.6 0.0 copy-done.1
  84.6 0.1 fusion.4
  84.8 0.0 copy-start.3
  84.8 0.0 copy-start.4
  84.8 5.4 %shard_map.95 = (bf16[256,640]{1,0:T(8,128)(2,1)S(1)}, bf16[256,640]{1,0:T(8,128)(2,1)S(1)}) custom-call(s32[20]{0:T(128)S(1)} %pad_add_fusion.1.meta, bf16[256,1280]{1,0:T(8,128)(2,1)S(1)} %get-tuple-element.20.xa, bf16[256,1280]{1,0:T(8,128)(2,1)S(1)} %collective-permute-done.4._.xb, f32[1,1920]{1,0:T(1,128)S(1)} %reshape.81.bias, ...), custom_call_target="tpu_custom_call" | custom-call | tf_op jit(solution)/shard_map/pallas_call | solution.py:327
  90.2 2.3 %collective-permute-start.11 = (bf16[256,640]{1,0:T(8,128)(2,1)S(1)}, bf16[256,640]{1,0:T(8,128)(2,1)S(1)}, u32[]{:S(2)}, u32[]{:S(2)}) collective-permute-start(bf16[256,640]{1,0:T(8,128)(2,1)S(1)} %get-tuple-element.24), channel_id=1, source_target_pairs={{0,8},{8,0},{16,24},{24,16},{32,40},{40,32},{48,56},{56,48},{64,72... | collective-permute-start | bytes 983048 | tf_op jit(solution)/shard_map/ppermute | solution.py:62
  92.5 1.2 %collective-permute-done.11.attb = bf16[256,640]{1,0:T(8,128)(2,1)S(1)} collective-permute-done((bf16[256,640]{1,0:T(8,128)(2,1)S(1)}, bf16[256,640]{1,0:T(8,128)(2,1)S(1)}, u32[]{:S(2)}, u32[]{:S(2)}) %collective-permute-start.11) | collective-permute-done | bytes 327712 | tf_op jit(solution)/shard_map/ppermute | solution.py:62
  93.7 0.0 collective-permute-done.12.wb
  93.7 3.0 %shard_map.96 = bf16[64,5120]{1,0:T(8,128)(2,1)} custom-call(s32[20]{0:T(128)S(1)} %pad_add_fusion.1.meta, bf16[256,640]{1,0:T(8,128)(2,1)S(1)} %get-tuple-element.23.atta, bf16[256,640]{1,0:T(8,128)(2,1)S(1)} %collective-permute-done.11.attb, bf16[1280,640]{1,0:T(8,128)(2,1)S(1)} %get-tuple-element.25.wa, bf16[1280,640]{1,0:T(8,128)(2,1)S(1)} %collective-permute-done.12.wb, ...), custom_call_target="tpu_custom_call" | custom-call | tf_op jit(solution)/shard_map/pallas_call | solution.py:337
  (13 shorter events, 0.1 us)
Async XLA Ops:
  2.9 8.0 %copy-start = (bf16[1,1,7,64,1280]{4,3,2,1,0:T(8,128)(2,1)S(1)}, bf16[1,1,7,64,1280]{4,3,2,1,0:T(8,128)(2,1)}, u32[]{:S(2)}) copy-start(bf16[1,1,7,64,1280]{4,3,2,1,0:T(8,128)(2,1)} %own.1) | copy-start | bytes 3440644
  3.0 35.8 %copy-start.6 = (s32[64,1,7]{0,1,2:T(1,128)S(1)}, s32[64,1,7]{0,1,2:T(1,128)}, u32[]{:S(2)}) copy-start(s32[64,1,7]{0,1,2:T(1,128)} %param.16) | copy-start | bytes 5380
  3.0 36.3 %copy-start.5 = (s32[64,1,7,2]{0,3,2,1:T(2,128)S(1)}, s32[64,1,7,2]{0,3,2,1:T(2,128)}, u32[]{:S(2)}) copy-start(s32[64,1,7,2]{0,3,2,1:T(2,128)} %param.17) | copy-start | bytes 10756
  3.0 32.2 %collective-permute-start.5 = (bf16[160,2560]{1,0:T(8,128)(2,1)S(1)}, bf16[160,2560]{1,0:T(8,128)(2,1)}, u32[]{:S(2)}, u32[]{:S(2)}) collective-permute-start(bf16[160,2560]{1,0:T(8,128)(2,1)S(1)} %pad_maximum_fusion.2), channel_id=1, source_target_pairs={{0,2},{8,14},{16,18},{24,30},{32,34},{40,46},{48,50},{56,62},{64,6... | collective-permute-start | bytes 2457608 | tf_op jit(solution)/shard_map/ppermute | solution.py:62
  8.4 31.8 %collective-permute-start = (bf16[320,2560]{1,0:T(8,128)(2,1)S(1)}, bf16[320,2560]{1,0:T(8,128)(2,1)}, u32[]{:S(2)}, u32[]{:S(2)}) collective-permute-start(bf16[320,2560]{1,0:T(8,128)(2,1)S(1)} %constant_dynamic-update-slice_fusion.own), channel_id=1, source_target_pairs={{0,257},{8,12},{16,273},{24,28},{32,289},{40,44},{48,305},{56,60},... | collective-permute-start | bytes 4915208 | tf_op jit(solution)/shard_map/ppermute | solution.py:62
  11.6 28.6 %collective-permute-start.1 = (bf16[64,1280]{1,0:T(8,128)(2,1)}, bf16[64,1280]{1,0:T(8,128)(2,1)S(1)}, u32[]{:S(2)}, u32[]{:S(2)}) collective-permute-start(bf16[64,1280]{1,0:T(8,128)(2,1)} %get-tuple-element.41), channel_id=1, source_target_pairs={{0,8},{8,16},{16,24},{24,32},{32,40},{40,48},{48,56},{56,64},{64,7... | collective-permute-start | bytes 491528 | tf_op jit(solution)/shard_map/ppermute | solution.py:67
  17.2 23.0 %collective-permute-start.2 = (bf16[64,1280]{1,0:T(8,128)(2,1)}, bf16[64,1280]{1,0:T(8,128)(2,1)S(1)}, u32[]{:S(2)}, u32[]{:S(2)}) collective-permute-start(bf16[64,1280]{1,0:T(8,128)(2,1)} %get-tuple-element.40), channel_id=1, source_target_pairs={{0,16},{8,24},{16,32},{24,40},{32,48},{40,56},{48,64},{56,72},{64,... | collective-permute-start | bytes 491528 | tf_op jit(solution)/shard_map/ppermute | solution.py:67
  20.8 53.5 %collective-permute-start.3 = (bf16[64,1280]{1,0:T(8,128)(2,1)S(1)}, bf16[64,1280]{1,0:T(8,128)(2,1)S(1)}, u32[]{:S(2)}, u32[]{:S(2)}) collective-permute-start(bf16[64,1280]{1,0:T(8,128)(2,1)S(1)} %get-tuple-element.39), channel_id=1, source_target_pairs={{0,24},{8,32},{16,40},{24,48},{32,56},{40,64},{48,72},{56,80},{64,... | collective-permute-start | bytes 491528 | tf_op jit(solution)/shard_map/ppermute | solution.py:67
  35.2 16.2 %collective-permute-start.8 = (bf16[160,2560]{1,0:T(8,128)(2,1)}, bf16[160,2560]{1,0:T(8,128)(2,1)}, u32[]{:S(2)}, u32[]{:S(2)}) collective-permute-start(bf16[160,2560]{1,0:T(8,128)(2,1)} %collective-permute-done.5.refs_0_.a), channel_id=1, source_target_pairs={{0,16},{8,24},{16,0},{24,8},{32,48},{40,56},{48,32},{56,40},{64,80... | collective-permute-start | bytes 2457608 | tf_op jit(solution)/shard_map/ppermute | solution.py:62
  40.2 23.6 %collective-permute-start.6 = (bf16[320,2560]{1,0:T(8,128)(2,1)}, bf16[320,2560]{1,0:T(8,128)(2,1)S(1)}, u32[]{:S(2)}, u32[]{:S(2)}) collective-permute-start(bf16[320,2560]{1,0:T(8,128)(2,1)} %collective-permute-done.refs_2_.b), channel_id=1, source_target_pairs={{0,2},{8,265},{16,18},{24,281},{32,34},{40,297},{48,50},{56,313},{... | collective-permute-start | bytes 4915208 | tf_op jit(solution)/shard_map/ppermute | solution.py:62
  44.8 19.0 %collective-permute-start.7 = (bf16[320,2560]{1,0:T(8,128)(2,1)}, bf16[320,2560]{1,0:T(8,128)(2,1)S(1)}, u32[]{:S(2)}, u32[]{:S(2)}) collective-permute-start(bf16[320,2560]{1,0:T(8,128)(2,1)} %collective-permute-done.refs_2_.b), channel_id=1, source_target_pairs={{0,6},{16,22},{32,38},{48,54},{64,70},{80,86},{96,102},{112,118},{... | collective-permute-start | bytes 4915208 | tf_op jit(solution)/shard_map/ppermute | solution.py:62
  52.9 21.3 %copy-start.2 = (f32[1280]{0:T(1024)S(1)}, f32[1280]{0:T(1024)}, u32[]{:S(2)}) copy-start(f32[1280]{0:T(1024)} %param.10) | copy-start | bytes 15364
  52.9 27.5 %collective-permute-start.9 = (bf16[320,2560]{1,0:T(8,128)(2,1)S(1)}, bf16[320,2560]{1,0:T(8,128)(2,1)S(1)}, u32[]{:S(2)}, u32[]{:S(2)}) collective-permute-start(bf16[320,2560]{1,0:T(8,128)(2,1)S(1)} %shard_map.92), channel_id=1, source_target_pairs={{0,8},{8,0},{16,24},{24,16},{32,40},{40,32},{48,56},{56,48},{64,72... | collective-permute-start | bytes 4915208 | tf_op jit(solution)/shard_map/ppermute | solution.py:62
  64.1 16.3 %collective-permute-start.10 = (bf16[320,2560]{1,0:T(8,128)(2,1)S(1)}, bf16[320,2560]{1,0:T(8,128)(2,1)S(1)}, u32[]{:S(2)}, u32[]{:S(2)}) collective-permute-start(bf16[320,2560]{1,0:T(8,128)(2,1)S(1)} %shard_map.93), channel_id=1, source_target_pairs={{0,8},{8,0},{16,24},{24,16},{32,40},{40,32},{48,56},{56,48},{64,72... | collective-permute-start | bytes 4915208 | tf_op jit(solution)/shard_map/ppermute | solution.py:62
  76.3 8.3 %copy-start.1 = (f32[3840]{0:T(1024)S(1)}, f32[3840]{0:T(1024)}, u32[]{:S(2)}) copy-start(f32[3840]{0:T(1024)} %param.12) | copy-start | bytes 46084
  76.4 4.0 %collective-permute-start.4 = (bf16[256,1280]{1,0:T(8,128)(2,1)S(1)}, bf16[256,1280]{1,0:T(8,128)(2,1)S(1)}, u32[]{:S(2)}, u32[]{:S(2)}) collective-permute-start(bf16[256,1280]{1,0:T(8,128)(2,1)S(1)} %get-tuple-element.20.xa), channel_id=1, source_target_pairs={{0,8},{8,0},{16,24},{24,16},{32,40},{40,32},{48,56},{56,48},{64,72... | collective-permute-start | bytes 1966088 | tf_op jit(solution)/shard_map/ppermute | solution.py:62
  82.6 11.1 %collective-permute-start.12 = (bf16[1280,640]{1,0:T(8,128)(2,1)S(1)}, bf16[1280,640]{1,0:T(8,128)(2,1)S(1)}, u32[]{:S(2)}, u32[]{:S(2)}) collective-permute-start(bf16[1280,640]{1,0:T(8,128)(2,1)S(1)} %get-tuple-element.25.wa), channel_id=1, source_target_pairs={{0,8},{8,0},{16,24},{24,16},{32,40},{40,32},{48,56},{56,48},{64,72... | collective-permute-start | bytes 4915208 | tf_op jit(solution)/shard_map/ppermute | solution.py:62
  84.8 7.7 %copy-start.3 = (f32[1280]{0:T(1024)S(1)}, f32[1280]{0:T(1024)}, u32[]{:S(2)}) copy-start(f32[1280]{0:T(1024)} %param.14) | copy-start | bytes 15364
  84.8 7.7 %copy-start.4 = (f32[1280]{0:T(1024)S(1)}, f32[1280]{0:T(1024)}, u32[]{:S(2)}) copy-start(f32[1280]{0:T(1024)} %param.15) | copy-start | bytes 15364
  90.2 3.5 %collective-permute-start.11 = (bf16[256,640]{1,0:T(8,128)(2,1)S(1)}, bf16[256,640]{1,0:T(8,128)(2,1)S(1)}, u32[]{:S(2)}, u32[]{:S(2)}) collective-permute-start(bf16[256,640]{1,0:T(8,128)(2,1)S(1)} %get-tuple-element.24), channel_id=1, source_target_pairs={{0,8},{8,0},{16,24},{24,16},{32,40},{40,32},{48,56},{56,48},{64,72... | collective-permute-start | bytes 983048 | tf_op jit(solution)/shard_map/ppermute | solution.py:62
